TPU v7x, 32 devices: a whole 2x2x4 slice. The times are simulated.
32 devices in a mesh: tm: 8 (over z, x), chan: 4 (over y, core).
Axes of the slice: x: 2, y: 2, z: 4, core: 2. Of those that a mesh axis runs over, the one named last changes fastest.
Arguments:
- fwd_in: bfloat16 [16384, 512], P('tm', 'chan'), may hold values from -28 to 28, as said below
- bwd_in: bfloat16 [16384, 512], P('tm', 'chan'), may hold values from -28 to 28, as said below
Outputs:
- forward_error: bfloat16 [16384, 512], P('tm', 'chan')
- backward_error: bfloat16 [16384, 512], P('tm', 'chan')
Inputs may be any that keep to these rules, and one draw needn't show every extreme that they name: `fwd_in`: real-valued samples. `bwd_in`: real-valued samples.
All inputs are finite; a program needn't handle non-finite values.
Results may differ from a plain program's by a relative error of at most 0.0066.
Values may be sent and summed in bfloat16 or wider, within the bound.
No kernel may reach another device: no remote copies, remote signals or barrier semaphores. Data moves between devices by JAX's collectives and lax.ppermute only.
A program may use at most 64 MiB of HBM per device.

v0:
```python
import jax
import jax.numpy as jnp
from jax import lax
from jax.sharding import PartitionSpec as P

ORDERS = 2
NSTEPS = 6


HIGH = lax.Precision.HIGHEST


def from_behind(value, axis, by):
    devices = lax.axis_size(axis)
    pairs = [(i, i + by) for i in range(devices) if 0 <= i + by < devices]
    return lax.ppermute(value, axis, pairs)


def gram(left, right):
    return lax.dot_general(
        left, right, (((0,), (0,)), ((), ())), preferred_element_type=jnp.float32
    )


def full_inverse(matrix):
    factor = lax.rsqrt(jnp.sum(matrix * matrix) + 1e-06)
    iterate = factor * jnp.eye(matrix.shape[0], dtype=jnp.float32)
    for step in range(NSTEPS):
        product = jnp.dot(matrix, iterate, precision=HIGH)
        iterate = 2.0 * iterate - jnp.dot(product, iterate, precision=HIGH)
    return iterate


def local(fwd_in, bwd_in):
    arrived = (
        lax.all_to_all(fwd_in, "chan", split_axis=0, concat_axis=1, tiled=True),
        lax.all_to_all(bwd_in, "chan", split_axis=0, concat_axis=1, tiled=True),
    )
    forward = arrived[0]
    backward = arrived[1]
    for order in range(ORDERS):
        before = from_behind(backward[-1:], ("tm", "chan"), 1)
        shifted = jnp.concatenate([before, backward[:-1]], axis=0)
        cov_fwd = gram(forward, forward)
        cov_bwd = gram(shifted, shifted)
        cov_cross = gram(forward, shifted)
        cov_fwd, cov_bwd, cov_cross = lax.psum((cov_fwd, cov_bwd, cov_cross), ("tm", "chan"))
        inv_fwd = full_inverse(cov_fwd)
        inv_bwd = full_inverse(cov_bwd)
        refl_fwd = (-jnp.dot(cov_cross, inv_bwd, precision=HIGH)).astype(jnp.bfloat16)
        refl_bwd = (
            -lax.dot_general(cov_cross, inv_fwd, (((0,), (0,)), ((), ())), precision=HIGH)
        ).astype(jnp.bfloat16)
        new_forward = forward.astype(jnp.float32) + lax.dot_general(
            shifted, refl_fwd, (((1,), (1,)), ((), ())), preferred_element_type=jnp.float32
        )
        new_backward = shifted.astype(jnp.float32) + lax.dot_general(
            forward, refl_bwd, (((1,), (1,)), ((), ())), preferred_element_type=jnp.float32
        )
        forward = new_forward.astype(jnp.bfloat16)
        backward = new_backward.astype(jnp.bfloat16)
    result = (
        lax.all_to_all(forward, "chan", split_axis=1, concat_axis=0, tiled=True),
        lax.all_to_all(backward, "chan", split_axis=1, concat_axis=0, tiled=True),
    )
    return (result[0], result[1])


def solution(mesh):
    in_specs = (P("tm", "chan"), P("tm", "chan"))
    out_specs = (P("tm", "chan"), P("tm", "chan"))
    return jax.shard_map(local, mesh=mesh, in_specs=in_specs, out_specs=out_specs, check_vma=False)
```

profile of v0, /device:TPU:0, one launch (start us, length us, event | category | flops | bytes accessed | tf_op | source)
XLA Modules:
  0.0 456.9 jit_solution(3833216040009583880)
XLA Ops:
  7.2 4.4 all-to-all-start.1
  12.6 7.8 %all-to-all-done.1 = bf16[4,512,128]{2,1,0:T(8,128)(2,1)S(1)} async-done(((bf16[4,512,128]{2,1,0:T(8,128)(2,1)}), bf16[4,512,128]{2,1,0:T(8,128)(2,1)S(1)}, u32[]{:S(2)}, u32[]{:S(2)}) %all-to-all-start.1) | async-done | bytes 524320 | tf_op jit(solution)/shard_map/all_to_all | solution.py:37
  20.4 3.5 all-to-all-start
  23.9 2.3 collective-permute-start
  26.3 6.4 %all-to-all-done = bf16[4,512,128]{1,2,0:T(8,128)(2,1)S(1)} async-done(((bf16[4,512,128]{1,2,0:T(8,128)(2,1)}), bf16[4,512,128]{1,2,0:T(8,128)(2,1)S(1)}, u32[]{:S(2)}, u32[]{:S(2)}) %all-to-all-start) | async-done | bytes 524320 | tf_op jit(solution)/shard_map/all_to_all | solution.py:36
  38.1 139.6 %all-reduce.7.cloned.1.call-done = (f32[512,512]{0,1:T(8,128)}, f32[512,512]{1,0:T(8,128)}, f32[512,512]{1,0:T(8,128)}) async-done(((f32[512,512]{0,1:T(8,128)}, f32[512,512]{1,0:T(8,128)}, f32[512,512]{1,0:T(8,128)}), (f32[512,512]{0,1:T(8,128)}, f32[512,512]{1,0:T(8,128)}, f32[512,512]{1,0:T(8,128)})) %all-reduce.7.cloned.1.call-update) | async-done | bytes 3145744 | tf_op jit(solution)/shard_map/psum | solution.py:47
  177.6 2.5 multiply_reduce_fusion.2
  186.3 1.8 convolution_subtract_fusion.19
  190.0 1.8 convolution_subtract_fusion.18
  191.8 2.1 fusion.64
  197.6 1.8 convolution_subtract_fusion.16
  201.4 1.9 convolution_subtract_fusion.15
  205.7 2.2 fusion.19
  209.8 1.9 convolution_subtract_fusion.14
  213.5 1.8 convolution_subtract_fusion.13
  219.1 2.0 fusion.71
  221.1 1.9 convolution_subtract_fusion.11
  224.8 1.9 convolution_subtract_fusion.10
  226.7 1.9 fusion.28
  228.5 1.8 fusion.30
  237.4 139.8 %all-reduce.5.cloned.1.call-done = (f32[512,512]{1,0:T(8,128)}, f32[512,512]{1,0:T(8,128)}, f32[512,512]{1,0:T(8,128)}) async-done(((f32[512,512]{1,0:T(8,128)}, f32[512,512]{1,0:T(8,128)}, f32[512,512]{1,0:T(8,128)}), (f32[512,512]{1,0:T(8,128)}, f32[512,512]{1,0:T(8,128)}, f32[512,512]{1,0:T(8,128)})) %all-reduce.5.cloned.1.call-update) | async-done | bytes 3145744 | tf_op jit(solution)/shard_map/psum | solution.py:47
  377.1 2.2 multiply_reduce_fusion.1
  389.2 2.3 convolution_subtract_fusion.8
  395.2 1.8 fusion.76
  400.8 1.9 convolution_subtract_fusion.5
  402.7 2.0 fusion.31
  406.0 3.6 all-to-all-start.2
  422.1 2.1 fusion.81
  431.6 1.8 convolution_subtract_fusion
  433.5 1.9 fusion.33
  436.8 3.5 all-to-all-start.3
  441.3 7.8 %all-to-all-done.3 = bf16[512,4,128]{2,0,1:T(8,128)(2,1)S(1)} async-done(((bf16[512,4,128]{2,0,1:T(8,128)(2,1)}), bf16[512,4,128]{2,0,1:T(8,128)(2,1)S(1)}, u32[]{:S(2)}, u32[]{:S(2)}) %all-to-all-start.3) | async-done | bytes 524320 | tf_op jit(solution)/shard_map/all_to_all | solution.py:64
  (80 shorter events, 77.4 us)
Async XLA Ops:
  7.2 4.4 copy-start.9
  7.2 13.2 %all-to-all-start.1 = ((bf16[4,512,128]{2,1,0:T(8,128)(2,1)}), bf16[4,512,128]{2,1,0:T(8,128)(2,1)S(1)}, u32[]{:S(2)}, u32[]{:S(2)}) async-start(bf16[4,512,128]{2,1,0:T(8,128)(2,1)} %bitcast.154), calls=%async_computation.1 | async-start | bytes 1048576 | tf_op jit(solution)/shard_map/all_to_all | solution.py:37
  20.4 12.3 %all-to-all-start = ((bf16[4,512,128]{1,2,0:T(8,128)(2,1)}), bf16[4,512,128]{1,2,0:T(8,128)(2,1)S(1)}, u32[]{:S(2)}, u32[]{:S(2)}) async-start(bf16[4,512,128]{1,2,0:T(8,128)(2,1)} %copy.9), calls=%async_computation | async-start | bytes 1048576 | tf_op jit(solution)/shard_map/all_to_all | solution.py:36
  23.9 153.8 %all-reduce.7.cloned.1.call-start = ((), (), s32[]{:S(2)}) async-start(), calls=%async_computation.5 | async-start | bytes 6291456 | tf_op jit(solution)/shard_map/psum | solution.py:47
  23.9 10.9 %collective-permute-start = (bf16[1,512]{1,0:T(2,128)(2,1)S(1)}, bf16[1,512]{1,0:T(2,128)(2,1)S(1)}, u32[]{:S(2)}, u32[]{:S(2)}) collective-permute-start(bf16[1,512]{1,0:T(2,128)(2,1)S(1)} %slice_bitcast_fusion), channel_id=1, source_target_pairs={{0,1},{1,2},{2,3},{3,4},{4,5},{5,6},{6,7},{7,8},{8,9},{9,10},{10,1... | collective-permute-start | bytes 3080 | tf_op jit(solution)/shard_map/ppermute | solution.py:16
  37.9 339.3 %all-reduce.5.cloned.1.call-start = ((), (), s32[]{:S(2)}) async-start(), calls=%async_computation.4 | async-start | bytes 6291456 | tf_op jit(solution)/shard_map/psum | solution.py:47
  177.6 3.2 copy-start.2
  201.4 2.6 copy-start.1
  224.8 1.9 copy-start.5
  230.9 5.0 %copy-start.6 = (bf16[512,512]{1,0:T(8,128)(2,1)}, bf16[512,512]{1,0:T(8,128)(2,1)S(1)}, u32[]{:S(2)}) copy-start(bf16[512,512]{1,0:T(8,128)(2,1)S(1)} %add_convert_fusion.1) | copy-start | bytes 1572868
  230.9 3.5 collective-permute-start.1
  377.1 2.9 copy-start.3
  400.8 1.9 copy-start.4
  402.7 2.1 copy-start.7
  406.0 3.6 copy-start
  406.0 30.8 %all-to-all-start.2 = ((bf16[512,4,128]{0,2,1:T(8,128)(2,1)}), bf16[512,4,128]{0,2,1:T(8,128)(2,1)S(1)}, u32[]{:S(2)}, u32[]{:S(2)}) async-start(bf16[512,4,128]{0,2,1:T(8,128)(2,1)} %bitcast.155), calls=%async_computation.2 | async-start | bytes 1048576 | tf_op jit(solution)/shard_map/all_to_all | solution.py:63
  433.5 1.9 copy-start.8
  436.8 12.3 %all-to-all-start.3 = ((bf16[512,4,128]{2,0,1:T(8,128)(2,1)}), bf16[512,4,128]{2,0,1:T(8,128)(2,1)S(1)}, u32[]{:S(2)}, u32[]{:S(2)}) async-start(bf16[512,4,128]{2,0,1:T(8,128)(2,1)} %bitcast.133), calls=%async_computation.3 | async-start | bytes 1048576 | tf_op jit(solution)/shard_map/all_to_all | solution.py:64
Sparse Core Ops, SparseCore 0:
  38.0 139.6 all-reduce.6
  237.5 139.6 all-reduce.4
where the time goes:
time: 460 us; the launch traced here: 457 us
  waiting for transfers between devices  301 us (65%)
  matrix products  109 us (24%)
  starting transfers between devices  19 us (4%)
  between operations  17.6 us (4%)
  other arithmetic  5.56 us (1%)
    psum x2, waiting for transfers between devices, local(): lax.psum((cov_fwd, cov_bwd, cov_cross), ('tm', 'chan'))  279 us
    dot_general x24, matrix products, full_inverse(): iterate = 2.0 * iterate - jnp.dot(product, iterate, precision=HIGH)  45 us
    dot_general x24, matrix products, full_inverse(): product = jnp.dot(matrix, iterate, precision=HIGH)  44.7 us
  transfers between devices with their start and end apart: 8, of which 5 were waited for; matrix products, arithmetic and copies ran while one was open for 7% of the time, Pallas kernels for 0%

commit v1 on v0

v1 whole, which is shorter than its diff:
```python
import functools

import jax
import jax.numpy as jnp
from jax import lax
from jax.experimental import pallas as pl
from jax.experimental.pallas import tpu as pltpu
from jax.sharding import Mesh, PartitionSpec as P

ORDERS = 2
NSTEPS = 6
F32 = jnp.float32
BF16 = jnp.bfloat16
PARTS = ("z", "x", "y")
LANES = 128
VMEM = pl.BlockSpec(memory_space=pltpu.VMEM)


def swap(value, axis):
    return lax.ppermute(value, axis, [(0, 1), (1, 0)])


def from_behind(value, axes):
    devices = lax.axis_size(axes)
    return lax.ppermute(value, axes, [(i, i + 1) for i in range(devices - 1)])


def after(value, *others):
    return lax.optimization_barrier((value,) + others)[0]


def call(body, shapes, scratch, flops, *args):
    size = sum(a.size * a.dtype.itemsize for a in args) + sum(s.size * s.dtype.itemsize for s in shapes)
    return pl.pallas_call(
        body,
        out_shape=shapes,
        in_specs=[VMEM] * len(args),
        out_specs=[VMEM] * len(shapes),
        scratch_shapes=scratch,
        compiler_params=pltpu.CompilerParams(vmem_limit_bytes=32 << 20),
        cost_estimate=pl.CostEstimate(flops=flops, bytes_accessed=size, transcendentals=0),
    )(*args)


def place():
    return lax.axis_index("z"), lax.axis_index("x") * 2 + lax.axis_index("y"), lax.axis_index("core")


def dot(a, b):
    return jnp.dot(a, b, preferred_element_type=F32)


def dot_first(a, b):
    return lax.dot_general(a, b, (((0,), (0,)), ((), ())), preferred_element_type=F32)


def dot_last(a, b):
    return lax.dot_general(a, b, (((1,), (1,)), ((), ())), preferred_element_type=F32)


def halves(value):
    high = value.astype(BF16)
    return high, (value - high.astype(F32)).astype(BF16)


def assemble(pieces, out, width):
    y, core = lax.axis_index("y"), lax.axis_index("core")
    for i, piece in enumerate(pieces):
        block = (y ^ (i & 1)) * 2 + (core ^ (i >> 1))
        out[:, :, pl.ds(pl.multiple_of(block * width, LANES), width)] = piece[...]


def delay(source, before, out):
    rows = source.shape[0]
    step = min(rows, 256)
    top = lax.broadcasted_iota(jnp.int32, (step, 1), 0) == 0
    for r in range(0, rows, step):
        edge = (before[...] if r == 0 else source[r - 16 : r]).astype(F32)[15:16]
        moved = pltpu.roll(source[r : r + step].astype(F32), 1, 0)
        out[r : r + step] = jnp.where(top, edge, moved).astype(BF16)


def pack_gram(samples, packed, width):
    blocks = samples.shape[1] // width
    k, rows = 0, {}
    for i in range(0, blocks, 2):
        value = dot_first(samples[:, i * width : (i + 2) * width], samples[:, i * width :])
        rows[i], rows[i + 1] = (i, value[:width]), (i, value[width:])
    for i in range(blocks):
        start, value = rows[i]
        for j in range(i, blocks):
            packed[k * width : (k + 1) * width] = value[:, (j - start) * width : (j - start + 1) * width]
            k += 1
    if packed.shape[0] > k * width:
        packed[k * width :] = jnp.zeros((packed.shape[0] - k * width, LANES), F32)


def own_gram(here, samples, packed, width):
    core = lax.axis_index("core")
    samples[...] = here[core]
    rows = samples.shape[0]

    @pl.when((core == 1) & (lax.axis_index(PARTS) == lax.axis_size(PARTS) - 1))
    def _():
        tail = samples[rows - 16 :].astype(F32)
        inside = lax.broadcasted_iota(jnp.int32, (16, 1), 0) < 15
        samples[rows - 16 :] = jnp.where(inside, tail, 0.0).astype(BF16)

    pack_gram(samples, packed, width)


def unpack(pieces, out, base=0):
    z, xy, _ = place()
    for i, piece in enumerate(pieces):
        depth, rows = piece.shape[0], piece.shape[1]
        for k in range(depth):
            part = lax.rem(z + depth - k, depth) * 4 + (xy ^ i)
            out[pl.ds(pl.multiple_of(base + part * rows, 8), rows)] = piece[k]


def first_kernel(width, *refs):
    pieces, (here, packed, samples) = refs[:4], refs[4:]
    assemble(pieces, here, width)
    own_gram(here, samples, packed, width)


def cross_kernel(width, here, before, shifted, packed):
    core = lax.axis_index("core")
    delay(here.at[1], before, shifted)
    channels = here.shape[2]
    half = channels // 2
    value = dot_first(here[0, :, pl.ds(pl.multiple_of(core * half, LANES), half)], shifted[...])
    for j in range(channels // LANES):
        packed[j * half : (j + 1) * half] = value[:, j * LANES : (j + 1) * LANES]
    used = half * channels // LANES
    if packed.shape[0] > used:
        packed[used:] = jnp.zeros((packed.shape[0] - used, LANES), F32)


def gather_kernel(width, *refs):
    pieces, before, here, shifted = refs[:4], refs[4], refs[5], refs[6]
    assemble(pieces, here, width)
    delay(here.at[1], before, shifted)


def inverse_kernel(width, *refs):
    pieces, out, packed = refs[:4], refs[4], refs[5]
    errors, highs, lows, its, ihighs, ilows = refs[6:]
    unpack(pieces, packed)
    channels = out.shape[0]
    blocks = channels // width
    k, norm = 0, jnp.zeros((8, LANES), F32)
    for i in range(blocks):
        for j in range(i, blocks):
            block = packed[k * width : (k + 1) * width]
            squares = jnp.sum((block * block).reshape(-1, 8, LANES), axis=0)
            norm = norm + (squares if i == j else 2.0 * squares)
            k += 1
    factor = lax.rsqrt(jnp.sum(norm, keepdims=True) + 1e-06)
    eye = lax.broadcasted_iota(jnp.int32, (width, width), 0) == lax.broadcasted_iota(jnp.int32, (width, width), 1)

    def put(table, high, low, slot, rows, cols, value):
        table[slot, rows, cols] = value
        high[slot, rows, cols], low[slot, rows, cols] = halves(value)

    k = 0
    for i in range(blocks):
        for j in range(i, blocks):
            value = packed[k * width : (k + 1) * width] * factor
            k += 1
            for a, b, v in ((i, j, value),) + (() if i == j else ((j, i, value.T),)):
                rows, cols = pl.ds(a * width, width), pl.ds(b * width, width)
                put(errors, highs, lows, 0, rows, cols, v)
                put(its, ihighs, ilows, 1, rows, cols, jnp.where(eye, 2.0, 0.0) - v if a == b else -v)
    step = channels // 2
    every = pl.ds(0, channels)
    for n in range(NSTEPS):
        now, later = n % 2, (n + 1) % 2
        for r in range(0, channels, step):
            rows = pl.ds(r, step)
            high, low = highs[now, rows], lows[now, rows]
            if n < NSTEPS - 1:
                value = dot(high, highs[now]) + dot(high, lows[now]) + dot(low, highs[now])
                put(errors, highs, lows, later, rows, every, 2.0 * errors[now, rows] - value)
            if n >= 1:
                value = dot(high, ihighs[now]) + dot(high, ilows[now]) + dot(low, ihighs[now])
                value = 2.0 * its[now, rows] - value
                if n < NSTEPS - 1:
                    put(its, ihighs, ilows, later, rows, every, value)
                else:
                    out[rows] = value * factor


def reflect_kernel(*refs):
    ours, theirs, inv, out = refs[:4], refs[4], refs[5], refs[6]
    packed, high, low, ihigh, ilow = refs[7:]
    core = lax.axis_index("core")
    channels = out.shape[0]
    half = channels // 2

    def fill(start):
        rows = pl.ds(pl.multiple_of(start, 16), half)
        for j in range(channels // LANES):
            cols = pl.ds(j * LANES, LANES)
            high[rows, cols], low[rows, cols] = halves(packed[j * half : (j + 1) * half])

    unpack(ours, packed)
    fill(core * half)
    unpack([theirs.at[i] for i in range(4)], packed)
    fill((1 - core) * half)
    ihigh[...], ilow[...] = halves(inv[...])
    for chosen, product in ((0, dot_first), (1, dot)):

        @pl.when(core == chosen)
        def _():
            value = product(high[...], ihigh[...]) + product(high[...], ilow[...]) + product(low[...], ihigh[...])
            out[...] = (-value).astype(BF16)


def update(here, shifted, refl, out, rows):
    forward, backward = here[0, rows], shifted[rows]
    out[0, rows] = (forward.astype(F32) + dot_last(backward, refl[0])).astype(BF16)
    out[1, rows] = (backward.astype(F32) + dot_last(forward, refl[1])).astype(BF16)


def by_kind(ours, theirs, refl):
    core = lax.axis_index("core")
    refl[1 - core] = ours[...]
    refl[core] = theirs[...]


def update_gram_kernel(width, here, shifted, ours, theirs, out, packed, refl, samples):
    by_kind(ours, theirs, refl)
    step = 256
    for r in range(0, here.shape[1], step):
        update(here, shifted, refl, out, slice(r, r + step))
    own_gram(out, samples, packed, width)


def update_delay_kernel(here, shifted, ours, theirs, before, ours_tail, out, later, refl, edge):
    by_kind(ours, theirs, refl)
    step = 256
    for r in range(0, here.shape[1], step):
        update(here, shifted, refl, out, slice(r, r + step))
    y = lax.axis_index("y")
    edge[0] = ours_tail[...]
    edge[1] = before[...]
    delay(out.at[1], edge.at[y], later)


def last_kernel(width, here, shifted, there, there_shifted, ours, theirs, forward, backward, refl):
    y, core = lax.axis_index("y"), lax.axis_index("core")
    by_kind(ours, theirs, refl)
    mine = pl.multiple_of((y * 2 + core) * width, LANES)
    half = here.shape[1]
    left, right = refl[0, pl.ds(mine, width)], refl[1, pl.ds(mine, width)]
    for time, (both, late) in ((y, (here, shifted)), (1 - y, (there, there_shifted))):
        rows = pl.ds(pl.multiple_of(time * half, 16), half)
        cols = pl.ds(mine, width)
        forward[rows] = (both[0, :, cols].astype(F32) + dot_last(late[...], left)).astype(BF16)
        backward[rows] = (late[:, cols].astype(F32) + dot_last(both[0], right)).astype(BF16)


def scatter_sum(packed):
    parts = lax.axis_size(PARTS)
    cut = packed.reshape(parts, -1, LANES)
    return jnp.sum(lax.all_to_all(cut, PARTS, 0, 0, tiled=True), axis=0)


def z_gather(piece):
    size = lax.axis_size("z")
    shift = lambda by: [(i, (i + by) % size) for i in range(size)]
    return jnp.stack([piece] + [lax.ppermute(piece, "z", shift(by)) for by in range(1, size)])


def xy_gather(piece):
    return [
        piece,
        swap(piece, "y"),
        swap(piece, "x"),
        lax.ppermute(piece, ("x", "y"), [(i, 3 - i) for i in range(4)]),
    ]


def rounded(rows, parts):
    return -(-rows // (8 * parts)) * 8 * parts


def local(fwd_in, bwd_in):
    y = lax.axis_index("y")
    samples, width = fwd_in.shape
    half = samples // 2
    channels = width * 4
    parts = lax.axis_size(PARTS)
    blocks = channels // width
    sym_rows = rounded(blocks * (blocks + 1) // 2 * width, parts)
    cross_rows = rounded(channels // 2 * channels // LANES, parts)
    both = jnp.stack([fwd_in, bwd_in])
    mine = lax.dynamic_slice_in_dim(both, y * half, half, 1)
    other = lax.dynamic_slice_in_dim(both, (1 - y) * half, half, 1)
    square = lambda *lead: pltpu.VMEM(lead + (channels, channels), F32)
    square16 = lambda *lead: pltpu.VMEM(lead + (channels, channels), BF16)
    shape = jax.ShapeDtypeStruct

    across = swap(other, "y")
    mine_core = swap(mine, "core")
    across_core = swap(across, "core")
    here, packed = call(
        functools.partial(first_kernel, width),
        [shape((2, half, channels), BF16), shape((sym_rows, LANES), F32)],
        [pltpu.VMEM((half, channels), BF16)],
        2 * half * channels * channels,
        mine, across, mine_core, across_core,
    )
    there = there_shifted = None
    for order in range(ORDERS):
        before = from_behind(here[1, half - 16 :], PARTS)
        before_z = from_behind(here[1, half - 16 :], ("z", "x"))
        column = z_gather(scatter_sum(packed))
        pieces = xy_gather(column)
        shifted, cross = call(
            functools.partial(cross_kernel, width),
            [shape((half, channels), BF16), shape((cross_rows, LANES), F32)],
            [],
            half * channels * channels,
            here, before,
        )
        cross_column = z_gather(scatter_sum(cross))
        ours = xy_gather(cross_column)
        theirs = swap(jnp.stack(ours), "core")
        (inv,) = call(
            functools.partial(inverse_kernel, width),
            [shape((channels, channels), F32)],
            [pltpu.VMEM((sym_rows, LANES), F32)] + [square(2), square16(2), square16(2)] * 2,
            60 * channels**3,
            *pieces,
        )
        (refl,) = call(
            reflect_kernel,
            [shape((channels, channels), BF16)],
            [pltpu.VMEM((cross_rows, LANES), F32)] + [square16()] * 4,
            6 * channels**3,
            *ours, theirs, inv,
        )
        refl_core = swap(refl, "core")
        if order == 0:
            late = after(mine, column)
            across2 = swap(late, "y")
            other_core = swap(other, "core")
            across2_core = swap(across2, "core")
            edge = jnp.where(y == 0, here[1, half - 16 :], before_z)
            there, there_shifted = call(
                functools.partial(gather_kernel, width),
                [shape((2, half, channels), BF16), shape((half, channels), BF16)],
                [],
                0,
                other, across2, other_core, across2_core, edge,
            )
        if order < ORDERS - 1:
            here_new, packed = call(
                functools.partial(update_gram_kernel, width),
                [shape((2, half, channels), BF16), shape((sym_rows, LANES), F32)],
                [square16(2), pltpu.VMEM((half, channels), BF16)],
                6 * half * channels * channels,
                here, shifted, refl, refl_core,
            )
            tail = here_new[1, half - 16 :]
            there, there_shifted = call(
                update_delay_kernel,
                [shape((2, half, channels), BF16), shape((half, channels), BF16)],
                [square16(2), pltpu.VMEM((2, 16, channels), BF16)],
                4 * half * channels * channels,
                there, there_shifted, refl, refl_core, from_behind(tail, ("z", "x")), tail,
            )
            here = here_new
    forward, backward = call(
        functools.partial(last_kernel, width),
        [shape((samples, width), BF16)] * 2,
        [square16(2)],
        4 * samples * channels * width,
        here, shifted, there, there_shifted, refl, refl_core,
    )
    return forward, backward


def solution(mesh):
    tm, chan = mesh.shape["tm"], mesh.shape["chan"]
    split = Mesh(mesh.devices.reshape(tm // 2, 2, chan // 2, 2), ("z", "x", "y", "core"))
    spec = P(("z", "x"), ("y", "core"))
    return jax.shard_map(local, mesh=split, in_specs=(spec, spec), out_specs=(spec, spec), check_vma=False)
```

time: 460 us -> 203 us (0.44)
  waiting for transfers between devices: 301 us -> 55.9 us
  matrix products: 109 us -> 0 us
  blocking collectives: 0 us -> 42.3 us
  starting transfers between devices: 19 us -> 58.5 us
  Pallas kernels: 0 us -> 36 us
  between operations: 17.6 us -> 0.98 us
    psum x2 -> x0, waiting for transfers between devices: 279 us -> none  [local(): lax.psum((cov_fwd, cov_bwd, cov_cross), ('tm', 'chan'))]
    dot_general x62 -> x0, matrix products: 109 us -> none  [the longest x24 45 us: full_inverse(): iterate = 2.0 * iterate - jnp.dot(product, iterate, precision=HIGH)]
    ppermute x2 -> x38, starting transfers between devices: 3.83 us -> 50.4 us  [the longest x12 17.2 us: z_gather(): lax.ppermute(piece, 'z', shift(by))]
    all_to_all x0 -> x2, blocking collectives: none -> 42.3 us  [scatter_sum(): return jnp.sum(lax.all_to_all(cut, PARTS, 0, 0, tiled=True), axis=0)]
    pallas_call x0 -> x11, Pallas kernels: none -> 36 us  [call(): pl.pallas_call(body, out_shape=shapes, in_specs=[VMEM] * len(args), out_s...]
    ppermute x2 -> x38, waiting for transfers between devices: 0.01 us -> 32.3 us  [the longest x18 21.9 us: swap(): return lax.ppermute(value, axis, [(0, 1), (1, 0)])]
    all_to_all x4 -> x2, starting transfers between devices: 14.9 us -> 8.16 us  [scatter_sum(): return jnp.sum(lax.all_to_all(cut, PARTS, 0, 0, tiled=True), axis=0)]
    all_to_all x4 -> x2, waiting for transfers between devices: 22.1 us -> 23.6 us  [scatter_sum(): return jnp.sum(lax.all_to_all(cut, PARTS, 0, 0, tiled=True), axis=0)]
  transfers between devices with their start and end apart: 8 -> 40, of which waited for: 5 -> 18; matrix products, arithmetic and copies ran while one was open for 7% -> 2% of each run, Pallas kernels for 0% -> 12%
where the time goes in v1:
time: 203 us; the launch traced here: 202 us
  starting transfers between devices  58.5 us (29%)
  waiting for transfers between devices  55.9 us (28%)
  blocking collectives  42.3 us (21%)
  Pallas kernels  36 us (18%)
  other arithmetic  4.41 us (2%)
  local copies, waits for them, and re-layouts  4.41 us (2%)
    all_to_all x2, blocking collectives, scatter_sum(): return jnp.sum(lax.all_to_all(cut, PARTS, 0, 0, tiled=True), axis=0)  42.3 us
    pallas_call x11, Pallas kernels, call(): pl.pallas_call(body, out_shape=shapes, in_specs=[VMEM] * len(args), out_s...  36 us
    all_to_all x2, waiting for transfers between devices, scatter_sum(): return jnp.sum(lax.all_to_all(cut, PARTS, 0, 0, tiled=True), axis=0)  23.6 us
    ppermute x18, waiting for transfers between devices, swap(): return lax.ppermute(value, axis, [(0, 1), (1, 0)])  21.9 us
    ppermute x12, starting transfers between devices, z_gather(): lax.ppermute(piece, 'z', shift(by))  17.2 us
    ppermute x18, starting transfers between devices, swap(): return lax.ppermute(value, axis, [(0, 1), (1, 0)])  13.9 us
    ppermute x4, starting transfers between devices, from_behind(): return lax.ppermute(value, axes, [(i, i + 1) for i in range(devices - 1)])  13.6 us
    all_to_all x2, starting transfers between devices, scatter_sum(): return jnp.sum(lax.all_to_all(cut, PARTS, 0, 0, tiled=True), axis=0)  8.16 us
  transfers between devices with their start and end apart: 40, of which 18 were waited for; matrix products, arithmetic and copies ran while one was open for 2% of the time, Pallas kernels for 12%

profile of v1, /device:TPU:0, one launch (start us, length us, event | category | flops | bytes accessed | tf_op | source)
XLA Modules:
  0.0 202.4 jit_solution(12626616976591070042)
XLA Ops:
  1.9 3.0 %collective-permute-start = (bf16[2,1024,128]{2,1,0:T(8,128)(2,1)S(1)}, bf16[2,1024,128]{2,1,0:T(8,128)(2,1)S(1)}, u32[]{:S(2)}, u32[]{:S(2)}) collective-permute-start(bf16[2,1024,128]{2,1,0:T(8,128)(2,1)S(1)} %get-tuple-element.28.refs_0_), channel_id=1, source_target_pairs={{0,2},{2,0},{1,3},{3,1},{4,6},{6,4},{5,7},{7,5},{8,10},{10,8},{9,1... | collective-permute-start | bytes 1572872 | tf_op jit(solution)/shard_map/ppermute | solution.py:20
  4.9 11.9 %collective-permute-done.refs_1_ = bf16[2,1024,128]{2,1,0:T(8,128)(2,1)S(1)} collective-permute-done((bf16[2,1024,128]{2,1,0:T(8,128)(2,1)S(1)}, bf16[2,1024,128]{2,1,0:T(8,128)(2,1)S(1)}, u32[]{:S(2)}, u32[]{:S(2)}) %collective-permute-start) | collective-permute-done | bytes 524320 | tf_op jit(solution)/shard_map/ppermute | solution.py:20
  16.9 1.9 collective-permute-done.2.refs_3_
  18.8 2.0 shard_map.41
  20.8 3.6 %collective-permute-start.3 = (bf16[16,512]{1,0:T(8,128)(2,1)S(1)}, bf16[16,512]{1,0:T(8,128)(2,1)S(1)}, u32[]{:S(2)}, u32[]{:S(2)}) collective-permute-start(bf16[16,512]{1,0:T(8,128)(2,1)S(1)} %slice_bitcast_fusion.1), channel_id=1, source_target_pairs={{0,2},{2,4},{4,6},{6,8},{8,10},{10,12},{12,14},{14,16},{16,18},{18... | collective-permute-start | bytes 49160 | tf_op jit(solution)/shard_map/ppermute | solution.py:25
  27.7 21.8 %all_to_all.20 = f32[16,64,128]{2,1,0:T(8,128)S(1)} all-to-all(f32[16,64,128]{2,1,0:T(8,128)S(1)} %bitcast.39), channel_id=1, replica_groups=mesh['z'=4,'x'=2,'y'=2,'core'=2] {'z','x','y'}, dimensions={0} | all-to-all | bytes 1048576 | tf_op jit(solution)/shard_map/all_to_all | solution.py:267
  49.5 3.9 %all-to-all-start.1 = ((f32[16,80,128]{2,1,0:T(8,128)}), f32[16,80,128]{2,1,0:T(8,128)S(1)}, u32[]{:S(2)}, u32[]{:S(2)}) async-start(f32[16,80,128]{2,1,0:T(8,128)} %bitcast.12), calls=%async_computation.1 | async-start | bytes 1310720 | tf_op jit(solution)/shard_map/all_to_all | solution.py:267
  53.4 3.8 %collective-permute-start.6 = (f32[64,128]{1,0:T(8,128)S(1)}, f32[64,128]{1,0:T(8,128)S(1)}, u32[]{:S(2)}, u32[]{:S(2)}) collective-permute-start(f32[64,128]{1,0:T(8,128)S(1)} %reduce_sum.36), channel_id=1, source_target_pairs={{0,24},{8,0},{16,8},{24,16},{1,25},{9,1},{17,9},{25,17},{2,26},{10... | collective-permute-start | bytes 98312 | tf_op jit(solution)/shard_map/ppermute | solution.py:273
  58.3 13.0 %all-to-all-done.1 = f32[16,80,128]{2,1,0:T(8,128)S(1)} async-done(((f32[16,80,128]{2,1,0:T(8,128)}), f32[16,80,128]{2,1,0:T(8,128)S(1)}, u32[]{:S(2)}, u32[]{:S(2)}) %all-to-all-start.1) | async-done | bytes 655392 | tf_op jit(solution)/shard_map/all_to_all | solution.py:267
  71.3 2.3 %collective-permute-start.13 = (f32[80,128]{1,0:T(8,128)S(1)}, f32[80,128]{1,0:T(8,128)S(1)}, u32[]{:S(2)}, u32[]{:S(2)}) collective-permute-start(f32[80,128]{1,0:T(8,128)S(1)} %reduce_sum.37), channel_id=1, source_target_pairs={{0,24},{8,0},{16,8},{24,16},{1,25},{9,1},{17,9},{25,17},{2,26},{10... | collective-permute-start | bytes 122888 | tf_op jit(solution)/shard_map/ppermute | solution.py:273
  76.7 1.7 collective-permute-start.8
  78.9 2.0 %collective-permute-done.11 = f32[80,128]{1,0:T(8,128)S(1)} collective-permute-done((f32[80,128]{1,0:T(8,128)S(1)}, f32[80,128]{1,0:T(8,128)S(1)}, u32[]{:S(2)}, u32[]{:S(2)}) %collective-permute-start.11) | collective-permute-done | bytes 40992 | tf_op jit(solution)/shard_map/ppermute | solution.py:273
  86.4 1.7 collective-permute-done.16.refs_3_
  88.1 1.7 collective-permute-done.15.refs_2_
  89.8 9.4 %shard_map.43.refs_5_ = f32[512,512]{1,0:T(8,128)S(1)} custom-call(f32[4,80,128]{2,1,0:T(8,128)S(1)} %pad_maximum_fusion.2.refs_0_, f32[4,80,128]{2,1,0:T(8,128)S(1)} %collective-permute-done.14.refs_1_, f32[4,80,128]{2,1,0:T(8,128)S(1)} %collective-permute-done.15.refs_2_, f32[4,80,128]{2,1,0:T(8,128)S(1)} %collective-permute-done.16.refs_3_), custom_call_target="tpu_custom_call" | custom-call | flops 8053063680 | bytes 1703936 | tf_op jit(solution)/shard_map/pallas_call | solution.py:34
  101.0 1.9 collective-permute-done.17.theirs
  102.9 2.8 %shard_map.45 = (bf16[2,1024,512]{2,1,0:T(8,128)(2,1)S(1)}, f32[1280,128]{1,0:T(8,128)S(1)}) custom-call(bf16[2,1024,512]{2,1,0:T(8,128)(2,1)S(1)} %copy-done.1, bf16[1024,512]{1,0:T(8,128)(2,1)S(1)} %copy-done.10, bf16[512,512]{1,0:T(8,128)(2,1)S(1)} %shard_map.44.ours, bf16[512,512]{1,0:T(8,128)(2,1)S(1)} %collective-permute-done.17.theirs), custom_call_target="tpu_custom_call" | custom-call | flops 1610612736 | bytes 6946816 | tf_op jit(solution)/shard_map/pallas_call | solution.py:34
  105.8 3.3 %collective-permute-start.18 = (bf16[16,512]{1,0:T(8,128)(2,1)S(1)}, bf16[16,512]{1,0:T(8,128)(2,1)S(1)}, u32[]{:S(2)}, u32[]{:S(2)}) collective-permute-start(bf16[16,512]{1,0:T(8,128)(2,1)S(1)} %slice_bitcast_fusion.ours_tail), channel_id=1, source_target_pairs={{0,2},{2,4},{4,6},{6,8},{8,10},{10,12},{12,14},{14,16},{16,18},{18... | collective-permute-start | bytes 49160 | tf_op jit(solution)/shard_map/ppermute | solution.py:25
  112.0 20.5 %all_to_all.21 = f32[16,64,128]{2,1,0:T(8,128)} all-to-all(f32[16,64,128]{2,1,0:T(8,128)S(1)} %bitcast.40), channel_id=1, replica_groups=mesh['z'=4,'x'=2,'y'=2,'core'=2] {'z','x','y'}, dimensions={0} | all-to-all | bytes 1048576 | tf_op jit(solution)/shard_map/all_to_all | solution.py:267
  132.5 4.3 %all-to-all-start.3 = ((f32[16,80,128]{2,1,0:T(8,128)}), f32[16,80,128]{2,1,0:T(8,128)}, u32[]{:S(2)}, u32[]{:S(2)}) async-start(f32[16,80,128]{2,1,0:T(8,128)} %bitcast.38), calls=%async_computation.3 | async-start | bytes 1310720 | tf_op jit(solution)/shard_map/all_to_all | solution.py:267
  136.7 1.8 collective-permute-start.19
  139.6 3.4 %collective-permute-start.26 = (f32[64,128]{1,0:T(8,128)S(1)}, f32[64,128]{1,0:T(8,128)S(1)}, u32[]{:S(2)}, u32[]{:S(2)}) collective-permute-start(f32[64,128]{1,0:T(8,128)S(1)} %reduce_sum.38), channel_id=1, source_target_pairs={{0,24},{8,0},{16,8},{24,16},{1,25},{9,1},{17,9},{25,17},{2,26},{10... | collective-permute-start | bytes 98312 | tf_op jit(solution)/shard_map/ppermute | solution.py:273
  144.1 10.6 %all-to-all-done.3 = f32[16,80,128]{2,1,0:T(8,128)} async-done(((f32[16,80,128]{2,1,0:T(8,128)}), f32[16,80,128]{2,1,0:T(8,128)}, u32[]{:S(2)}, u32[]{:S(2)}) %all-to-all-start.3) | async-done | bytes 655392 | tf_op jit(solution)/shard_map/all_to_all | solution.py:267
  155.8 2.1 %collective-permute-start.33 = (f32[80,128]{1,0:T(8,128)S(1)}, f32[80,128]{1,0:T(8,128)S(1)}, u32[]{:S(2)}, u32[]{:S(2)}) collective-permute-start(f32[80,128]{1,0:T(8,128)S(1)} %reduce_sum.39), channel_id=1, source_target_pairs={{0,24},{8,0},{16,8},{24,16},{1,25},{9,1},{17,9},{25,17},{2,26},{10... | collective-permute-start | bytes 122888 | tf_op jit(solution)/shard_map/ppermute | solution.py:273
  163.4 1.8 collective-permute-done.31
  170.3 1.7 collective-permute-done.36.refs_3_
  173.7 9.4 %shard_map.49.refs_5_ = f32[512,512]{1,0:T(8,128)S(1)} custom-call(f32[4,80,128]{2,1,0:T(8,128)S(1)} %pad_maximum_fusion.3.refs_0_, f32[4,80,128]{2,1,0:T(8,128)S(1)} %collective-permute-done.34.refs_1_, f32[4,80,128]{2,1,0:T(8,128)S(1)} %collective-permute-done.35.refs_2_, f32[4,80,128]{2,1,0:T(8,128)S(1)} %collective-permute-done.36.refs_3_), custom_call_target="tpu_custom_call" | custom-call | flops 8053063680 | bytes 1703936 | tf_op jit(solution)/shard_map/pallas_call | solution.py:34
  183.2 2.7 %shard_map.50.ours = bf16[512,512]{1,0:T(8,128)(2,1)} custom-call(f32[4,64,128]{2,1,0:T(8,128)S(1)} %get-tuple-element.31.refs_0_, f32[4,64,128]{2,1,0:T(8,128)S(1)} %collective-permute-done.27.refs_1_, f32[4,64,128]{2,1,0:T(8,128)S(1)} %collective-permute-done.28.refs_2_, f32[4,64,128]{2,1,0:T(8,128)S(1)} %collective-permute-done.29.refs_3_, ...), custom_call_target="tpu_custom_call" | custom-call | flops 805306368 | bytes 2621440 | tf_op jit(solution)/shard_map/pallas_call | solution.py:34
  185.8 3.5 %collective-permute-start.22 = (bf16[16,512]{1,0:T(8,128)(2,1)S(1)}, bf16[16,512]{1,0:T(8,128)(2,1)S(1)}, u32[]{:S(2)}, u32[]{:S(2)}) collective-permute-start(bf16[16,512]{1,0:T(8,128)(2,1)S(1)} %slice_bitcast_fusion.1), channel_id=1, source_target_pairs={{0,4},{4,8},{8,12},{12,16},{16,20},{20,24},{24,28},{1,5},{5,9},{9,... | collective-permute-start | bytes 49160 | tf_op jit(solution)/shard_map/ppermute | solution.py:25
  189.3 3.2 %collective-permute-start.23 = (bf16[16,512]{1,0:T(8,128)(2,1)S(1)}, bf16[16,512]{1,0:T(8,128)(2,1)S(1)}, u32[]{:S(2)}, u32[]{:S(2)}) collective-permute-start(bf16[16,512]{1,0:T(8,128)(2,1)S(1)} %slice_bitcast_fusion.ours_tail), channel_id=1, source_target_pairs={{0,4},{4,8},{8,12},{12,16},{16,20},{20,24},{24,28},{1,5},{5,9},{9,... | collective-permute-start | bytes 49160 | tf_op jit(solution)/shard_map/ppermute | solution.py:25
  193.3 2.2 %shard_map.47 = (bf16[2,1024,512]{2,1,0:T(8,128)(2,1)S(1)}, bf16[1024,512]{1,0:T(8,128)(2,1)S(1)}) custom-call(bf16[2,1024,128]{2,1,0:T(8,128)(2,1)S(1)} %get-tuple-element.28.refs_0_, bf16[2,1024,128]{2,1,0:T(8,128)(2,1)} %collective-permute-done.19.refs_1_, bf16[2,1024,128]{2,1,0:T(8,128)(2,1)} %collective-permute-done.20.refs_2_, ...), custom_call_target="tpu_custom_call" | custom-call | bytes 5259264 | tf_op jit(solution)/shard_map/pallas_call | solution.py:34
  199.1 3.4 %shard_map.51 = (bf16[2048,128]{1,0:T(8,128)(2,1)}, bf16[2048,128]{1,0:T(8,128)(2,1)}) custom-call(bf16[2,1024,512]{2,1,0:T(8,128)(2,1)S(1)} %get-tuple-element.19.here, bf16[1024,512]{1,0:T(8,128)(2,1)S(1)} %copy-done.3, bf16[2,1024,512]{2,1,0:T(8,128)(2,1)S(1)} %get-tuple-element.24.there, bf16[1024,512]{1,0:T(8,128)(2,1)S(1)} %get-tuple-element.25.there_shifted, ...), custom_call_target="tpu_custom_call" | custom-call | flops 536870912 | bytes 8388608 | tf_op jit(solution)/shard_map/pallas_call | solution.py:34
  (97 shorter events, 39.2 us)
Async XLA Ops:
  1.9 15.0 %collective-permute-start = (bf16[2,1024,128]{2,1,0:T(8,128)(2,1)S(1)}, bf16[2,1024,128]{2,1,0:T(8,128)(2,1)S(1)}, u32[]{:S(2)}, u32[]{:S(2)}) collective-permute-start(bf16[2,1024,128]{2,1,0:T(8,128)(2,1)S(1)} %get-tuple-element.28.refs_0_), channel_id=1, source_target_pairs={{0,2},{2,0},{1,3},{3,1},{4,6},{6,4},{5,7},{7,5},{8,10},{10,8},{9,1... | collective-permute-start | bytes 1572872 | tf_op jit(solution)/shard_map/ppermute | solution.py:20
  4.9 11.9 %collective-permute-start.1 = (bf16[2,1024,128]{2,1,0:T(8,128)(2,1)S(1)}, bf16[2,1024,128]{2,1,0:T(8,128)(2,1)S(1)}, u32[]{:S(2)}, u32[]{:S(2)}) collective-permute-start(bf16[2,1024,128]{2,1,0:T(8,128)(2,1)S(1)} %get-tuple-element.21.refs_0_), channel_id=1, source_target_pairs={{0,1},{1,0},{2,3},{3,2},{4,5},{5,4},{6,7},{7,6},{8,9},{9,8},{10,11... | collective-permute-start | bytes 1572872 | tf_op jit(solution)/shard_map/ppermute | solution.py:20
  49.5 21.8 %all-to-all-start.1 = ((f32[16,80,128]{2,1,0:T(8,128)}), f32[16,80,128]{2,1,0:T(8,128)S(1)}, u32[]{:S(2)}, u32[]{:S(2)}) async-start(f32[16,80,128]{2,1,0:T(8,128)} %bitcast.12), calls=%async_computation.1 | async-start | bytes 1310720 | tf_op jit(solution)/shard_map/all_to_all | solution.py:267
  53.4 21.8 %collective-permute-start.6 = (f32[64,128]{1,0:T(8,128)S(1)}, f32[64,128]{1,0:T(8,128)S(1)}, u32[]{:S(2)}, u32[]{:S(2)}) collective-permute-start(f32[64,128]{1,0:T(8,128)S(1)} %reduce_sum.36), channel_id=1, source_target_pairs={{0,24},{8,0},{16,8},{24,16},{1,25},{9,1},{17,9},{25,17},{2,26},{10... | collective-permute-start | bytes 98312 | tf_op jit(solution)/shard_map/ppermute | solution.py:273
  57.2 18.2 %collective-permute-start.5 = (f32[64,128]{1,0:T(8,128)S(1)}, f32[64,128]{1,0:T(8,128)S(1)}, u32[]{:S(2)}, u32[]{:S(2)}) collective-permute-start(f32[64,128]{1,0:T(8,128)S(1)} %reduce_sum.36), channel_id=1, source_target_pairs={{0,16},{8,24},{16,0},{24,8},{1,17},{9,25},{17,1},{25,9},{2,18},{10... | collective-permute-start | bytes 98312 | tf_op jit(solution)/shard_map/ppermute | solution.py:273
  57.2 18.2 %collective-permute-start.4 = (f32[64,128]{1,0:T(8,128)S(1)}, f32[64,128]{1,0:T(8,128)S(1)}, u32[]{:S(2)}, u32[]{:S(2)}) collective-permute-start(f32[64,128]{1,0:T(8,128)S(1)} %reduce_sum.36), channel_id=1, source_target_pairs={{0,8},{8,16},{16,24},{24,0},{1,9},{9,17},{17,25},{25,1},{2,10},{10... | collective-permute-start | bytes 98312 | tf_op jit(solution)/shard_map/ppermute | solution.py:273
  71.3 7.0 %collective-permute-start.13 = (f32[80,128]{1,0:T(8,128)S(1)}, f32[80,128]{1,0:T(8,128)S(1)}, u32[]{:S(2)}, u32[]{:S(2)}) collective-permute-start(f32[80,128]{1,0:T(8,128)S(1)} %reduce_sum.37), channel_id=1, source_target_pairs={{0,24},{8,0},{16,8},{24,16},{1,25},{9,1},{17,9},{25,17},{2,26},{10... | collective-permute-start | bytes 122888 | tf_op jit(solution)/shard_map/ppermute | solution.py:273
  75.2 5.8 %collective-permute-start.11 = (f32[80,128]{1,0:T(8,128)S(1)}, f32[80,128]{1,0:T(8,128)S(1)}, u32[]{:S(2)}, u32[]{:S(2)}) collective-permute-start(f32[80,128]{1,0:T(8,128)S(1)} %reduce_sum.37), channel_id=1, source_target_pairs={{0,8},{8,16},{16,24},{24,0},{1,9},{9,17},{17,25},{25,1},{2,10},{10... | collective-permute-start | bytes 122888 | tf_op jit(solution)/shard_map/ppermute | solution.py:273
  75.4 7.7 %collective-permute-start.9 = (f32[4,64,128]{2,1,0:T(8,128)S(1)}, f32[4,64,128]{2,1,0:T(8,128)S(1)}, u32[]{:S(2)}, u32[]{:S(2)}) collective-permute-start(f32[4,64,128]{2,1,0:T(8,128)S(1)} %get-tuple-element.33.refs_0_), channel_id=1, source_target_pairs={{0,6},{2,4},{4,2},{6,0},{1,7},{3,5},{5,3},{7,1},{8,14},{10,12},{12... | collective-permute-start | bytes 393224 | tf_op jit(solution)/shard_map/ppermute | solution.py:281
  76.7 8.8 %collective-permute-start.8 = (f32[4,64,128]{2,1,0:T(8,128)S(1)}, f32[4,64,128]{2,1,0:T(8,128)S(1)}, u32[]{:S(2)}, u32[]{:S(2)}) collective-permute-start(f32[4,64,128]{2,1,0:T(8,128)S(1)} %get-tuple-element.33.refs_0_), channel_id=1, source_target_pairs={{0,4},{4,0},{1,5},{5,1},{2,6},{6,2},{3,7},{7,3},{8,12},{12,8},{9,1... | collective-permute-start | bytes 393224 | tf_op jit(solution)/shard_map/ppermute | solution.py:20
  78.4 7.9 %collective-permute-start.7 = (f32[4,64,128]{2,1,0:T(8,128)S(1)}, f32[4,64,128]{2,1,0:T(8,128)S(1)}, u32[]{:S(2)}, u32[]{:S(2)}) collective-permute-start(f32[4,64,128]{2,1,0:T(8,128)S(1)} %get-tuple-element.33.refs_0_), channel_id=1, source_target_pairs={{0,2},{2,0},{1,3},{3,1},{4,6},{6,4},{5,7},{7,5},{8,10},{10,8},{9,1... | collective-permute-start | bytes 393224 | tf_op jit(solution)/shard_map/ppermute | solution.py:20
  81.0 7.1 %collective-permute-start.16 = (f32[4,80,128]{2,1,0:T(8,128)S(1)}, f32[4,80,128]{2,1,0:T(8,128)S(1)}, u32[]{:S(2)}, u32[]{:S(2)}) collective-permute-start(f32[4,80,128]{2,1,0:T(8,128)S(1)} %pad_maximum_fusion.2.refs_0_), channel_id=1, source_target_pairs={{0,6},{2,4},{4,2},{6,0},{1,7},{3,5},{5,3},{7,1},{8,14},{10,12},{12... | collective-permute-start | bytes 491528 | tf_op jit(solution)/shard_map/ppermute | solution.py:281
  82.5 7.4 %collective-permute-start.15 = (f32[4,80,128]{2,1,0:T(8,128)S(1)}, f32[4,80,128]{2,1,0:T(8,128)S(1)}, u32[]{:S(2)}, u32[]{:S(2)}) collective-permute-start(f32[4,80,128]{2,1,0:T(8,128)S(1)} %pad_maximum_fusion.2.refs_0_), channel_id=1, source_target_pairs={{0,4},{4,0},{1,5},{5,1},{2,6},{6,2},{3,7},{7,3},{8,12},{12,8},{9,1... | collective-permute-start | bytes 491528 | tf_op jit(solution)/shard_map/ppermute | solution.py:20
  83.1 6.7 %collective-permute-start.14 = (f32[4,80,128]{2,1,0:T(8,128)S(1)}, f32[4,80,128]{2,1,0:T(8,128)S(1)}, u32[]{:S(2)}, u32[]{:S(2)}) collective-permute-start(f32[4,80,128]{2,1,0:T(8,128)S(1)} %pad_maximum_fusion.2.refs_0_), channel_id=1, source_target_pairs={{0,2},{2,0},{1,3},{3,1},{4,6},{6,4},{5,7},{7,5},{8,10},{10,8},{9,1... | collective-permute-start | bytes 491528 | tf_op jit(solution)/shard_map/ppermute | solution.py:20
  86.3 13.0 %collective-permute-start.10 = (f32[4,4,64,128]{3,2,1,0:T(8,128)S(1)}, f32[4,4,64,128]{3,2,1,0:T(8,128)S(1)}, u32[]{:S(2)}, u32[]{:S(2)}) collective-permute-start(f32[4,4,64,128]{3,2,1,0:T(8,128)S(1)} %pad_maximum_fusion), channel_id=1, source_target_pairs={{0,1},{1,0},{2,3},{3,2},{4,5},{5,4},{6,7},{7,6},{8,9},{9,8},{10,11... | collective-permute-start | bytes 1572872 | tf_op jit(solution)/shard_map/ppermute | solution.py:20
  132.5 22.2 %all-to-all-start.3 = ((f32[16,80,128]{2,1,0:T(8,128)}), f32[16,80,128]{2,1,0:T(8,128)}, u32[]{:S(2)}, u32[]{:S(2)}) async-start(f32[16,80,128]{2,1,0:T(8,128)} %bitcast.38), calls=%async_computation.3 | async-start | bytes 1310720 | tf_op jit(solution)/shard_map/all_to_all | solution.py:267
  136.7 30.0 %collective-permute-start.19 = (bf16[2,1024,128]{2,1,0:T(8,128)(2,1)S(1)}, bf16[2,1024,128]{2,1,0:T(8,128)(2,1)}, u32[]{:S(2)}, u32[]{:S(2)}) collective-permute-start(bf16[2,1024,128]{2,1,0:T(8,128)(2,1)S(1)} %get-tuple-element.21.refs_0_), channel_id=1, source_target_pairs={{0,2},{2,0},{1,3},{3,1},{4,6},{6,4},{5,7},{7,5},{8,10},{10,8},{9,1... | collective-permute-start | bytes 1572872 | tf_op jit(solution)/shard_map/ppermute | solution.py:20
  139.6 18.3 %collective-permute-start.26 = (f32[64,128]{1,0:T(8,128)S(1)}, f32[64,128]{1,0:T(8,128)S(1)}, u32[]{:S(2)}, u32[]{:S(2)}) collective-permute-start(f32[64,128]{1,0:T(8,128)S(1)} %reduce_sum.38), channel_id=1, source_target_pairs={{0,24},{8,0},{16,8},{24,16},{1,25},{9,1},{17,9},{25,17},{2,26},{10... | collective-permute-start | bytes 98312 | tf_op jit(solution)/shard_map/ppermute | solution.py:273
  143.0 16.5 %collective-permute-start.25 = (f32[64,128]{1,0:T(8,128)S(1)}, f32[64,128]{1,0:T(8,128)S(1)}, u32[]{:S(2)}, u32[]{:S(2)}) collective-permute-start(f32[64,128]{1,0:T(8,128)S(1)} %reduce_sum.38), channel_id=1, source_target_pairs={{0,16},{8,24},{16,0},{24,8},{1,17},{9,25},{17,1},{25,9},{2,18},{10... | collective-permute-start | bytes 98312 | tf_op jit(solution)/shard_map/ppermute | solution.py:273
  143.0 16.6 %collective-permute-start.24 = (f32[64,128]{1,0:T(8,128)S(1)}, f32[64,128]{1,0:T(8,128)S(1)}, u32[]{:S(2)}, u32[]{:S(2)}) collective-permute-start(f32[64,128]{1,0:T(8,128)S(1)} %reduce_sum.38), channel_id=1, source_target_pairs={{0,8},{8,16},{16,24},{24,0},{1,9},{9,17},{17,25},{25,1},{2,10},{10... | collective-permute-start | bytes 98312 | tf_op jit(solution)/shard_map/ppermute | solution.py:273
  159.6 7.8 %collective-permute-start.29 = (f32[4,64,128]{2,1,0:T(8,128)S(1)}, f32[4,64,128]{2,1,0:T(8,128)S(1)}, u32[]{:S(2)}, u32[]{:S(2)}) collective-permute-start(f32[4,64,128]{2,1,0:T(8,128)S(1)} %get-tuple-element.31.refs_0_), channel_id=1, source_target_pairs={{0,6},{2,4},{4,2},{6,0},{1,7},{3,5},{5,3},{7,1},{8,14},{10,12},{12... | collective-permute-start | bytes 393224 | tf_op jit(solution)/shard_map/ppermute | solution.py:281
  161.0 8.8 %collective-permute-start.28 = (f32[4,64,128]{2,1,0:T(8,128)S(1)}, f32[4,64,128]{2,1,0:T(8,128)S(1)}, u32[]{:S(2)}, u32[]{:S(2)}) collective-permute-start(f32[4,64,128]{2,1,0:T(8,128)S(1)} %get-tuple-element.31.refs_0_), channel_id=1, source_target_pairs={{0,4},{4,0},{1,5},{5,1},{2,6},{6,2},{3,7},{7,3},{8,12},{12,8},{9,1... | collective-permute-start | bytes 393224 | tf_op jit(solution)/shard_map/ppermute | solution.py:20
  162.9 7.0 %collective-permute-start.27 = (f32[4,64,128]{2,1,0:T(8,128)S(1)}, f32[4,64,128]{2,1,0:T(8,128)S(1)}, u32[]{:S(2)}, u32[]{:S(2)}) collective-permute-start(f32[4,64,128]{2,1,0:T(8,128)S(1)} %get-tuple-element.31.refs_0_), channel_id=1, source_target_pairs={{0,2},{2,0},{1,3},{3,1},{4,6},{6,4},{5,7},{7,5},{8,10},{10,8},{9,1... | collective-permute-start | bytes 393224 | tf_op jit(solution)/shard_map/ppermute | solution.py:20
  165.3 6.7 %collective-permute-start.36 = (f32[4,80,128]{2,1,0:T(8,128)S(1)}, f32[4,80,128]{2,1,0:T(8,128)S(1)}, u32[]{:S(2)}, u32[]{:S(2)}) collective-permute-start(f32[4,80,128]{2,1,0:T(8,128)S(1)} %pad_maximum_fusion.3.refs_0_), channel_id=1, source_target_pairs={{0,6},{2,4},{4,2},{6,0},{1,7},{3,5},{5,3},{7,1},{8,14},{10,12},{12... | collective-permute-start | bytes 491528 | tf_op jit(solution)/shard_map/ppermute | solution.py:281
  166.8 6.9 %collective-permute-start.35 = (f32[4,80,128]{2,1,0:T(8,128)S(1)}, f32[4,80,128]{2,1,0:T(8,128)S(1)}, u32[]{:S(2)}, u32[]{:S(2)}) collective-permute-start(f32[4,80,128]{2,1,0:T(8,128)S(1)} %pad_maximum_fusion.3.refs_0_), channel_id=1, source_target_pairs={{0,4},{4,0},{1,5},{5,1},{2,6},{6,2},{3,7},{7,3},{8,12},{12,8},{9,1... | collective-permute-start | bytes 491528 | tf_op jit(solution)/shard_map/ppermute | solution.py:20
  167.4 6.3 %collective-permute-start.34 = (f32[4,80,128]{2,1,0:T(8,128)S(1)}, f32[4,80,128]{2,1,0:T(8,128)S(1)}, u32[]{:S(2)}, u32[]{:S(2)}) collective-permute-start(f32[4,80,128]{2,1,0:T(8,128)S(1)} %pad_maximum_fusion.3.refs_0_), channel_id=1, source_target_pairs={{0,2},{2,0},{1,3},{3,1},{4,6},{6,4},{5,7},{7,5},{8,10},{10,8},{9,1... | collective-permute-start | bytes 491528 | tf_op jit(solution)/shard_map/ppermute | solution.py:20
  169.8 23.5 %collective-permute-start.20 = (bf16[2,1024,128]{2,1,0:T(8,128)(2,1)S(1)}, bf16[2,1024,128]{2,1,0:T(8,128)(2,1)}, u32[]{:S(2)}, u32[]{:S(2)}) collective-permute-start(bf16[2,1024,128]{2,1,0:T(8,128)(2,1)S(1)} %get-tuple-element.28.refs_0_), channel_id=1, source_target_pairs={{0,1},{1,0},{2,3},{3,2},{4,5},{5,4},{6,7},{7,6},{8,9},{9,8},{10,11... | collective-permute-start | bytes 1572872 | tf_op jit(solution)/shard_map/ppermute | solution.py:20
  169.9 23.4 %collective-permute-start.21 = (bf16[2,1024,128]{2,1,0:T(8,128)(2,1)}, bf16[2,1024,128]{2,1,0:T(8,128)(2,1)}, u32[]{:S(2)}, u32[]{:S(2)}) collective-permute-start(bf16[2,1024,128]{2,1,0:T(8,128)(2,1)} %collective-permute-done.19.refs_1_), channel_id=1, source_target_pairs={{0,1},{1,0},{2,3},{3,2},{4,5},{5,4},{6,7},{7,6},{8,9},{9,8},{10,11... | collective-permute-start | bytes 1572872 | tf_op jit(solution)/shard_map/ppermute | solution.py:20
  172.0 11.1 %collective-permute-start.30 = (f32[4,4,64,128]{3,2,1,0:T(8,128)S(1)}, f32[4,4,64,128]{3,2,1,0:T(8,128)S(1)}, u32[]{:S(2)}, u32[]{:S(2)}) collective-permute-start(f32[4,4,64,128]{3,2,1,0:T(8,128)S(1)} %pad_maximum_fusion.1), channel_id=1, source_target_pairs={{0,1},{1,0},{2,3},{3,2},{4,5},{5,4},{6,7},{7,6},{8,9},{9,8},{10,11... | collective-permute-start | bytes 1572872 | tf_op jit(solution)/shard_map/ppermute | solution.py:20
  185.8 13.2 %collective-permute-start.37 = (bf16[512,512]{1,0:T(8,128)(2,1)}, bf16[512,512]{1,0:T(8,128)(2,1)}, u32[]{:S(2)}, u32[]{:S(2)}) collective-permute-start(bf16[512,512]{1,0:T(8,128)(2,1)} %shard_map.50.ours), channel_id=1, source_target_pairs={{0,1},{1,0},{2,3},{3,2},{4,5},{5,4},{6,7},{7,6},{8,9},{9,8},{10,11... | collective-permute-start | bytes 1572872 | tf_op jit(solution)/shard_map/ppermute | solution.py:20
  185.8 6.7 %collective-permute-start.22 = (bf16[16,512]{1,0:T(8,128)(2,1)S(1)}, bf16[16,512]{1,0:T(8,128)(2,1)S(1)}, u32[]{:S(2)}, u32[]{:S(2)}) collective-permute-start(bf16[16,512]{1,0:T(8,128)(2,1)S(1)} %slice_bitcast_fusion.1), channel_id=1, source_target_pairs={{0,4},{4,8},{8,12},{12,16},{16,20},{20,24},{24,28},{1,5},{5,9},{9,... | collective-permute-start | bytes 49160 | tf_op jit(solution)/shard_map/ppermute | solution.py:25
  189.3 6.1 %collective-permute-start.23 = (bf16[16,512]{1,0:T(8,128)(2,1)S(1)}, bf16[16,512]{1,0:T(8,128)(2,1)S(1)}, u32[]{:S(2)}, u32[]{:S(2)}) collective-permute-start(bf16[16,512]{1,0:T(8,128)(2,1)S(1)} %slice_bitcast_fusion.ours_tail), channel_id=1, source_target_pairs={{0,4},{4,8},{8,12},{12,16},{16,20},{20,24},{24,28},{1,5},{5,9},{9,... | collective-permute-start | bytes 49160 | tf_op jit(solution)/shard_map/ppermute | solution.py:25
  (19 other events, 113.8 us)

commit v2 on v0

v2 whole, which is shorter than its diff:
```python
import functools

import jax
import jax.numpy as jnp
from jax import lax
from jax.experimental import pallas as pl
from jax.experimental.pallas import tpu as pltpu
from jax.sharding import Mesh, PartitionSpec as P

ORDERS = 2
NSTEPS = 6
F32 = jnp.float32
BF16 = jnp.bfloat16
PARTS = ("z", "x", "y")
LANES = 128
VMEM = pl.BlockSpec(memory_space=pltpu.VMEM)


def swap(value, axis):
    return lax.ppermute(value, axis, [(0, 1), (1, 0)])


def from_behind(value, axes):
    devices = lax.axis_size(axes)
    return lax.ppermute(value, axes, [(i, i + 1) for i in range(devices - 1)])


def after(value, *others):
    return lax.optimization_barrier((value,) + others)[0]


def call(body, shapes, scratch, flops, *args):
    size = sum(a.size * a.dtype.itemsize for a in args) + sum(s.size * s.dtype.itemsize for s in shapes)
    return pl.pallas_call(
        body,
        out_shape=shapes,
        in_specs=[VMEM] * len(args),
        out_specs=[VMEM] * len(shapes),
        scratch_shapes=scratch,
        compiler_params=pltpu.CompilerParams(vmem_limit_bytes=16 << 20),
        cost_estimate=pl.CostEstimate(flops=flops, bytes_accessed=size, transcendentals=0),
    )(*args)


def dot(a, b):
    return jnp.dot(a, b, preferred_element_type=F32)


def dot_first(a, b):
    return lax.dot_general(a, b, (((0,), (0,)), ((), ())), preferred_element_type=F32)


def dot_last(a, b):
    return lax.dot_general(a, b, (((1,), (1,)), ((), ())), preferred_element_type=F32)


def halves(value):
    high = value.astype(BF16)
    return high, (value - high.astype(F32)).astype(BF16)


def thirds(value):
    high, rest = value.astype(BF16), value - value.astype(BF16).astype(F32)
    return (high,) + halves(rest)


def at(index, size):
    return pl.ds(pl.multiple_of(index * size, size), size)


def delay(source, before, out):
    rows = source.shape[0]
    step = min(rows, 256)
    top = lax.broadcasted_iota(jnp.int32, (step, 1), 0) == 0
    for r in range(0, rows, step):
        edge = (before[...] if r == 0 else source[r - 16 : r]).astype(F32)[15:16]
        moved = pltpu.roll(source[r : r + step].astype(F32), 1, 0)
        out[r : r + step] = jnp.where(top, edge, moved).astype(BF16)


def drop_end(samples, here):
    rows = samples.shape[0]

    @pl.when((lax.axis_index("core") == 1) & here)
    def _():
        tail = samples[rows - 16 :].astype(F32)
        inside = lax.broadcasted_iota(jnp.int32, (16, 1), 0) < 15
        samples[rows - 16 :] = jnp.where(inside, tail, 0.0).astype(BF16)


def emit(blocks, flat, outs, start, each):
    used = 0
    for block in blocks:
        flat[used : used + block.shape[0]] = block
        used += block.shape[0]
    depth = outs[0].shape[0]
    parts = depth * len(outs)
    if parts * each > used:
        flat[used : parts * each] = jnp.zeros((parts * each - used, LANES), F32)
    z, x, y = lax.axis_index("z"), lax.axis_index("x"), lax.axis_index("y")
    for i, out in enumerate(outs):
        for k in range(depth):
            part = lax.rem(z + k, depth) * len(outs) + ((x * 2 + y if len(outs) == 4 else x) ^ i)
            out[k, start : start + each] = flat[at(part, each)]


def sources(depth):
    z, x, y = lax.axis_index("z"), lax.axis_index("x"), lax.axis_index("y")
    for i in range(4):
        for k in range(depth):
            xs, ys = x ^ (i >> 1), y ^ (i & 1)
            zx = lax.rem(z + depth - k, depth) * 2 + xs
            yield i, k, zx, ys


def gather_blocks(piece, depth, start, near_each, far_each, near, far):
    for i, k, zx, ys in sources(depth):
        near[ys, at(zx, near_each)] = piece(i)[k, start : start + near_each]
        far[at(zx * 2 + ys, far_each)] = piece(i)[k, start + near_each : start + near_each + far_each]


def steps(first, last, errors, highs, lows, its, ihighs, ilows, finish):
    channels = errors.shape[1]
    step = channels // 2
    for n in range(first, last):
        now, later = n % 2, (n + 1) % 2
        for r in range(0, channels, step):
            rows = pl.ds(r, step)
            high, low = highs[now, rows], lows[now, rows]
            if n < NSTEPS - 1:
                value = dot(high, highs[now]) + dot(high, lows[now]) + dot(low, highs[now])
                value = 2.0 * errors[now, rows] - value
                errors[later, rows] = value
                highs[later, rows], lows[later, rows] = halves(value)
            if n >= 1:
                value = dot(high, ihighs[now]) + dot(high, ilows[now]) + dot(low, ihighs[now])
                value = 2.0 * its[now, rows] - value
                if n == NSTEPS - 1:
                    finish(rows, value)
                else:
                    its[later, rows] = value
                    ihighs[later, rows], ilows[later, rows] = halves(value)


def put(table, high, low, slot, rows, cols, value):
    table[slot, rows, cols] = value
    high[slot, rows, cols], low[slot, rows, cols] = halves(value)


def by_kind(ours, theirs, refl):
    core = lax.axis_index("core")
    refl[1 - core] = ours[...]
    refl[core] = theirs[...]


def update(both, shifted, refl, out):
    step = 256
    for r in range(0, both.shape[1], step):
        rows = slice(r, r + step)
        forward, backward = both[0, rows], shifted[rows]
        out[0, rows] = (forward.astype(F32) + dot_last(backward, refl[0])).astype(BF16)
        out[1, rows] = (backward.astype(F32) + dot_last(forward, refl[1])).astype(BF16)


def update_edge(edge, refl, out):
    late = pltpu.roll(edge[1].astype(F32), 1, 0)
    out[...] = (late + dot_last(edge[0], refl[1])).astype(BF16)


def near_kernel(width, pd, xd, both, both_core, halo, halo_core, *refs):
    packed, (chosen, behind, late, edge, flat) = refs[:2], refs[2:]
    core = lax.axis_index("core")
    own, other = at(core, width), at(1 - core, width)
    chosen[:, own], chosen[:, other] = both[core], both_core[core]
    behind[:, own], behind[:, other] = both[1], both_core[1]
    edge[:, own], edge[:, other] = halo[1], halo_core[1]
    zx = ("z", "x")
    drop_end(chosen, lax.axis_index(zx) == lax.axis_size(zx) - 1)
    value = dot_first(chosen[...], chosen[...])
    emit([value[:width, :width], value[:width, width:], value[width:, width:]], flat, packed, 0, pd)
    delay(behind, edge, late)
    value = dot_first(both[0], late[...])
    emit([value[:, :width], value[:, width:]], flat, packed, pd, xd)


def far_kernel(width, po, xo, both, across, both_core, across_core, halo, halo_core, halo_y, halo_y_core, *refs):
    (here, edge, shifted), packed, (tails, samples, flat) = refs[:3], refs[3:7], refs[7:]
    y, core = lax.axis_index("y"), lax.axis_index("core")
    half = here.shape[1]
    pair = 2 * width
    mine, beside = at(y * 2 + core, width), at(y * 2 + 1 - core, width)
    over, over_beside = at((1 - y) * 2 + core, width), at((1 - y) * 2 + 1 - core, width)
    rows = at(y, half)
    here[:, :, mine], here[:, :, beside] = both[:, rows], both_core[:, rows]
    here[:, :, over], here[:, :, over_beside] = across[...], across_core[...]
    edge[:, :, over], edge[:, :, over_beside] = halo_y[...], halo_y_core[...]

    @pl.when(y == 0)
    def _():
        edge[:, :, mine], edge[:, :, beside] = halo[...], halo_core[...]

    @pl.when(y == 1)
    def _():
        edge[:, :, mine], edge[:, :, beside] = both[:, half - 16 : half], both_core[:, half - 16 : half]

    samples[...] = here[core]
    drop_end(samples, lax.axis_index(PARTS) == lax.axis_size(PARTS) - 1)
    value = dot_first(samples[:, :pair], samples[:, pair:])
    blocks = lambda v: [v[i : i + width, j : j + width] for i in (0, width) for j in (0, width)]
    emit(blocks(value), flat, packed, 0, po)
    delay(here.at[1], edge.at[1], shifted)
    value = dot_first(here[0, :, at(core, pair)], shifted[:, at(1 - core, pair)])
    emit(blocks(value), flat, packed, po, xo)
    for i, rows in enumerate((here[0, half - 16 :], shifted[half - 16 :])):
        row = rows.astype(F32)[15:16]
        for j in range(4):
            tails[i * 4 + j : i * 4 + j + 1] = row[:, j * LANES : (j + 1) * LANES]


def inverse_kernel(width, pd, po, stop, *refs):
    pieces, (full, error, iterate, scale), (near, far) = refs[:4], refs[4:8], refs[8:10]
    tables = refs[10:]
    errors, highs, lows, its, ihighs, ilows = tables
    gather_blocks(lambda i: pieces[i], pieces[0].shape[0], 0, pd, po, near, far)
    table = {}
    for i in range(2):
        table[2 * i, 2 * i] = lambda i=i: near[i, :width]
        table[2 * i, 2 * i + 1] = lambda i=i: near[i, width : 2 * width]
        table[2 * i + 1, 2 * i + 1] = lambda i=i: near[i, 2 * width : 3 * width]
        for j in range(2):
            table[i, 2 + j] = lambda i=i, j=j: far[(i * 2 + j) * width : (i * 2 + j + 1) * width]
    norm = jnp.zeros((8, LANES), F32)
    for (i, j), read in table.items():
        block = read()
        squares = jnp.sum((block * block).reshape(-1, 8, LANES), axis=0)
        norm = norm + (squares if i == j else 2.0 * squares)
    factor = lax.rsqrt(jnp.sum(norm, keepdims=True) + 1e-06)
    eye = lax.broadcasted_iota(jnp.int32, (width, width), 0) == lax.broadcasted_iota(jnp.int32, (width, width), 1)
    for (i, j), read in table.items():
        block = read()
        for a, b, v in ((i, j, block),) + (() if i == j else ((j, i, block.T),)):
            rows, cols = pl.ds(a * width, width), pl.ds(b * width, width)
            full[rows, cols] = v
            v = v * factor
            put(errors, highs, lows, 0, rows, cols, v)
            put(its, ihighs, ilows, 1, rows, cols, jnp.where(eye, 2.0, 0.0) - v if a == b else -v)
    scale[...] = jnp.broadcast_to(factor, scale.shape)
    steps(0, stop, *tables, None)
    error[...], iterate[...] = errors[stop % 2], its[stop % 2]


def reflect_kernel(width, xd, xo, ours, theirs, inv, out, cross, last, near, far, high, low):
    core = lax.axis_index("core")
    depth = ours.shape[1]
    for gathered, home in ((ours, core), (theirs, 1 - core)):
        gather_blocks(lambda i: gathered.at[i], depth, 0, xd, xo, near, far)
        for i in range(2):
            for j in range(2):
                places = (
                    (at(2 * i + home, width), at(2 * i + j, width), near[i, j * width : (j + 1) * width]),
                    (at(2 * home + i, width), at(2 * (1 - home) + j, width), far[(i * 2 + j) * width : (i * 2 + j + 1) * width]),
                )
                for rows, cols, value in places:
                    cross[rows, cols] = value
                    high[rows, cols], low[rows, cols] = halves(value)
    xy = lax.axis_index("x") * 2 + lax.axis_index("y")
    last[...] = ours[xy ^ 3, lax.rem(lax.axis_index("z") + 1, depth), xd + xo : xd + xo + 8]
    for chosen, product in ((0, dot_first), (1, dot)):

        @pl.when(core == chosen)
        def _():
            value = product(high[...], inv[0]) + product(high[...], inv[1]) + product(low[...], inv[0])
            out[...] = (-value).astype(BF16)


def update_cross_kernel(each, here, shifted, edge, ours, theirs, out, late, *refs):
    packed, (refl, ahead, flat) = refs[:4], refs[4:]
    by_kind(ours, theirs, refl)
    update_edge(edge, refl, ahead)
    update(here, shifted, refl, out)
    delay(out.at[1], ahead, late)
    channels = here.shape[2]
    value = dot_first(out[0, :, at(lax.axis_index("core"), channels // 2)], late[...])
    emit([value[:, j : j + LANES] for j in range(0, channels, LANES)], flat, packed, 0, each)


def there_kernel(width, both, across, both_core, across_core, edge, ours, theirs, out, late, refl, raw, shifted, ahead):
    y, core = lax.axis_index("y"), lax.axis_index("core")
    by_kind(ours, theirs, refl)
    rows = at(1 - y, raw.shape[1])
    raw[:, :, at(y * 2 + core, width)], raw[:, :, at(y * 2 + 1 - core, width)] = both[:, rows], both_core[:, rows]
    raw[:, :, at((1 - y) * 2 + core, width)] = across[...]
    raw[:, :, at((1 - y) * 2 + 1 - core, width)] = across_core[...]
    delay(raw.at[1], edge.at[1], shifted)
    update_edge(edge, refl, ahead)
    update(raw, shifted, refl, out)
    delay(out.at[1], ahead, late)


def predict_kernel(own, other, cross, theirs, last, work, scale, row):
    core = lax.axis_index("core")
    channels = own.shape[0]
    refl = theirs[...]
    for chosen, product in ((0, dot_last), (1, dot)):

        @pl.when(core == chosen)
        def _():
            parts = thirds(cross[...])
            work[...] = product(refl, parts[2]) + product(refl, parts[1]) + product(refl, parts[0])

    mixed = work[...]
    total = own[...] + (mixed + mixed.T)
    parts = thirds(other[...])
    parts = thirds(dot(refl, parts[2]) + dot(refl, parts[1]) + dot(refl, parts[0]))
    work[...] = total + (dot_last(parts[2], refl) + dot_last(parts[1], refl) + dot_last(parts[0], refl))

    @pl.when(core == 1)
    def _():
        row[...] = jnp.zeros_like(row)
        for i in range(2):
            for j in range(4):
                row[i, 0:1, j * LANES : (j + 1) * LANES] = last[i * 4 + j : i * 4 + j + 1]
        end = (row[1] + dot_last(row[0].astype(BF16), refl)).astype(BF16)
        work[...] -= dot_first(end, end)

    total = work[...]
    norm = jnp.sum((total * total).reshape(-1, 8, channels), axis=0)
    factor = lax.rsqrt(jnp.sum(norm, keepdims=True) + 1e-06)
    scale[...] = jnp.broadcast_to(factor, scale.shape)


def begin_kernel(stop, matrix, scale, error, iterate, *tables):
    errors, highs, lows, its, ihighs, ilows = tables
    channels = matrix.shape[0]
    factor = scale[0:1, 0:1]
    every = pl.ds(0, channels)
    step = 128
    for r in range(0, channels, step):
        rows = pl.ds(r, step)
        value = matrix[rows] * factor
        put(errors, highs, lows, 0, rows, every, value)
        shape = (step, channels)
        eye = lax.broadcasted_iota(jnp.int32, shape, 0) + r == lax.broadcasted_iota(jnp.int32, shape, 1)
        put(its, ihighs, ilows, 1, rows, every, jnp.where(eye, 2.0, 0.0) - value)
    steps(0, stop, *tables, None)
    error[...], iterate[...] = errors[stop % 2], its[stop % 2]


def finish_kernel(start, error, iterate, scale, out, *tables):
    errors, highs, lows, its, ihighs, ilows = tables
    channels = error.shape[0]
    every = pl.ds(0, channels)
    put(errors, highs, lows, start % 2, every, every, error[...])
    put(its, ihighs, ilows, start % 2, every, every, iterate[...])
    factor = scale[0:1, 0:1]

    def finish(rows, value):
        out[0, rows], out[1, rows] = halves(value * factor)

    steps(start, NSTEPS, *tables, finish)


def last_kernel(width, ours, theirs, inv, inv_core, here, shifted, there, there_shifted, forward, backward, flat, high, low):
    y, core = lax.axis_index("y"), lax.axis_index("core")
    channels = here.shape[2]
    half, depth, each = channels // 2, ours.shape[1], ours.shape[2]
    for gathered, home in ((ours, core), (theirs, 1 - core)):
        for i, k, zx, ys in sources(depth):
            flat[at(zx * 2 + ys, each)] = gathered[i, k]
        rows = at(home, half)
        for j in range(channels // LANES):
            cols = pl.ds(j * LANES, LANES)
            high[rows, cols], low[rows, cols] = halves(flat[j * half : (j + 1) * half])
    mine = at(y * 2 + core, width)

    def reflect(lefts, rights, product):
        value = product(lefts[0], rights[0]) + product(lefts[0], rights[1]) + product(lefts[1], rights[0])
        return (-value).astype(BF16)

    def final(of_fwd, of_bwd):
        left = reflect((high[mine], low[mine]), (of_bwd[0], of_bwd[1]), dot)
        right = reflect((high[:, mine], low[:, mine]), (of_fwd[0], of_fwd[1]), dot_first)
        for time, both, late in ((y, here, shifted), (1 - y, there, there_shifted)):
            rows = at(time, here.shape[1])
            forward[rows] = (both[0, :, mine].astype(F32) + dot_last(late[...], left)).astype(BF16)
            backward[rows] = (late[:, mine].astype(F32) + dot_last(both[0], right)).astype(BF16)

    @pl.when(core == 0)
    def _():
        final(inv, inv_core)

    @pl.when(core == 1)
    def _():
        final(inv_core, inv)


def ahead(piece, by):
    size = lax.axis_size("z")
    return lax.ppermute(piece, "z", [(i, (i + by) % size) for i in range(size)])


def exchange(pieces):
    both = [(i, 3 - i) for i in range(4)]
    return [pieces[0], swap(pieces[1], "y"), swap(pieces[2], "x"), lax.ppermute(pieces[3], ("x", "y"), both)]


def scatter_z(pieces):
    total = sum(pieces[1:], pieces[0])
    return sum((ahead(total[k], k) for k in range(1, total.shape[0])), total[0])


def z_gather(piece):
    return jnp.stack([piece] + [ahead(piece, by) for by in range(1, lax.axis_size("z"))])


def xy_gather(piece):
    return exchange([piece] * 4)


def share(rows, parts):
    return -(-rows // (8 * parts)) * 8


def local(fwd_in, bwd_in):
    y = lax.axis_index("y")
    zx = ("z", "x")
    samples, width = fwd_in.shape
    half, pair, channels = samples // 2, 2 * width, 4 * width
    depth, near_parts, parts = lax.axis_size("z"), lax.axis_size(zx), lax.axis_size(PARTS)
    pd, xd = share(3 * width, near_parts), share(2 * width, near_parts)
    po, xo = share(4 * width, parts), share(4 * width, parts)
    each = share(8 * width, parts)
    shape = jax.ShapeDtypeStruct
    square = lambda *lead: pltpu.VMEM(lead + (channels, channels), F32)
    square16 = lambda *lead: pltpu.VMEM(lead + (channels, channels), BF16)
    tables = [square(2), square16(2), square16(2)] * 2
    flat = lambda *rows: pltpu.VMEM((max(rows), LANES), F32)
    kernel = functools.partial

    halo = from_behind(jnp.stack([fwd_in[samples - 16 :], bwd_in[samples - 16 :]]), zx)
    cut = lambda which: jnp.stack([lax.dynamic_slice_in_dim(a, which * half, half, 0) for a in (fwd_in, bwd_in)])
    other = cut(1 - y)
    across = swap(other, "y")
    both = jnp.stack([after(fwd_in, other), bwd_in])
    both_core = swap(both, "core")
    halo_core = swap(halo, "core")
    halo_y = swap(jnp.where(y == 0, both[:, half - 16 : half], halo), "y")
    near = call(
        kernel(near_kernel, width, pd, xd),
        [shape((depth, pd + xd, LANES), F32)] * 2,
        [pltpu.VMEM((samples, pair), BF16)] * 3 + [pltpu.VMEM((16, pair), BF16), flat(near_parts * pd, near_parts * xd)],
        3 * samples * pair * pair,
        both, both_core, halo, halo_core,
    )
    near_x = swap(near[1], "x")
    halo_y_core = swap(after(halo_y, near[1]), "core")
    across = after(across, near[1], halo_y_core)
    across2 = swap(after(cut(y), across), "y")
    across_core = swap(across, "core")
    here, edge, shifted, *far, tails = call(
        kernel(far_kernel, width, po, xo),
        [
            shape((2, half, channels), BF16),
            shape((2, 16, channels), BF16),
            shape((half, channels), BF16),
            *[shape((depth, po + xo, LANES), F32)] * 4,
            shape((8, LANES), F32),
        ],
        [pltpu.VMEM((half, channels), BF16), flat(parts * po, parts * xo)],
        4 * half * pair * pair,
        both, across, both_core, across_core, halo, halo_core, halo_y, halo_y_core,
    )
    near_sum = scatter_z([after(near[0], far[0]), near_x])
    swapped = exchange(far)
    far_sum = scatter_z([after(swapped[0], across2)] + swapped[1:])
    chunk = jnp.concatenate([near_sum[:pd], far_sum[:po], near_sum[pd:], far_sum[po:], tails])
    column = z_gather(chunk)
    pieces = xy_gather(column[:, : pd + po])
    stop = NSTEPS // 2
    state = [shape((channels, channels), F32)] * 2 + [shape((8, LANES), F32)]
    full, error, iterate, scale = call(
        kernel(inverse_kernel, width, pd, po, stop),
        [shape((channels, channels), F32)] + state,
        [pltpu.VMEM((2, near_parts * pd, LANES), F32), flat(parts * po)] + tables,
        30 * channels**3,
        *pieces,
    )
    ours = jnp.stack(xy_gather(after(column[:, pd + po :], *pieces)))
    theirs = swap(after(ours, error), "core")
    finish = lambda *args: call(
        kernel(finish_kernel, stop), [shape((2, channels, channels), BF16)], tables, 30 * channels**3, *args
    )[0]
    inv = finish(error, iterate, scale)
    refl, cross, last = call(
        kernel(reflect_kernel, width, xd, xo),
        [shape((channels, channels), BF16), shape((channels, channels), F32), shape((8, LANES), F32)],
        [pltpu.VMEM((2, near_parts * xd, LANES), F32), flat(parts * xo), square16(), square16()],
        6 * channels**3,
        ours, theirs, inv,
    )
    refl_core = swap(refl, "core")
    here2, shifted2, *packed = call(
        kernel(update_cross_kernel, each),
        [shape((2, half, channels), BF16), shape((half, channels), BF16)] + [shape((depth, each, LANES), F32)] * 4,
        [square16(2), pltpu.VMEM((16, channels), BF16), flat(parts * each)],
        5 * half * channels * channels,
        here, shifted, edge, refl, refl_core,
    )
    across2_core = swap(after(across2, column), "core")
    full_core = swap(after(full, refl_core), "core")
    matrix2, scale2 = call(
        predict_kernel,
        [shape((channels, channels), F32), shape((8, LANES), F32)],
        [pltpu.VMEM((2, 16, channels), F32)],
        18 * channels**3,
        after(full, packed[0]), full_core, cross, refl_core, last,
    )
    error2, iterate2 = call(
        kernel(begin_kernel, stop), state[:2], tables, 30 * channels**3, matrix2, scale2
    )
    swapped = exchange(packed)
    cross_sum = after(scatter_z([after(swapped[0], matrix2)] + swapped[1:]), error2)
    inv2 = finish(after(error2, cross_sum), iterate2, scale2)
    inv2_core = swap(inv2, "core")
    column2 = z_gather(cross_sum)
    tail = here[:, half - 16 :]
    edge2 = jnp.where(y == 0, tail, from_behind(tail, zx))
    there2, there_shifted2 = call(
        kernel(there_kernel, width),
        [shape((2, half, channels), BF16), shape((half, channels), BF16)],
        [square16(2), pltpu.VMEM((2, half, channels), BF16), pltpu.VMEM((half, channels), BF16), pltpu.VMEM((16, channels), BF16)],
        4 * half * channels * channels,
        both, across2, both_core, across2_core, edge2, refl, after(refl_core, column2),
    )
    ours2 = jnp.stack(xy_gather(after(column2, inv2)))
    theirs2 = swap(after(ours2, there2), "core")
    return call(
        kernel(last_kernel, width),
        [shape((samples, width), BF16)] * 2,
        [flat(parts * each), square16(), square16()],
        4 * samples * channels * width,
        ours2, theirs2, inv2, inv2_core, here2, shifted2, there2, there_shifted2,
    )


def solution(mesh):
    tm, chan = mesh.shape["tm"], mesh.shape["chan"]
    split = Mesh(mesh.devices.reshape(tm // 2, 2, chan // 2, 2), ("z", "x", "y", "core"))
    spec = P(("z", "x"), ("y", "core"))
    return jax.shard_map(local, mesh=split, in_specs=(spec, spec), out_specs=(spec, spec), check_vma=False)
```

time: 460 us -> 139 us (0.30)
  waiting for transfers between devices: 301 us -> 45.6 us
  matrix products: 109 us -> 0 us
  starting transfers between devices: 19 us -> 54.9 us
  Pallas kernels: 0 us -> 33 us
  between operations: 17.6 us -> 1.03 us
    psum x2 -> x0, waiting for transfers between devices: 279 us -> none  [local(): lax.psum((cov_fwd, cov_bwd, cov_cross), ('tm', 'chan'))]
    dot_general x62 -> x0, matrix products: 109 us -> none  [the longest x24 45 us: full_inverse(): iterate = 2.0 * iterate - jnp.dot(product, iterate, precision=HIGH)]
    ppermute x2 -> x46, starting transfers between devices: 3.83 us -> 54.9 us  [the longest x15 21.3 us: ahead(): return lax.ppermute(piece, 'z', [(i, (i + by) % size) for i in range(size)])]
    ppermute x2 -> x46, waiting for transfers between devices: 0.01 us -> 45.6 us  [the longest x24 27.3 us: swap(): return lax.ppermute(value, axis, [(0, 1), (1, 0)])]
    pallas_call x0 -> x11, Pallas kernels: none -> 33 us  [call(): pl.pallas_call(body, out_shape=shapes, in_specs=[VMEM] * len(args), out_s...]
    all_to_all x4 -> x0, waiting for transfers between devices: 22.1 us -> none  [the longest x1 7.84 us: local(): lax.all_to_all(bwd_in, 'chan', split_axis=0, concat_axis=1, tiled=True)]
    all_to_all x4 -> x0, starting transfers between devices: 14.9 us -> none  [the longest x1 4.38 us: local(): lax.all_to_all(bwd_in, 'chan', split_axis=0, concat_axis=1, tiled=True)]
    reduce_sum x3 -> x0, other arithmetic: 5.56 us -> none  [full_inverse(): factor = lax.rsqrt(jnp.sum(matrix * matrix) + 1e-06)]
  transfers between devices with their start and end apart: 8 -> 46, of which waited for: 5 -> 23; matrix products, arithmetic and copies ran while one was open for 7% -> 1% of each run, Pallas kernels for 0% -> 21%
where the time goes in v2:
time: 139 us
  starting transfers between devices  54.9 us (39%)
  waiting for transfers between devices  45.6 us (33%)
  Pallas kernels  33 us (24%)
  local copies, waits for them, and re-layouts  2.82 us (2%)
  other arithmetic  1.93 us (1%)
    pallas_call x11, Pallas kernels, call(): pl.pallas_call(body, out_shape=shapes, in_specs=[VMEM] * len(args), out_s...  33 us
    ppermute x24, waiting for transfers between devices, swap(): return lax.ppermute(value, axis, [(0, 1), (1, 0)])  27.3 us
    ppermute x15, starting transfers between devices, ahead(): return lax.ppermute(piece, 'z', [(i, (i + by) % size) for i in range(size)])  21.3 us
    ppermute x24, starting transfers between devices, swap(): return lax.ppermute(value, axis, [(0, 1), (1, 0)])  17.1 us
    ppermute x15, waiting for transfers between devices, ahead(): return lax.ppermute(piece, 'z', [(i, (i + by) % size) for i in range(size)])  9.51 us
    ppermute x5, starting transfers between devices, exchange(): lax.ppermute(pieces[3], ('x', 'y'), both)  9.19 us
    ppermute x5, waiting for transfers between devices, exchange(): lax.ppermute(pieces[3], ('x', 'y'), both)  7.46 us
    ppermute x2, starting transfers between devices, from_behind(): return lax.ppermute(value, axes, [(i, i + 1) for i in range(devices - 1)])  7.29 us
  transfers between devices with their start and end apart: 46, of which 23 were waited for; matrix products, arithmetic and copies ran while one was open for 1% of the time, Pallas kernels for 21%

profile of v2, /device:TPU:0, one launch (start us, length us, event | category | flops | bytes accessed | tf_op | source)
XLA Modules:
  0.0 139.2 jit_solution(8153551377853160620)
XLA Ops:
  0.7 2.0 %dynamic-slice_bitcast_fusion = (bf16[1,1024,128]{2,1,0:T(8,128)(2,1)S(1)}, bf16[1,1024,128]{2,1,0:T(8,128)(2,1)S(1)}, bf16[1,1024,128]{2,1,0:T(8,128)(2,1)S(1)}, bf16[1,1024,128]{2,1,0:T(8,128)(2,1)}) fusion(bf16[2048,128]{1,0:T(8,128)(2,1)} %param.3, s32[]{:T(128)S(6)} %select_n.27, s32[]{:T(128)S(6)} %select_n.24, bf16[2048,128]{1,0:T(8,128)(2,1)} %param.2), kind=kLoop, calls=%fused_computation.8 | loop fusion | bytes 2097160 | tf_op jit(solution)/shard_map/stack | solution.py:441
  4.2 2.6 %collective-permute-start = (bf16[2,1024,128]{2,1,0:T(8,128)(2,1)}, bf16[2,1024,128]{2,1,0:T(8,128)(2,1)S(1)}, u32[]{:S(2)}, u32[]{:S(2)}) collective-permute-start(bf16[2,1024,128]{2,1,0:T(8,128)(2,1)} %pad_maximum_fusion.2), channel_id=1, source_target_pairs={{0,2},{2,0},{1,3},{3,1},{4,6},{6,4},{5,7},{7,5},{8,10},{10,8},{9,1... | collective-permute-start | bytes 1572872 | tf_op jit(solution)/shard_map/ppermute | solution.py:20
  7.5 3.4 %collective-permute-start.2 = (bf16[2,16,128]{2,1,0:T(8,128)(2,1)S(1)}, bf16[2,16,128]{2,1,0:T(8,128)(2,1)S(1)}, u32[]{:S(2)}, u32[]{:S(2)}) collective-permute-start(bf16[2,16,128]{2,1,0:T(8,128)(2,1)S(1)} %pad_maximum_fusion.7), channel_id=1, source_target_pairs={{0,4},{4,8},{8,12},{12,16},{16,20},{20,24},{24,28},{1,5},{5,9},{9,... | collective-permute-start | bytes 24584 | tf_op jit(solution)/shard_map/ppermute | solution.py:25
  14.4 5.3 %collective-permute-done.4.halo_y = bf16[2,16,128]{2,1,0:T(8,128)(2,1)S(1)} collective-permute-done((bf16[2,16,128]{2,1,0:T(8,128)(2,1)S(1)}, bf16[2,16,128]{2,1,0:T(8,128)(2,1)S(1)}, u32[]{:S(2)}, u32[]{:S(2)}) %collective-permute-start.4) | collective-permute-done | bytes 8224 | tf_op jit(solution)/shard_map/ppermute | solution.py:20
  21.1 1.8 %collective-permute-start.11 = (bf16[2,1024,128]{2,1,0:T(8,128)(2,1)S(1)}, bf16[2,1024,128]{2,1,0:T(8,128)(2,1)S(1)}, u32[]{:S(2)}, u32[]{:S(2)}) collective-permute-start(bf16[2,1024,128]{2,1,0:T(8,128)(2,1)S(1)} %pad_maximum_fusion.3), channel_id=1, source_target_pairs={{0,2},{2,0},{1,3},{3,1},{4,6},{6,4},{5,7},{7,5},{8,10},{10,8},{9,1... | collective-permute-start | bytes 1572872 | tf_op jit(solution)/shard_map/ppermute | solution.py:20
  25.7 3.4 %collective-permute-done.7 = f32[4,80,128]{2,1,0:T(8,128)S(1)} collective-permute-done((f32[4,80,128]{2,1,0:T(8,128)S(1)}, f32[4,80,128]{2,1,0:T(8,128)S(1)}, u32[]{:S(2)}, u32[]{:S(2)}) %collective-permute-start.7) | collective-permute-done | bytes 163872 | tf_op jit(solution)/shard_map/ppermute | solution.py:20
  30.7 2.2 %collective-permute-start.10 = (f32[80,128]{1,0:T(8,128)S(1)}, f32[80,128]{1,0:T(8,128)S(1)}, u32[]{:S(2)}, u32[]{:S(2)}) collective-permute-start(f32[80,128]{1,0:T(8,128)S(1)} %get-tuple-element.99), channel_id=1, source_target_pairs={{0,24},{8,0},{16,8},{24,16},{1,25},{9,1},{17,9},{25,17},{2,26},{10... | collective-permute-start | bytes 122888 | tf_op jit(solution)/shard_map/ppermute | solution.py:399
  40.3 2.8 %collective-permute-done.13 = f32[4,64,128]{2,1,0:T(8,128)S(1)} collective-permute-done((f32[4,64,128]{2,1,0:T(8,128)S(1)}, f32[4,64,128]{2,1,0:T(8,128)S(1)}, u32[]{:S(2)}, u32[]{:S(2)}) %collective-permute-start.13) | collective-permute-done | bytes 131104 | tf_op jit(solution)/shard_map/ppermute | solution.py:20
  44.6 1.8 %collective-permute-start.15 = (f32[64,128]{1,0:T(8,128)S(1)}, f32[64,128]{1,0:T(8,128)S(1)}, u32[]{:S(2)}, u32[]{:S(2)}) collective-permute-start(f32[64,128]{1,0:T(8,128)S(1)} %get-tuple-element.104), channel_id=1, source_target_pairs={{0,8},{8,16},{16,24},{24,0},{1,9},{9,17},{17,25},{25,1},{2,10},{10... | collective-permute-start | bytes 98312 | tf_op jit(solution)/shard_map/ppermute | solution.py:399
  46.5 2.1 %collective-permute-start.17 = (f32[64,128]{1,0:T(8,128)S(1)}, f32[64,128]{1,0:T(8,128)S(1)}, u32[]{:S(2)}, u32[]{:S(2)}) collective-permute-start(f32[64,128]{1,0:T(8,128)S(1)} %get-tuple-element.105), channel_id=1, source_target_pairs={{0,24},{8,0},{16,8},{24,16},{1,25},{9,1},{17,9},{25,17},{2,26},{10... | collective-permute-start | bytes 98312 | tf_op jit(solution)/shard_map/ppermute | solution.py:399
  50.7 2.6 %collective-permute-done.16 = f32[64,128]{1,0:T(8,128)S(1)} collective-permute-done((f32[64,128]{1,0:T(8,128)S(1)}, f32[64,128]{1,0:T(8,128)S(1)}, u32[]{:S(2)}, u32[]{:S(2)}) %collective-permute-start.16) | collective-permute-done | bytes 32800 | tf_op jit(solution)/shard_map/ppermute | solution.py:399
  53.4 2.2 %collective-permute-start.20 = (f32[152,128]{1,0:T(8,128)S(1)}, f32[152,128]{1,0:T(8,128)S(1)}, u32[]{:S(2)}, u32[]{:S(2)}) collective-permute-start(f32[152,128]{1,0:T(8,128)S(1)} %constant_dynamic-update-slice_fusion), channel_id=1, source_target_pairs={{0,24},{8,0},{16,8},{24,16},{1,25},{9,1},{17,9},{25,17},{2,26},{10... | collective-permute-start | bytes 233480 | tf_op jit(solution)/shard_map/ppermute | solution.py:399
  56.5 3.0 %collective-permute-done.20 = f32[152,128]{1,0:T(8,128)S(1)} collective-permute-done((f32[152,128]{1,0:T(8,128)S(1)}, f32[152,128]{1,0:T(8,128)S(1)}, u32[]{:S(2)}, u32[]{:S(2)}) %collective-permute-start.20) | collective-permute-done | bytes 77856 | tf_op jit(solution)/shard_map/ppermute | solution.py:399
  62.0 2.6 %collective-permute-start.23 = (f32[4,80,128]{2,1,0:T(8,128)S(1)}, f32[4,80,128]{2,1,0:T(8,128)S(1)}, u32[]{:S(2)}, u32[]{:S(2)}) collective-permute-start(f32[4,80,128]{2,1,0:T(8,128)S(1)} %slice.103.refs_0_), channel_id=1, source_target_pairs={{0,6},{2,4},{4,2},{6,0},{1,7},{3,5},{5,3},{7,1},{8,14},{10,12},{12... | collective-permute-start | bytes 491528 | tf_op jit(solution)/shard_map/ppermute | solution.py:404
  65.5 2.7 %collective-permute-done.23.refs_3_ = f32[4,80,128]{2,1,0:T(8,128)S(1)} collective-permute-done((f32[4,80,128]{2,1,0:T(8,128)S(1)}, f32[4,80,128]{2,1,0:T(8,128)S(1)}, u32[]{:S(2)}, u32[]{:S(2)}) %collective-permute-start.23) | collective-permute-done | bytes 163872 | tf_op jit(solution)/shard_map/ppermute | solution.py:404
  68.2 3.2 %collective-permute-done.22.refs_2_ = f32[4,80,128]{2,1,0:T(8,128)S(1)} collective-permute-done((f32[4,80,128]{2,1,0:T(8,128)S(1)}, f32[4,80,128]{2,1,0:T(8,128)S(1)}, u32[]{:S(2)}, u32[]{:S(2)}) %collective-permute-start.22) | collective-permute-done | bytes 163872 | tf_op jit(solution)/shard_map/ppermute | solution.py:20
  72.4 3.3 %collective-permute-start.26 = (f32[4,72,128]{2,1,0:T(8,128)S(1)}, f32[4,72,128]{2,1,0:T(8,128)S(1)}, u32[]{:S(2)}, u32[]{:S(2)}) collective-permute-start(f32[4,72,128]{2,1,0:T(8,128)S(1)} %slice.102), channel_id=1, source_target_pairs={{0,6},{2,4},{4,2},{6,0},{1,7},{3,5},{5,3},{7,1},{8,14},{10,12},{12... | collective-permute-start | bytes 442376 | tf_op jit(solution)/shard_map/ppermute | solution.py:404
  76.2 5.3 %shard_map.43 = (f32[512,512]{1,0:T(8,128)S(1)}, f32[512,512]{1,0:T(8,128)S(1)}, f32[512,512]{1,0:T(8,128)S(1)}, f32[8,128]{1,0:T(8,128)S(1)}) custom-call(f32[4,80,128]{2,1,0:T(8,128)S(1)} %slice.103.refs_0_, f32[4,80,128]{2,1,0:T(8,128)S(1)} %collective-permute-done.21.refs_1_, f32[4,80,128]{2,1,0:T(8,128)S(1)} %collective-permute-done.22.refs_2_, ...), custom_call_target="tpu_custom_call" | custom-call | flops 4026531840 | bytes 3805184 | tf_op jit(solution)/shard_map/pallas_call | solution.py:34
  81.7 4.5 %shard_map.44.inv = bf16[2,512,512]{2,1,0:T(8,128)(2,1)S(1)} custom-call(f32[512,512]{1,0:T(8,128)S(1)} %get-tuple-element.65.error, f32[512,512]{1,0:T(8,128)S(1)} %get-tuple-element.67.iterate, f32[8,128]{1,0:T(8,128)S(1)} %get-tuple-element.68.scale), custom_call_target="tpu_custom_call" | custom-call | flops 4026531840 | bytes 3149824 | tf_op jit(solution)/shard_map/pallas_call | solution.py:34
  90.1 3.9 %collective-permute-start.43 = (bf16[2,16,512]{2,1,0:T(8,128)(2,1)S(1)}, bf16[2,16,512]{2,1,0:T(8,128)(2,1)S(1)}, u32[]{:S(2)}, u32[]{:S(2)}) collective-permute-start(bf16[2,16,512]{2,1,0:T(8,128)(2,1)S(1)} %slice.87), channel_id=1, source_target_pairs={{0,4},{4,8},{8,12},{12,16},{16,20},{20,24},{24,28},{1,5},{5,9},{9,... | collective-permute-start | bytes 98312 | tf_op jit(solution)/shard_map/ppermute | solution.py:25
  94.1 2.0 %shard_map.46 = (bf16[2,1024,512]{2,1,0:T(8,128)(2,1)S(1)}, bf16[1024,512]{1,0:T(8,128)(2,1)S(1)}, f32[4,64,128]{2,1,0:T(8,128)S(1)}, f32[4,64,128]{2,1,0:T(8,12...) custom-call(bf16[2,1024,512]{2,1,0:T(8,128)(2,1)S(1)} %get-tuple-element.52.here, ...), custom_call_target="tpu_custom_call" | custom-call | flops 1342177280 | bytes 7897088 | tf_op jit(solution)/shard_map/pallas_call | solution.py:34
  99.7 3.1 %shard_map.47 = (f32[512,512]{1,0:T(8,128)S(1)}, f32[8,128]{1,0:T(8,128)S(1)}) custom-call(f32[512,512]{1,0:T(8,128)S(1)} %get-tuple-element.73.own, f32[512,512]{1,0:T(8,128)S(1)} %collective-permute-done.29.other, f32[512,512]{1,0:T(8,128)S(1)} %get-tuple-element.74.cross, bf16[512,512]{1,0:T(8,128)(2,1)S(1)} %collective-permute-done.28.theirs, ...), custom_call_target="tpu_custom_call" | custom-call | flops 2415919104 | bytes 4726784 | tf_op jit(solution)/shard_map/pallas_call | solution.py:34
  104.2 1.9 %collective-permute-done.32 = f32[4,64,128]{2,1,0:T(8,128)S(1)} collective-permute-done((f32[4,64,128]{2,1,0:T(8,128)S(1)}, f32[4,64,128]{2,1,0:T(8,128)S(1)}, u32[]{:S(2)}, u32[]{:S(2)}) %collective-permute-start.32) | collective-permute-done | bytes 131104 | tf_op jit(solution)/shard_map/ppermute | solution.py:404
  106.2 3.8 %collective-permute-start.35 = (f32[64,128]{1,0:T(8,128)S(1)}, f32[64,128]{1,0:T(8,128)S(1)}, u32[]{:S(2)}, u32[]{:S(2)}) collective-permute-start(f32[64,128]{1,0:T(8,128)S(1)} %get-tuple-element.102), channel_id=1, source_target_pairs={{0,24},{8,0},{16,8},{24,16},{1,25},{9,1},{17,9},{25,17},{2,26},{10... | collective-permute-start | bytes 98312 | tf_op jit(solution)/shard_map/ppermute | solution.py:399
  110.0 4.6 %shard_map.48 = (f32[512,512]{1,0:T(8,128)S(1)}, f32[512,512]{1,0:T(8,128)S(1)}) custom-call(f32[512,512]{1,0:T(8,128)S(1)} %get-tuple-element.76.matrix, f32[8,128]{1,0:T(8,128)S(1)} %get-tuple-element.81.scale), custom_call_target="tpu_custom_call" | custom-call | flops 4026531840 | bytes 3149824 | tf_op jit(solution)/shard_map/pallas_call | solution.py:34
  115.8 1.9 %collective-permute-start.37 = (f32[64,128]{1,0:T(8,128)S(1)}, f32[64,128]{1,0:T(8,128)S(1)}, u32[]{:S(2)}, u32[]{:S(2)}) collective-permute-start(f32[64,128]{1,0:T(8,128)S(1)} %fusion.5), channel_id=1, source_target_pairs={{0,16},{8,24},{16,0},{24,8},{1,17},{9,25},{17,1},{25,9},{2,18},{10... | collective-permute-start | bytes 98312 | tf_op jit(solution)/shard_map/ppermute | solution.py:399
  117.7 1.9 %collective-permute-start.36 = (f32[64,128]{1,0:T(8,128)S(1)}, f32[64,128]{1,0:T(8,128)S(1)}, u32[]{:S(2)}, u32[]{:S(2)}) collective-permute-start(f32[64,128]{1,0:T(8,128)S(1)} %fusion.5), channel_id=1, source_target_pairs={{0,8},{8,16},{16,24},{24,0},{1,9},{9,17},{17,25},{25,1},{2,10},{10... | collective-permute-start | bytes 98312 | tf_op jit(solution)/shard_map/ppermute | solution.py:399
  119.7 4.6 %shard_map.49.inv = bf16[2,512,512]{2,1,0:T(8,128)(2,1)S(1)} custom-call(f32[512,512]{1,0:T(8,128)S(1)} %get-tuple-element.84.error, f32[512,512]{1,0:T(8,128)S(1)} %get-tuple-element.85.iterate, f32[8,128]{1,0:T(8,128)S(1)} %get-tuple-element.81.scale), custom_call_target="tpu_custom_call" | custom-call | flops 4026531840 | bytes 3149824 | tf_op jit(solution)/shard_map/pallas_call | solution.py:34
  127.9 2.3 %shard_map.50 = (bf16[2,1024,512]{2,1,0:T(8,128)(2,1)S(1)}, bf16[1024,512]{1,0:T(8,128)(2,1)S(1)}) custom-call(bf16[2,2048,128]{2,1,0:T(8,128)(2,1)S(1)} %pad_maximum_fusion.both, bf16[2,1024,128]{2,1,0:T(8,128)(2,1)S(1)} %collective-permute-done.11.across, bf16[2,2048,128]{2,1,0:T(8,128)(2,1)S(1)} %collective-permute-done.1.both_core, ...), custom_call_target="tpu_custom_call" | custom-call | flops 1073741824 | bytes 7372800 | tf_op jit(solution)/shard_map/pallas_call | solution.py:34
  131.6 2.6 %collective-permute-done.40 = f32[4,64,128]{2,1,0:T(8,128)S(1)} collective-permute-done((f32[4,64,128]{2,1,0:T(8,128)S(1)}, f32[4,64,128]{2,1,0:T(8,128)S(1)}, u32[]{:S(2)}, u32[]{:S(2)}) %collective-permute-start.40) | collective-permute-done | bytes 131104 | tf_op jit(solution)/shard_map/ppermute | solution.py:20
  134.4 1.9 %collective-permute-done.44.theirs = f32[4,4,64,128]{3,2,1,0:T(8,128)S(1)} collective-permute-done((f32[4,4,64,128]{3,2,1,0:T(8,128)S(1)}, f32[4,4,64,128]{3,2,1,0:T(8,128)S(1)}, u32[]{:S(2)}, u32[]{:S(2)}) %collective-permute-start.44) | collective-permute-done | bytes 524320 | tf_op jit(solution)/shard_map/ppermute | solution.py:20
  136.3 3.0 %shard_map.51 = (bf16[2048,128]{1,0:T(8,128)(2,1)}, bf16[2048,128]{1,0:T(8,128)(2,1)}) custom-call(f32[4,4,64,128]{3,2,1,0:T(8,128)S(1)} %pad_maximum_fusion.4.ours, f32[4,4,64,128]{3,2,1,0:T(8,128)S(1)} %collective-permute-done.44.theirs, bf16[2,512,512]{2,1,0:T(8,128)(2,1)S(1)} %shard_map.49.inv, ...), custom_call_target="tpu_custom_call" | custom-call | flops 536870912 | bytes 10485760 | tf_op jit(solution)/shard_map/pallas_call | solution.py:34
  (107 shorter events, 43.7 us)
Async XLA Ops:
  3.7 9.8 %collective-permute-start.1 = (bf16[2,2048,128]{2,1,0:T(8,128)(2,1)S(1)}, bf16[2,2048,128]{2,1,0:T(8,128)(2,1)S(1)}, u32[]{:S(2)}, u32[]{:S(2)}) collective-permute-start(bf16[2,2048,128]{2,1,0:T(8,128)(2,1)S(1)} %pad_maximum_fusion.both), channel_id=1, source_target_pairs={{0,1},{1,0},{2,3},{3,2},{4,5},{5,4},{6,7},{7,6},{8,9},{9,8},{10,11... | collective-permute-start | bytes 3145736 | tf_op jit(solution)/shard_map/ppermute | solution.py:20
  4.2 15.5 %collective-permute-start = (bf16[2,1024,128]{2,1,0:T(8,128)(2,1)}, bf16[2,1024,128]{2,1,0:T(8,128)(2,1)S(1)}, u32[]{:S(2)}, u32[]{:S(2)}) collective-permute-start(bf16[2,1024,128]{2,1,0:T(8,128)(2,1)} %pad_maximum_fusion.2), channel_id=1, source_target_pairs={{0,2},{2,0},{1,3},{3,1},{4,6},{6,4},{5,7},{7,5},{8,10},{10,8},{9,1... | collective-permute-start | bytes 1572872 | tf_op jit(solution)/shard_map/ppermute | solution.py:20
  12.9 6.8 %collective-permute-start.4 = (bf16[2,16,128]{2,1,0:T(8,128)(2,1)S(1)}, bf16[2,16,128]{2,1,0:T(8,128)(2,1)S(1)}, u32[]{:S(2)}, u32[]{:S(2)}) collective-permute-start(bf16[2,16,128]{2,1,0:T(8,128)(2,1)S(1)} %fusion.10), channel_id=1, source_target_pairs={{0,2},{2,0},{1,3},{3,1},{4,6},{6,4},{5,7},{7,5},{8,10},{10,8},{9,1... | collective-permute-start | bytes 24584 | tf_op jit(solution)/shard_map/ppermute | solution.py:20
  21.1 14.3 %collective-permute-start.11 = (bf16[2,1024,128]{2,1,0:T(8,128)(2,1)S(1)}, bf16[2,1024,128]{2,1,0:T(8,128)(2,1)S(1)}, u32[]{:S(2)}, u32[]{:S(2)}) collective-permute-start(bf16[2,1024,128]{2,1,0:T(8,128)(2,1)S(1)} %pad_maximum_fusion.3), channel_id=1, source_target_pairs={{0,2},{2,0},{1,3},{3,1},{4,6},{6,4},{5,7},{7,5},{8,10},{10,8},{9,1... | collective-permute-start | bytes 1572872 | tf_op jit(solution)/shard_map/ppermute | solution.py:20
  22.9 6.2 %collective-permute-start.7 = (f32[4,80,128]{2,1,0:T(8,128)S(1)}, f32[4,80,128]{2,1,0:T(8,128)S(1)}, u32[]{:S(2)}, u32[]{:S(2)}) collective-permute-start(f32[4,80,128]{2,1,0:T(8,128)S(1)} %get-tuple-element.49), channel_id=1, source_target_pairs={{0,4},{4,0},{1,5},{5,1},{2,6},{6,2},{3,7},{7,3},{8,12},{12,8},{9,1... | collective-permute-start | bytes 491528 | tf_op jit(solution)/shard_map/ppermute | solution.py:20
  29.1 9.5 %collective-permute-start.8 = (f32[80,128]{1,0:T(8,128)S(1)}, f32[80,128]{1,0:T(8,128)S(1)}, u32[]{:S(2)}, u32[]{:S(2)}) collective-permute-start(f32[80,128]{1,0:T(8,128)S(1)} %get-tuple-element.98), channel_id=1, source_target_pairs={{0,8},{8,16},{16,24},{24,0},{1,9},{9,17},{17,25},{25,1},{2,10},{10... | collective-permute-start | bytes 122888 | tf_op jit(solution)/shard_map/ppermute | solution.py:399
  30.7 8.1 %collective-permute-start.10 = (f32[80,128]{1,0:T(8,128)S(1)}, f32[80,128]{1,0:T(8,128)S(1)}, u32[]{:S(2)}, u32[]{:S(2)}) collective-permute-start(f32[80,128]{1,0:T(8,128)S(1)} %get-tuple-element.99), channel_id=1, source_target_pairs={{0,24},{8,0},{16,8},{24,16},{1,25},{9,1},{17,9},{25,17},{2,26},{10... | collective-permute-start | bytes 122888 | tf_op jit(solution)/shard_map/ppermute | solution.py:399
  37.1 6.1 %collective-permute-start.13 = (f32[4,64,128]{2,1,0:T(8,128)S(1)}, f32[4,64,128]{2,1,0:T(8,128)S(1)}, u32[]{:S(2)}, u32[]{:S(2)}) collective-permute-start(f32[4,64,128]{2,1,0:T(8,128)S(1)} %get-tuple-element.61), channel_id=1, source_target_pairs={{0,4},{4,0},{1,5},{5,1},{2,6},{6,2},{3,7},{7,3},{8,12},{12,8},{9,1... | collective-permute-start | bytes 393224 | tf_op jit(solution)/shard_map/ppermute | solution.py:20
  38.6 6.0 %collective-permute-start.14 = (f32[4,64,128]{2,1,0:T(8,128)S(1)}, f32[4,64,128]{2,1,0:T(8,128)S(1)}, u32[]{:S(2)}, u32[]{:S(2)}) collective-permute-start(f32[4,64,128]{2,1,0:T(8,128)S(1)} %get-tuple-element.62), channel_id=1, source_target_pairs={{0,6},{2,4},{4,2},{6,0},{1,7},{3,5},{5,3},{7,1},{8,14},{10,12},{12... | collective-permute-start | bytes 393224 | tf_op jit(solution)/shard_map/ppermute | solution.py:404
  44.6 6.1 %collective-permute-start.15 = (f32[64,128]{1,0:T(8,128)S(1)}, f32[64,128]{1,0:T(8,128)S(1)}, u32[]{:S(2)}, u32[]{:S(2)}) collective-permute-start(f32[64,128]{1,0:T(8,128)S(1)} %get-tuple-element.104), channel_id=1, source_target_pairs={{0,8},{8,16},{16,24},{24,0},{1,9},{9,17},{17,25},{25,1},{2,10},{10... | collective-permute-start | bytes 98312 | tf_op jit(solution)/shard_map/ppermute | solution.py:399
  53.4 6.0 %collective-permute-start.20 = (f32[152,128]{1,0:T(8,128)S(1)}, f32[152,128]{1,0:T(8,128)S(1)}, u32[]{:S(2)}, u32[]{:S(2)}) collective-permute-start(f32[152,128]{1,0:T(8,128)S(1)} %constant_dynamic-update-slice_fusion), channel_id=1, source_target_pairs={{0,24},{8,0},{16,8},{24,16},{1,25},{9,1},{17,9},{25,17},{2,26},{10... | collective-permute-start | bytes 233480 | tf_op jit(solution)/shard_map/ppermute | solution.py:399
  55.7 6.2 %collective-permute-start.18 = (f32[152,128]{1,0:T(8,128)S(1)}, f32[152,128]{1,0:T(8,128)S(1)}, u32[]{:S(2)}, u32[]{:S(2)}) collective-permute-start(f32[152,128]{1,0:T(8,128)S(1)} %constant_dynamic-update-slice_fusion), channel_id=1, source_target_pairs={{0,8},{8,16},{16,24},{24,0},{1,9},{9,17},{17,25},{25,1},{2,10},{10... | collective-permute-start | bytes 233480 | tf_op jit(solution)/shard_map/ppermute | solution.py:399
  62.0 6.3 %collective-permute-start.23 = (f32[4,80,128]{2,1,0:T(8,128)S(1)}, f32[4,80,128]{2,1,0:T(8,128)S(1)}, u32[]{:S(2)}, u32[]{:S(2)}) collective-permute-start(f32[4,80,128]{2,1,0:T(8,128)S(1)} %slice.103.refs_0_), channel_id=1, source_target_pairs={{0,6},{2,4},{4,2},{6,0},{1,7},{3,5},{5,3},{7,1},{8,14},{10,12},{12... | collective-permute-start | bytes 491528 | tf_op jit(solution)/shard_map/ppermute | solution.py:404
  64.5 6.9 %collective-permute-start.22 = (f32[4,80,128]{2,1,0:T(8,128)S(1)}, f32[4,80,128]{2,1,0:T(8,128)S(1)}, u32[]{:S(2)}, u32[]{:S(2)}) collective-permute-start(f32[4,80,128]{2,1,0:T(8,128)S(1)} %slice.103.refs_0_), channel_id=1, source_target_pairs={{0,4},{4,0},{1,5},{5,1},{2,6},{6,2},{3,7},{7,3},{8,12},{12,8},{9,1... | collective-permute-start | bytes 491528 | tf_op jit(solution)/shard_map/ppermute | solution.py:20
  65.1 7.3 %collective-permute-start.21 = (f32[4,80,128]{2,1,0:T(8,128)S(1)}, f32[4,80,128]{2,1,0:T(8,128)S(1)}, u32[]{:S(2)}, u32[]{:S(2)}) collective-permute-start(f32[4,80,128]{2,1,0:T(8,128)S(1)} %slice.103.refs_0_), channel_id=1, source_target_pairs={{0,2},{2,0},{1,3},{3,1},{4,6},{6,4},{5,7},{7,5},{8,10},{10,8},{9,1... | collective-permute-start | bytes 491528 | tf_op jit(solution)/shard_map/ppermute | solution.py:20
  72.4 9.2 %collective-permute-start.26 = (f32[4,72,128]{2,1,0:T(8,128)S(1)}, f32[4,72,128]{2,1,0:T(8,128)S(1)}, u32[]{:S(2)}, u32[]{:S(2)}) collective-permute-start(f32[4,72,128]{2,1,0:T(8,128)S(1)} %slice.102), channel_id=1, source_target_pairs={{0,6},{2,4},{4,2},{6,0},{1,7},{3,5},{5,3},{7,1},{8,14},{10,12},{12... | collective-permute-start | bytes 442376 | tf_op jit(solution)/shard_map/ppermute | solution.py:404
  75.7 5.9 %collective-permute-start.24 = (f32[4,72,128]{2,1,0:T(8,128)S(1)}, f32[4,72,128]{2,1,0:T(8,128)S(1)}, u32[]{:S(2)}, u32[]{:S(2)}) collective-permute-start(f32[4,72,128]{2,1,0:T(8,128)S(1)} %slice.102), channel_id=1, source_target_pairs={{0,2},{2,0},{1,3},{3,1},{4,6},{6,4},{5,7},{7,5},{8,10},{10,8},{9,1... | collective-permute-start | bytes 442376 | tf_op jit(solution)/shard_map/ppermute | solution.py:20
  89.7 8.3 %collective-permute-start.29 = (f32[512,512]{1,0:T(8,128)S(1)}, f32[512,512]{1,0:T(8,128)S(1)}, u32[]{:S(2)}, u32[]{:S(2)}) collective-permute-start(f32[512,512]{1,0:T(8,128)S(1)} %get-tuple-element.73.own), channel_id=1, source_target_pairs={{0,1},{1,0},{2,3},{3,2},{4,5},{5,4},{6,7},{7,6},{8,9},{9,8},{10,11... | collective-permute-start | bytes 3145736 | tf_op jit(solution)/shard_map/ppermute | solution.py:20
  90.1 37.4 %collective-permute-start.43 = (bf16[2,16,512]{2,1,0:T(8,128)(2,1)S(1)}, bf16[2,16,512]{2,1,0:T(8,128)(2,1)S(1)}, u32[]{:S(2)}, u32[]{:S(2)}) collective-permute-start(bf16[2,16,512]{2,1,0:T(8,128)(2,1)S(1)} %slice.87), channel_id=1, source_target_pairs={{0,4},{4,8},{8,12},{12,16},{16,20},{20,24},{24,28},{1,5},{5,9},{9,... | collective-permute-start | bytes 98312 | tf_op jit(solution)/shard_map/ppermute | solution.py:25
  94.0 33.9 %collective-permute-start.42 = (bf16[2,1024,128]{2,1,0:T(8,128)(2,1)S(1)}, bf16[2,1024,128]{2,1,0:T(8,128)(2,1)S(1)}, u32[]{:S(2)}, u32[]{:S(2)}) collective-permute-start(bf16[2,1024,128]{2,1,0:T(8,128)(2,1)S(1)} %collective-permute-done.11.across), channel_id=1, source_target_pairs={{0,1},{1,0},{2,3},{3,2},{4,5},{5,4},{6,7},{7,6},{8,9},{9,8},{10,11... | collective-permute-start | bytes 1572872 | tf_op jit(solution)/shard_map/ppermute | solution.py:20
  96.1 6.7 %collective-permute-start.30 = (f32[4,64,128]{2,1,0:T(8,128)S(1)}, f32[4,64,128]{2,1,0:T(8,128)S(1)}, u32[]{:S(2)}, u32[]{:S(2)}) collective-permute-start(f32[4,64,128]{2,1,0:T(8,128)S(1)} %get-tuple-element.78), channel_id=1, source_target_pairs={{0,2},{2,0},{1,3},{3,1},{4,6},{6,4},{5,7},{7,5},{8,10},{10,8},{9,1... | collective-permute-start | bytes 393224 | tf_op jit(solution)/shard_map/ppermute | solution.py:20
  97.9 6.3 %collective-permute-start.31 = (f32[4,64,128]{2,1,0:T(8,128)S(1)}, f32[4,64,128]{2,1,0:T(8,128)S(1)}, u32[]{:S(2)}, u32[]{:S(2)}) collective-permute-start(f32[4,64,128]{2,1,0:T(8,128)S(1)} %get-tuple-element.79), channel_id=1, source_target_pairs={{0,4},{4,0},{1,5},{5,1},{2,6},{6,2},{3,7},{7,3},{8,12},{12,8},{9,1... | collective-permute-start | bytes 393224 | tf_op jit(solution)/shard_map/ppermute | solution.py:20
  98.0 8.1 %collective-permute-start.32 = (f32[4,64,128]{2,1,0:T(8,128)S(1)}, f32[4,64,128]{2,1,0:T(8,128)S(1)}, u32[]{:S(2)}, u32[]{:S(2)}) collective-permute-start(f32[4,64,128]{2,1,0:T(8,128)S(1)} %get-tuple-element.80), channel_id=1, source_target_pairs={{0,6},{2,4},{4,2},{6,0},{1,7},{3,5},{5,3},{7,1},{8,14},{10,12},{12... | collective-permute-start | bytes 393224 | tf_op jit(solution)/shard_map/ppermute | solution.py:404
  106.1 8.5 %collective-permute-start.33 = (f32[64,128]{1,0:T(8,128)S(1)}, f32[64,128]{1,0:T(8,128)S(1)}, u32[]{:S(2)}, u32[]{:S(2)}) collective-permute-start(f32[64,128]{1,0:T(8,128)S(1)} %get-tuple-element.101), channel_id=1, source_target_pairs={{0,8},{8,16},{16,24},{24,0},{1,9},{9,17},{17,25},{25,1},{2,10},{10... | collective-permute-start | bytes 98312 | tf_op jit(solution)/shard_map/ppermute | solution.py:399
  106.2 8.4 %collective-permute-start.35 = (f32[64,128]{1,0:T(8,128)S(1)}, f32[64,128]{1,0:T(8,128)S(1)}, u32[]{:S(2)}, u32[]{:S(2)}) collective-permute-start(f32[64,128]{1,0:T(8,128)S(1)} %get-tuple-element.102), channel_id=1, source_target_pairs={{0,24},{8,0},{16,8},{24,16},{1,25},{9,1},{17,9},{25,17},{2,26},{10... | collective-permute-start | bytes 98312 | tf_op jit(solution)/shard_map/ppermute | solution.py:399
  114.8 9.4 %collective-permute-start.38 = (f32[64,128]{1,0:T(8,128)S(1)}, f32[64,128]{1,0:T(8,128)S(1)}, u32[]{:S(2)}, u32[]{:S(2)}) collective-permute-start(f32[64,128]{1,0:T(8,128)S(1)} %fusion.5), channel_id=1, source_target_pairs={{0,24},{8,0},{16,8},{24,16},{1,25},{9,1},{17,9},{25,17},{2,26},{10... | collective-permute-start | bytes 98312 | tf_op jit(solution)/shard_map/ppermute | solution.py:399
  115.8 8.5 %collective-permute-start.37 = (f32[64,128]{1,0:T(8,128)S(1)}, f32[64,128]{1,0:T(8,128)S(1)}, u32[]{:S(2)}, u32[]{:S(2)}) collective-permute-start(f32[64,128]{1,0:T(8,128)S(1)} %fusion.5), channel_id=1, source_target_pairs={{0,16},{8,24},{16,0},{24,8},{1,17},{9,25},{17,1},{25,9},{2,18},{10... | collective-permute-start | bytes 98312 | tf_op jit(solution)/shard_map/ppermute | solution.py:399
  117.7 6.6 %collective-permute-start.36 = (f32[64,128]{1,0:T(8,128)S(1)}, f32[64,128]{1,0:T(8,128)S(1)}, u32[]{:S(2)}, u32[]{:S(2)}) collective-permute-start(f32[64,128]{1,0:T(8,128)S(1)} %fusion.5), channel_id=1, source_target_pairs={{0,8},{8,16},{16,24},{24,0},{1,9},{9,17},{17,25},{25,1},{2,10},{10... | collective-permute-start | bytes 98312 | tf_op jit(solution)/shard_map/ppermute | solution.py:399
  124.2 12.0 %collective-permute-start.45 = (bf16[2,512,512]{2,1,0:T(8,128)(2,1)S(1)}, bf16[2,512,512]{2,1,0:T(8,128)(2,1)S(1)}, u32[]{:S(2)}, u32[]{:S(2)}) collective-permute-start(bf16[2,512,512]{2,1,0:T(8,128)(2,1)S(1)} %shard_map.49.inv), channel_id=1, source_target_pairs={{0,1},{1,0},{2,3},{3,2},{4,5},{5,4},{6,7},{7,6},{8,9},{9,8},{10,11... | collective-permute-start | bytes 3145736 | tf_op jit(solution)/shard_map/ppermute | solution.py:20
  124.4 7.3 %collective-permute-start.41 = (f32[4,64,128]{2,1,0:T(8,128)S(1)}, f32[4,64,128]{2,1,0:T(8,128)S(1)}, u32[]{:S(2)}, u32[]{:S(2)}) collective-permute-start(f32[4,64,128]{2,1,0:T(8,128)S(1)} %pad_maximum_fusion.6), channel_id=1, source_target_pairs={{0,6},{2,4},{4,2},{6,0},{1,7},{3,5},{5,3},{7,1},{8,14},{10,12},{12... | collective-permute-start | bytes 393224 | tf_op jit(solution)/shard_map/ppermute | solution.py:404
  125.8 8.4 %collective-permute-start.40 = (f32[4,64,128]{2,1,0:T(8,128)S(1)}, f32[4,64,128]{2,1,0:T(8,128)S(1)}, u32[]{:S(2)}, u32[]{:S(2)}) collective-permute-start(f32[4,64,128]{2,1,0:T(8,128)S(1)} %pad_maximum_fusion.6), channel_id=1, source_target_pairs={{0,4},{4,0},{1,5},{5,1},{2,6},{6,2},{3,7},{7,3},{8,12},{12,8},{9,1... | collective-permute-start | bytes 393224 | tf_op jit(solution)/shard_map/ppermute | solution.py:20
  127.5 6.7 %collective-permute-start.39 = (f32[4,64,128]{2,1,0:T(8,128)S(1)}, f32[4,64,128]{2,1,0:T(8,128)S(1)}, u32[]{:S(2)}, u32[]{:S(2)}) collective-permute-start(f32[4,64,128]{2,1,0:T(8,128)S(1)} %pad_maximum_fusion.6), channel_id=1, source_target_pairs={{0,2},{2,0},{1,3},{3,1},{4,6},{6,4},{5,7},{7,5},{8,10},{10,8},{9,1... | collective-permute-start | bytes 393224 | tf_op jit(solution)/shard_map/ppermute | solution.py:20
  (17 other events, 71.3 us)

commit v3 on v2

--- a/solution.py
+++ b/solution.py
@@ -88,7 +88,7 @@
         samples[rows - 16 :] = jnp.where(inside, tail, 0.0).astype(BF16)
 
 
-def emit(blocks, flat, outs, start, each):
+def emit(blocks, flat, outs, start, each, turned=True):
     used = 0
     for block in blocks:
         flat[used : used + block.shape[0]] = block
@@ -100,16 +100,16 @@
     z, x, y = lax.axis_index("z"), lax.axis_index("x"), lax.axis_index("y")
     for i, out in enumerate(outs):
         for k in range(depth):
-            part = lax.rem(z + k, depth) * len(outs) + ((x * 2 + y if len(outs) == 4 else x) ^ i)
+            part = (lax.rem(z + k, depth) if turned else k) * len(outs) + ((x * 2 + y if len(outs) == 4 else x) ^ i)
             out[k, start : start + each] = flat[at(part, each)]
 
 
-def sources(depth):
+def sources(depth, turned=True):
     z, x, y = lax.axis_index("z"), lax.axis_index("x"), lax.axis_index("y")
     for i in range(4):
         for k in range(depth):
             xs, ys = x ^ (i >> 1), y ^ (i & 1)
-            zx = lax.rem(z + depth - k, depth) * 2 + xs
+            zx = (lax.rem(z + depth - k, depth) if turned else k) * 2 + xs
             yield i, k, zx, ys
 
 
@@ -167,48 +167,52 @@
     out[...] = (late + dot_last(edge[0], refl[1])).astype(BF16)
 
 
-def near_kernel(width, pd, xd, both, both_core, halo, halo_core, *refs):
+def near_kernel(width, pd, xd, forward, backward, forward_core, backward_core, halo, halo_core, *refs):
     packed, (chosen, behind, late, edge, flat) = refs[:2], refs[2:]
     core = lax.axis_index("core")
     own, other = at(core, width), at(1 - core, width)
-    chosen[:, own], chosen[:, other] = both[core], both_core[core]
-    behind[:, own], behind[:, other] = both[1], both_core[1]
+    behind[:, own], behind[:, other] = backward[...], backward_core[...]
     edge[:, own], edge[:, other] = halo[1], halo_core[1]
+
+    @pl.when(core == 0)
+    def _():
+        chosen[:, own], chosen[:, other] = forward[...], forward_core[...]
+
+    @pl.when(core == 1)
+    def _():
+        chosen[...] = behind[...]
+
     zx = ("z", "x")
     drop_end(chosen, lax.axis_index(zx) == lax.axis_size(zx) - 1)
     value = dot_first(chosen[...], chosen[...])
     emit([value[:width, :width], value[:width, width:], value[width:, width:]], flat, packed, 0, pd)
     delay(behind, edge, late)
-    value = dot_first(both[0], late[...])
+    value = dot_first(forward[...], late[...])
     emit([value[:, :width], value[:, width:]], flat, packed, pd, xd)
 
 
-def far_kernel(width, po, xo, both, across, both_core, across_core, halo, halo_core, halo_y, halo_y_core, *refs):
-    (here, edge, shifted), packed, (tails, samples, flat) = refs[:3], refs[3:7], refs[7:]
+def far_kernel(width, po, xo, *refs):
+    own, across, halos = (refs[0:2], refs[2:4]), (refs[4:6], refs[6:8]), refs[8:12]
+    (here, edges, shifted), packed, (tails, samples, flat) = refs[12:15], refs[15:19], refs[19:]
     y, core = lax.axis_index("y"), lax.axis_index("core")
     half = here.shape[1]
     pair = 2 * width
-    mine, beside = at(y * 2 + core, width), at(y * 2 + 1 - core, width)
-    over, over_beside = at((1 - y) * 2 + core, width), at((1 - y) * 2 + 1 - core, width)
     rows = at(y, half)
-    here[:, :, mine], here[:, :, beside] = both[:, rows], both_core[:, rows]
-    here[:, :, over], here[:, :, over_beside] = across[...], across_core[...]
-    edge[:, :, over], edge[:, :, over_beside] = halo_y[...], halo_y_core[...]
-
-    @pl.when(y == 0)
-    def _():
-        edge[:, :, mine], edge[:, :, beside] = halo[...], halo_core[...]
-
-    @pl.when(y == 1)
-    def _():
-        edge[:, :, mine], edge[:, :, beside] = both[:, half - 16 : half], both_core[:, half - 16 : half]
-
+    for c in range(2):
+        mine = at(y * 2 + (core ^ c), width)
+        over = at((1 - y) * 2 + (core ^ c), width)
+        for kind in range(2):
+            here[kind, :, mine] = own[c][kind][rows]
+            here[kind, :, over] = across[c][kind][...]
+            edges[1, kind, :, mine] = own[c][kind][half - 16 : half]
+        edges[0, :, :, mine] = halos[c][...]
+        edges[:, :, :, over] = halos[2 + c][...]
     samples[...] = here[core]
     drop_end(samples, lax.axis_index(PARTS) == lax.axis_size(PARTS) - 1)
     value = dot_first(samples[:, :pair], samples[:, pair:])
     blocks = lambda v: [v[i : i + width, j : j + width] for i in (0, width) for j in (0, width)]
     emit(blocks(value), flat, packed, 0, po)
-    delay(here.at[1], edge.at[1], shifted)
+    delay(here.at[1], edges.at[y, 1], shifted)
     value = dot_first(here[0, :, at(core, pair)], shifted[:, at(1 - core, pair)])
     emit(blocks(value), flat, packed, po, xo)
     for i, rows in enumerate((here[0, half - 16 :], shifted[half - 16 :])):
@@ -273,24 +277,28 @@
             out[...] = (-value).astype(BF16)
 
 
-def update_cross_kernel(each, here, shifted, edge, ours, theirs, out, late, *refs):
+def update_cross_kernel(each, here, shifted, edges, ours, theirs, out, late, *refs):
     packed, (refl, ahead, flat) = refs[:4], refs[4:]
     by_kind(ours, theirs, refl)
-    update_edge(edge, refl, ahead)
+    update_edge(edges.at[lax.axis_index("y")], refl, ahead)
     update(here, shifted, refl, out)
     delay(out.at[1], ahead, late)
     channels = here.shape[2]
     value = dot_first(out[0, :, at(lax.axis_index("core"), channels // 2)], late[...])
-    emit([value[:, j : j + LANES] for j in range(0, channels, LANES)], flat, packed, 0, each)
-
-
-def there_kernel(width, both, across, both_core, across_core, edge, ours, theirs, out, late, refl, raw, shifted, ahead):
+    emit([value[:, j : j + LANES] for j in range(0, channels, LANES)], flat, packed, 0, each, turned=False)
+
+
+def there_kernel(width, *refs):
+    own, across, (edges, ours, theirs) = (refs[0:2], refs[2:4]), (refs[4:6], refs[6:8]), refs[8:11]
+    out, late, refl, raw, shifted, ahead = refs[11:]
     y, core = lax.axis_index("y"), lax.axis_index("core")
     by_kind(ours, theirs, refl)
+    edge = edges.at[1 - y]
     rows = at(1 - y, raw.shape[1])
-    raw[:, :, at(y * 2 + core, width)], raw[:, :, at(y * 2 + 1 - core, width)] = both[:, rows], both_core[:, rows]
-    raw[:, :, at((1 - y) * 2 + core, width)] = across[...]
-    raw[:, :, at((1 - y) * 2 + 1 - core, width)] = across_core[...]
+    for c in range(2):
+        for kind in range(2):
+            raw[kind, :, at(y * 2 + (core ^ c), width)] = own[c][kind][rows]
+            raw[kind, :, at((1 - y) * 2 + (core ^ c), width)] = across[c][kind][...]
     delay(raw.at[1], edge.at[1], shifted)
     update_edge(edge, refl, ahead)
     update(raw, shifted, refl, out)
@@ -365,7 +373,7 @@
     channels = here.shape[2]
     half, depth, each = channels // 2, ours.shape[1], ours.shape[2]
     for gathered, home in ((ours, core), (theirs, 1 - core)):
-        for i, k, zx, ys in sources(depth):
+        for i, k, zx, ys in sources(depth, turned=False):
             flat[at(zx * 2 + ys, each)] = gathered[i, k]
         rows = at(home, half)
         for j in range(channels // LANES):
@@ -437,45 +445,45 @@
     flat = lambda *rows: pltpu.VMEM((max(rows), LANES), F32)
     kernel = functools.partial
 
-    halo = from_behind(jnp.stack([fwd_in[samples - 16 :], bwd_in[samples - 16 :]]), zx)
-    cut = lambda which: jnp.stack([lax.dynamic_slice_in_dim(a, which * half, half, 0) for a in (fwd_in, bwd_in)])
-    other = cut(1 - y)
-    across = swap(other, "y")
-    both = jnp.stack([after(fwd_in, other), bwd_in])
-    both_core = swap(both, "core")
+    own = (fwd_in, bwd_in)
+    cut = lambda which: [lax.dynamic_slice_in_dim(a, which * half, half, 0) for a in own]
+    across = [swap(a, "y") for a in cut(1 - y)]
+    tail = lambda end: jnp.stack([a[end - 16 : end] for a in own])
+    halo = from_behind(tail(samples), zx)
+    own_core = [swap(a, "core") for a in own]
     halo_core = swap(halo, "core")
-    halo_y = swap(jnp.where(y == 0, both[:, half - 16 : half], halo), "y")
+    halo_y = swap(jnp.stack([halo, tail(half)]), "y")
     near = call(
         kernel(near_kernel, width, pd, xd),
         [shape((depth, pd + xd, LANES), F32)] * 2,
         [pltpu.VMEM((samples, pair), BF16)] * 3 + [pltpu.VMEM((16, pair), BF16), flat(near_parts * pd, near_parts * xd)],
         3 * samples * pair * pair,
-        both, both_core, halo, halo_core,
+        *own, *own_core, halo, halo_core,
     )
     near_x = swap(near[1], "x")
     halo_y_core = swap(after(halo_y, near[1]), "core")
-    across = after(across, near[1], halo_y_core)
-    across2 = swap(after(cut(y), across), "y")
-    across_core = swap(across, "core")
-    here, edge, shifted, *far, tails = call(
+    across_core = [swap(across[0], "core"), swap(after(across[1], near[1]), "core")]
+    here, edges, shifted, *far, tails = call(
         kernel(far_kernel, width, po, xo),
         [
             shape((2, half, channels), BF16),
-            shape((2, 16, channels), BF16),
+            shape((2, 2, 16, channels), BF16),
             shape((half, channels), BF16),
             *[shape((depth, po + xo, LANES), F32)] * 4,
             shape((8, LANES), F32),
         ],
         [pltpu.VMEM((half, channels), BF16), flat(parts * po, parts * xo)],
         4 * half * pair * pair,
-        both, across, both_core, across_core, halo, halo_core, halo_y, halo_y_core,
+        *own, *own_core, *across, *across_core, halo, halo_core, halo_y, halo_y_core,
     )
     near_sum = scatter_z([after(near[0], far[0]), near_x])
     swapped = exchange(far)
-    far_sum = scatter_z([after(swapped[0], across2)] + swapped[1:])
+    swapped[0] = after(swapped[0], near_sum)
+    across2 = [swap(after(a, swapped[1]), "y") for a in cut(y)]
+    far_sum = scatter_z(swapped)
     chunk = jnp.concatenate([near_sum[:pd], far_sum[:po], near_sum[pd:], far_sum[po:], tails])
     column = z_gather(chunk)
-    pieces = xy_gather(column[:, : pd + po])
+    pieces = xy_gather(after(column[:, : pd + po], *across2))
     stop = NSTEPS // 2
     state = [shape((channels, channels), F32)] * 2 + [shape((8, LANES), F32)]
     full, error, iterate, scale = call(
@@ -504,9 +512,9 @@
         [shape((2, half, channels), BF16), shape((half, channels), BF16)] + [shape((depth, each, LANES), F32)] * 4,
         [square16(2), pltpu.VMEM((16, channels), BF16), flat(parts * each)],
         5 * half * channels * channels,
-        here, shifted, edge, refl, refl_core,
-    )
-    across2_core = swap(after(across2, column), "core")
+        here, shifted, edges, refl, refl_core,
+    )
+    across2_core = [swap(a, "core") for a in across2]
     full_core = swap(after(full, refl_core), "core")
     matrix2, scale2 = call(
         predict_kernel,
@@ -519,18 +527,16 @@
         kernel(begin_kernel, stop), state[:2], tables, 30 * channels**3, matrix2, scale2
     )
     swapped = exchange(packed)
-    cross_sum = after(scatter_z([after(swapped[0], matrix2)] + swapped[1:]), error2)
-    inv2 = finish(after(error2, cross_sum), iterate2, scale2)
+    swapped[0] = after(swapped[0], matrix2)
+    column2 = jnp.sum(z_gather(sum(swapped[1:], swapped[0])), axis=0)
+    inv2 = finish(error2, iterate2, scale2)
     inv2_core = swap(inv2, "core")
-    column2 = z_gather(cross_sum)
-    tail = here[:, half - 16 :]
-    edge2 = jnp.where(y == 0, tail, from_behind(tail, zx))
     there2, there_shifted2 = call(
         kernel(there_kernel, width),
         [shape((2, half, channels), BF16), shape((half, channels), BF16)],
         [square16(2), pltpu.VMEM((2, half, channels), BF16), pltpu.VMEM((half, channels), BF16), pltpu.VMEM((16, channels), BF16)],
         4 * half * channels * channels,
-        both, across2, both_core, across2_core, edge2, refl, after(refl_core, column2),
+        *own, *own_core, *across2, *across2_core, edges, refl, after(refl_core, column2),
     )
     ours2 = jnp.stack(xy_gather(after(column2, inv2)))
     theirs2 = swap(after(ours2, there2), "core")

time: 139 us -> 122 us (0.88)
  starting transfers between devices: 54.9 us -> 45.3 us
  waiting for transfers between devices: 45.6 us -> 40.4 us
  other arithmetic: 1.93 us -> 0.29 us
    ppermute x15 -> x12, starting transfers between devices: 21.3 us -> 13.2 us  [ahead(): return lax.ppermute(piece, 'z', [(i, (i + by) % size) for i in range(size)])]
    ppermute x24 -> x29, waiting for transfers between devices: 27.3 us -> 20.1 us  [swap(): return lax.ppermute(value, axis, [(0, 1), (1, 0)])]
    ppermute x24 -> x29, starting transfers between devices: 17.1 us -> 21.5 us  [swap(): return lax.ppermute(value, axis, [(0, 1), (1, 0)])]
    ppermute x2 -> x1, starting transfers between devices: 7.29 us -> 3.86 us  [from_behind(): return lax.ppermute(value, axes, [(i, i + 1) for i in range(devices - 1)])]
    another operation x3 -> x2, local copies, waits for them, and re-layouts: 2.74 us -> 0.01 us  [local(): tail = lambda end: jnp.stack([a[end - 16:end] for a in own])]
    ppermute x5, starting transfers between devices: 9.19 us -> 6.82 us  [exchange(): lax.ppermute(pieces[3], ('x', 'y'), both)]
    dynamic_slice x0 -> x2, local copies, waits for them, and re-layouts: none -> 2.13 us  [local(): lax.dynamic_slice_in_dim(a, which * half, half, 0)]
    ppermute x15 -> x12, waiting for transfers between devices: 9.51 us -> 11.4 us  [ahead(): return lax.ppermute(piece, 'z', [(i, (i + by) % size) for i in range(size)])]
  transfers between devices with their start and end apart: 46 -> 47, of which waited for: 23 -> 27; matrix products, arithmetic and copies ran while one was open for 1% -> 2% of each run, Pallas kernels for 21% -> 24%
where the time goes in v3:
time: 122 us
  starting transfers between devices  45.3 us (37%)
  waiting for transfers between devices  40.4 us (33%)
  Pallas kernels  33.2 us (27%)
  local copies, waits for them, and re-layouts  2.18 us (2%)
    pallas_call x11, Pallas kernels, call(): pl.pallas_call(body, out_shape=shapes, in_specs=[VMEM] * len(args), out_s...  33.2 us
    ppermute x29, starting transfers between devices, swap(): return lax.ppermute(value, axis, [(0, 1), (1, 0)])  21.5 us
    ppermute x29, waiting for transfers between devices, swap(): return lax.ppermute(value, axis, [(0, 1), (1, 0)])  20.1 us
    ppermute x12, starting transfers between devices, ahead(): return lax.ppermute(piece, 'z', [(i, (i + by) % size) for i in range(size)])  13.2 us
    ppermute x12, waiting for transfers between devices, ahead(): return lax.ppermute(piece, 'z', [(i, (i + by) % size) for i in range(size)])  11.4 us
    ppermute x5, waiting for transfers between devices, exchange(): lax.ppermute(pieces[3], ('x', 'y'), both)  7.54 us
    ppermute x5, starting transfers between devices, exchange(): lax.ppermute(pieces[3], ('x', 'y'), both)  6.82 us
    ppermute x1, starting transfers between devices, from_behind(): return lax.ppermute(value, axes, [(i, i + 1) for i in range(devices - 1)])  3.86 us
  transfers between devices with their start and end apart: 47, of which 27 were waited for; matrix products, arithmetic and copies ran while one was open for 2% of the time, Pallas kernels for 24%

profile of v3, /device:TPU:0, one launch (start us, length us, event | category | flops | bytes accessed | tf_op | source)
XLA Modules:
  0.0 122.3 jit_solution(5093032411989555663)
XLA Ops:
  2.3 3.0 %collective-permute-start.2 = (bf16[1024,128]{1,0:T(8,128)(2,1)S(1)}, bf16[1024,128]{1,0:T(8,128)(2,1)S(1)}, u32[]{:S(2)}, u32[]{:S(2)}) collective-permute-start(bf16[1024,128]{1,0:T(8,128)(2,1)S(1)} %get-tuple-element.93), channel_id=1, source_target_pairs={{0,2},{2,0},{1,3},{3,1},{4,6},{6,4},{5,7},{7,5},{8,10},{10,8},{9,1... | collective-permute-start | bytes 786440 | tf_op jit(solution)/shard_map/ppermute | solution.py:20
  6.5 3.9 %collective-permute-start.5 = (bf16[2,16,128]{2,1,0:T(8,128)(2,1)S(1)}, bf16[2,16,128]{2,1,0:T(8,128)(2,1)S(1)}, u32[]{:S(2)}, u32[]{:S(2)}) collective-permute-start(bf16[2,16,128]{2,1,0:T(8,128)(2,1)S(1)} %pad_maximum_fusion.7), channel_id=1, source_target_pairs={{0,4},{4,8},{8,12},{12,16},{16,20},{20,24},{24,28},{1,5},{5,9},{9,... | collective-permute-start | bytes 24584 | tf_op jit(solution)/shard_map/ppermute | solution.py:25
  14.1 3.4 %collective-permute-done.3.refs_5_ = bf16[1024,128]{1,0:T(8,128)(2,1)S(1)} collective-permute-done((bf16[1024,128]{1,0:T(8,128)(2,1)S(1)}, bf16[1024,128]{1,0:T(8,128)(2,1)S(1)}, u32[]{:S(2)}, u32[]{:S(2)}) %collective-permute-start.3) | collective-permute-done | bytes 262176 | tf_op jit(solution)/shard_map/ppermute | solution.py:20
  17.5 1.7 %collective-permute-start.10 = (f32[4,80,128]{2,1,0:T(8,128)S(1)}, f32[4,80,128]{2,1,0:T(8,128)S(1)}, u32[]{:S(2)}, u32[]{:S(2)}) collective-permute-start(f32[4,80,128]{2,1,0:T(8,128)S(1)} %get-tuple-element.46), channel_id=1, source_target_pairs={{0,4},{4,0},{1,5},{5,1},{2,6},{6,2},{3,7},{7,3},{8,12},{12,8},{9,1... | collective-permute-start | bytes 491528 | tf_op jit(solution)/shard_map/ppermute | solution.py:20
  19.2 1.5 %collective-permute-start.8 = (bf16[2,2,16,128]{3,2,1,0:T(8,128)(2,1)S(1)}, bf16[2,2,16,128]{3,2,1,0:T(8,128)(2,1)S(1)}, u32[]{:S(2)}, u32[]{:S(2)}) collective-permute-start(bf16[2,2,16,128]{3,2,1,0:T(8,128)(2,1)S(1)} %pad_maximum_fusion.6), channel_id=1, source_target_pairs={{0,2},{2,0},{1,3},{3,1},{4,6},{6,4},{5,7},{7,5},{8,10},{10,8},{9,1... | collective-permute-start | bytes 49160 | tf_op jit(solution)/shard_map/ppermute | solution.py:20
  20.7 2.2 %collective-permute-done.8.refs_10_ = bf16[2,2,16,128]{3,2,1,0:T(8,128)(2,1)S(1)} collective-permute-done((bf16[2,2,16,128]{3,2,1,0:T(8,128)(2,1)S(1)}, bf16[2,2,16,128]{3,2,1,0:T(8,128)(2,1)S(1)}, u32[]{:S(2)}, u32[]{:S(2)}) %collective-permute-start.8) | collective-permute-done | bytes 16416 | tf_op jit(solution)/shard_map/ppermute | solution.py:20
  25.4 3.7 %collective-permute-start.13 = (f32[80,128]{1,0:T(8,128)S(1)}, f32[80,128]{1,0:T(8,128)S(1)}, u32[]{:S(2)}, u32[]{:S(2)}) collective-permute-start(f32[80,128]{1,0:T(8,128)S(1)} %get-tuple-element.99), channel_id=1, source_target_pairs={{0,24},{8,0},{16,8},{24,16},{1,25},{9,1},{17,9},{25,17},{2,26},{10... | collective-permute-start | bytes 122888 | tf_op jit(solution)/shard_map/ppermute | solution.py:407
  34.9 2.3 %collective-permute-done.16 = f32[4,64,128]{2,1,0:T(8,128)S(1)} collective-permute-done((f32[4,64,128]{2,1,0:T(8,128)S(1)}, f32[4,64,128]{2,1,0:T(8,128)S(1)}, u32[]{:S(2)}, u32[]{:S(2)}) %collective-permute-start.16) | collective-permute-done | bytes 131104 | tf_op jit(solution)/shard_map/ppermute | solution.py:412
  38.7 3.1 %collective-permute-start.19 = (f32[64,128]{1,0:T(8,128)S(1)}, f32[64,128]{1,0:T(8,128)S(1)}, u32[]{:S(2)}, u32[]{:S(2)}) collective-permute-start(f32[64,128]{1,0:T(8,128)S(1)} %get-tuple-element.102), channel_id=1, source_target_pairs={{0,24},{8,0},{16,8},{24,16},{1,25},{9,1},{17,9},{25,17},{2,26},{10... | collective-permute-start | bytes 98312 | tf_op jit(solution)/shard_map/ppermute | solution.py:407
  45.0 1.7 %collective-permute-done.18 = f32[64,128]{1,0:T(8,128)S(1)} collective-permute-done((f32[64,128]{1,0:T(8,128)S(1)}, f32[64,128]{1,0:T(8,128)S(1)}, u32[]{:S(2)}, u32[]{:S(2)}) %collective-permute-start.18) | collective-permute-done | bytes 32800 | tf_op jit(solution)/shard_map/ppermute | solution.py:407
  46.6 1.9 %collective-permute-done.17 = f32[64,128]{1,0:T(8,128)S(1)} collective-permute-done((f32[64,128]{1,0:T(8,128)S(1)}, f32[64,128]{1,0:T(8,128)S(1)}, u32[]{:S(2)}, u32[]{:S(2)}) %collective-permute-start.17) | collective-permute-done | bytes 32800 | tf_op jit(solution)/shard_map/ppermute | solution.py:407
  48.9 1.9 %collective-permute-start.20 = (f32[152,128]{1,0:T(8,128)S(1)}, f32[152,128]{1,0:T(8,128)S(1)}, u32[]{:S(2)}, u32[]{:S(2)}) collective-permute-start(f32[152,128]{1,0:T(8,128)S(1)} %constant_dynamic-update-slice_fusion), channel_id=1, source_target_pairs={{0,8},{8,16},{16,24},{24,0},{1,9},{9,17},{17,25},{25,1},{2,10},{10... | collective-permute-start | bytes 233480 | tf_op jit(solution)/shard_map/ppermute | solution.py:407
  50.8 2.5 %collective-permute-done.22 = f32[152,128]{1,0:T(8,128)S(1)} collective-permute-done((f32[152,128]{1,0:T(8,128)S(1)}, f32[152,128]{1,0:T(8,128)S(1)}, u32[]{:S(2)}, u32[]{:S(2)}) %collective-permute-start.22) | collective-permute-done | bytes 77856 | tf_op jit(solution)/shard_map/ppermute | solution.py:407
  54.1 2.1 %collective-permute-done.20 = f32[152,128]{1,0:T(8,128)S(1)} collective-permute-done((f32[152,128]{1,0:T(8,128)S(1)}, f32[152,128]{1,0:T(8,128)S(1)}, u32[]{:S(2)}, u32[]{:S(2)}) %collective-permute-start.20) | collective-permute-done | bytes 77856 | tf_op jit(solution)/shard_map/ppermute | solution.py:407
  58.3 1.5 %collective-permute-start.27 = (f32[4,80,128]{2,1,0:T(8,128)S(1)}, f32[4,80,128]{2,1,0:T(8,128)S(1)}, u32[]{:S(2)}, u32[]{:S(2)}) collective-permute-start(f32[4,80,128]{2,1,0:T(8,128)S(1)} %pad_maximum_fusion.2.refs_0_), channel_id=1, source_target_pairs={{0,6},{2,4},{4,2},{6,0},{1,7},{3,5},{5,3},{7,1},{8,14},{10,12},{12... | collective-permute-start | bytes 491528 | tf_op jit(solution)/shard_map/ppermute | solution.py:412
  59.8 2.1 %collective-permute-done.25.refs_1_ = f32[4,80,128]{2,1,0:T(8,128)S(1)} collective-permute-done((f32[4,80,128]{2,1,0:T(8,128)S(1)}, f32[4,80,128]{2,1,0:T(8,128)S(1)}, u32[]{:S(2)}, u32[]{:S(2)}) %collective-permute-start.25) | collective-permute-done | bytes 163872 | tf_op jit(solution)/shard_map/ppermute | solution.py:20
  63.0 3.2 %collective-permute-done.27.refs_3_ = f32[4,80,128]{2,1,0:T(8,128)S(1)} collective-permute-done((f32[4,80,128]{2,1,0:T(8,128)S(1)}, f32[4,80,128]{2,1,0:T(8,128)S(1)}, u32[]{:S(2)}, u32[]{:S(2)}) %collective-permute-start.27) | collective-permute-done | bytes 163872 | tf_op jit(solution)/shard_map/ppermute | solution.py:412
  69.7 5.3 %shard_map.43 = (f32[512,512]{1,0:T(8,128)S(1)}, f32[512,512]{1,0:T(8,128)S(1)}, f32[512,512]{1,0:T(8,128)S(1)}, f32[8,128]{1,0:T(8,128)S(1)}) custom-call(f32[4,80,128]{2,1,0:T(8,128)S(1)} %pad_maximum_fusion.2.refs_0_, f32[4,80,128]{2,1,0:T(8,128)S(1)} %collective-permute-done.25.refs_1_, f32[4,80,128]{2,1,0:T(8,128)S(1)} %collective-permute-done.26.refs_2_, ...), custom_call_target="tpu_custom_call" | custom-call | flops 4026531840 | bytes 3805184 | tf_op jit(solution)/shard_map/pallas_call | solution.py:34
  75.2 4.5 %shard_map.44.inv = bf16[2,512,512]{2,1,0:T(8,128)(2,1)S(1)} custom-call(f32[512,512]{1,0:T(8,128)S(1)} %get-tuple-element.64.error, f32[512,512]{1,0:T(8,128)S(1)} %get-tuple-element.66.iterate, f32[8,128]{1,0:T(8,128)S(1)} %get-tuple-element.67.scale), custom_call_target="tpu_custom_call" | custom-call | flops 4026531840 | bytes 3149824 | tf_op jit(solution)/shard_map/pallas_call | solution.py:34
  81.7 1.5 %collective-permute-done.32.theirs.refs_10_ = bf16[512,512]{1,0:T(8,128)(2,1)S(1)} collective-permute-done((bf16[512,512]{1,0:T(8,128)(2,1)S(1)}, bf16[512,512]{1,0:T(8,128)(2,1)S(1)}, u32[]{:S(2)}, u32[]{:S(2)}) %collective-permute-start.32) | collective-permute-done | bytes 524320 | tf_op jit(solution)/shard_map/ppermute | solution.py:20
  83.6 2.0 %shard_map.46 = (bf16[2,1024,512]{2,1,0:T(8,128)(2,1)S(1)}, bf16[1024,512]{1,0:T(8,128)(2,1)S(1)}, f32[4,64,128]{2,1,0:T(8,128)S(1)}, f32[4,64,128]{2,1,0:T(8,12...) custom-call(bf16[2,1024,512]{2,1,0:T(8,128)(2,1)S(1)} %get-tuple-element.49.here, ...), custom_call_target="tpu_custom_call" | custom-call | flops 1342177280 | bytes 7929856 | tf_op jit(solution)/shard_map/pallas_call | solution.py:34
  89.2 3.3 %shard_map.47 = (f32[512,512]{1,0:T(8,128)S(1)}, f32[8,128]{1,0:T(8,128)S(1)}) custom-call(f32[512,512]{1,0:T(8,128)S(1)} %get-tuple-element.72.own, f32[512,512]{1,0:T(8,128)S(1)} %collective-permute-done.33.other, f32[512,512]{1,0:T(8,128)S(1)} %get-tuple-element.73.cross, bf16[512,512]{1,0:T(8,128)(2,1)S(1)} %collective-permute-done.32.theirs.refs_10_, ...), custom_call_target="tpu_custom_call" | custom-call | flops 2415919104 | bytes 4726784 | tf_op jit(solution)/shard_map/pallas_call | solution.py:34
  93.0 1.6 %collective-permute-done.35 = f32[4,64,128]{2,1,0:T(8,128)S(1)} collective-permute-done((f32[4,64,128]{2,1,0:T(8,128)S(1)}, f32[4,64,128]{2,1,0:T(8,128)S(1)}, u32[]{:S(2)}, u32[]{:S(2)}) %collective-permute-start.35) | collective-permute-done | bytes 131104 | tf_op jit(solution)/shard_map/ppermute | solution.py:20
  97.1 4.6 %shard_map.48 = (f32[512,512]{1,0:T(8,128)S(1)}, f32[512,512]{1,0:T(8,128)S(1)}) custom-call(f32[512,512]{1,0:T(8,128)S(1)} %get-tuple-element.75.matrix, f32[8,128]{1,0:T(8,128)S(1)} %get-tuple-element.80.scale), custom_call_target="tpu_custom_call" | custom-call | flops 4026531840 | bytes 3149824 | tf_op jit(solution)/shard_map/pallas_call | solution.py:34
  101.7 4.6 %shard_map.49.inv = bf16[2,512,512]{2,1,0:T(8,128)(2,1)S(1)} custom-call(f32[512,512]{1,0:T(8,128)S(1)} %get-tuple-element.81.error, f32[512,512]{1,0:T(8,128)S(1)} %get-tuple-element.82.iterate, f32[8,128]{1,0:T(8,128)S(1)} %get-tuple-element.80.scale), custom_call_target="tpu_custom_call" | custom-call | flops 4026531840 | bytes 3149824 | tf_op jit(solution)/shard_map/pallas_call | solution.py:34
  108.1 1.8 %collective-permute-start.42 = (f32[4,64,128]{2,1,0:T(8,128)S(1)}, f32[4,64,128]{2,1,0:T(8,128)S(1)}, u32[]{:S(2)}, u32[]{:S(2)}) collective-permute-start(f32[4,64,128]{2,1,0:T(8,128)S(1)} %add_add_fusion), channel_id=1, source_target_pairs={{0,6},{2,4},{4,2},{6,0},{1,7},{3,5},{5,3},{7,1},{8,14},{10,12},{12... | collective-permute-start | bytes 393224 | tf_op jit(solution)/shard_map/ppermute | solution.py:412
  109.8 1.7 %collective-permute-start.41 = (f32[4,64,128]{2,1,0:T(8,128)S(1)}, f32[4,64,128]{2,1,0:T(8,128)S(1)}, u32[]{:S(2)}, u32[]{:S(2)}) collective-permute-start(f32[4,64,128]{2,1,0:T(8,128)S(1)} %add_add_fusion), channel_id=1, source_target_pairs={{0,4},{4,0},{1,5},{5,1},{2,6},{6,2},{3,7},{7,3},{8,12},{12,8},{9,1... | collective-permute-start | bytes 393224 | tf_op jit(solution)/shard_map/ppermute | solution.py:20
  111.6 2.1 %shard_map.50 = (bf16[2,1024,512]{2,1,0:T(8,128)(2,1)S(1)}, bf16[1024,512]{1,0:T(8,128)(2,1)S(1)}) custom-call(bf16[2048,128]{1,0:T(8,128)(2,1)S(1)} %copy-done, bf16[2048,128]{1,0:T(8,128)(2,1)S(1)} %copy-done.1, bf16[2048,128]{1,0:T(8,128)(2,1)S(1)} %collective-permute-done.forward_core.refs_2_, ...), custom_call_target="tpu_custom_call" | custom-call | flops 1073741824 | bytes 7405568 | tf_op jit(solution)/shard_map/pallas_call | solution.py:34
  113.7 1.6 %collective-permute-done.42 = f32[4,64,128]{2,1,0:T(8,128)S(1)} collective-permute-done((f32[4,64,128]{2,1,0:T(8,128)S(1)}, f32[4,64,128]{2,1,0:T(8,128)S(1)}, u32[]{:S(2)}, u32[]{:S(2)}) %collective-permute-start.42) | collective-permute-done | bytes 131104 | tf_op jit(solution)/shard_map/ppermute | solution.py:412
  115.3 2.0 %collective-permute-done.41 = f32[4,64,128]{2,1,0:T(8,128)S(1)} collective-permute-done((f32[4,64,128]{2,1,0:T(8,128)S(1)}, f32[4,64,128]{2,1,0:T(8,128)S(1)}, u32[]{:S(2)}, u32[]{:S(2)}) %collective-permute-start.41) | collective-permute-done | bytes 131104 | tf_op jit(solution)/shard_map/ppermute | solution.py:20
  117.4 1.9 %collective-permute-done.45.theirs = f32[4,4,64,128]{3,2,1,0:T(8,128)S(1)} collective-permute-done((f32[4,4,64,128]{3,2,1,0:T(8,128)S(1)}, f32[4,4,64,128]{3,2,1,0:T(8,128)S(1)}, u32[]{:S(2)}, u32[]{:S(2)}) %collective-permute-start.45) | collective-permute-done | bytes 524320 | tf_op jit(solution)/shard_map/ppermute | solution.py:20
  119.3 2.9 %shard_map.51 = (bf16[2048,128]{1,0:T(8,128)(2,1)}, bf16[2048,128]{1,0:T(8,128)(2,1)}) custom-call(f32[4,4,64,128]{3,2,1,0:T(8,128)S(1)} %pad_maximum_fusion.1.ours, f32[4,4,64,128]{3,2,1,0:T(8,128)S(1)} %collective-permute-done.45.theirs, bf16[2,512,512]{2,1,0:T(8,128)(2,1)S(1)} %shard_map.49.inv, ...), custom_call_target="tpu_custom_call" | custom-call | flops 536870912 | bytes 10485760 | tf_op jit(solution)/shard_map/pallas_call | solution.py:34
  (101 shorter events, 38.2 us)
Async XLA Ops:
  0.7 12.3 %collective-permute-start = (bf16[2048,128]{1,0:T(8,128)(2,1)}, bf16[2048,128]{1,0:T(8,128)(2,1)S(1)}, u32[]{:S(2)}, u32[]{:S(2)}) collective-permute-start(bf16[2048,128]{1,0:T(8,128)(2,1)} %refs_0_.3), channel_id=1, source_target_pairs={{0,1},{1,0},{2,3},{3,2},{4,5},{5,4},{6,7},{7,6},{8,9},{9,8},{10,11... | collective-permute-start | bytes 1572872 | tf_op jit(solution)/shard_map/ppermute | solution.py:20
  1.2 11.8 %collective-permute-start.1 = (bf16[2048,128]{1,0:T(8,128)(2,1)}, bf16[2048,128]{1,0:T(8,128)(2,1)S(1)}, u32[]{:S(2)}, u32[]{:S(2)}) collective-permute-start(bf16[2048,128]{1,0:T(8,128)(2,1)} %refs_1_.3), channel_id=1, source_target_pairs={{0,1},{1,0},{2,3},{3,2},{4,5},{5,4},{6,7},{7,6},{8,9},{9,8},{10,11... | collective-permute-start | bytes 1572872 | tf_op jit(solution)/shard_map/ppermute | solution.py:20
  2.3 10.1 %collective-permute-start.2 = (bf16[1024,128]{1,0:T(8,128)(2,1)S(1)}, bf16[1024,128]{1,0:T(8,128)(2,1)S(1)}, u32[]{:S(2)}, u32[]{:S(2)}) collective-permute-start(bf16[1024,128]{1,0:T(8,128)(2,1)S(1)} %get-tuple-element.93), channel_id=1, source_target_pairs={{0,2},{2,0},{1,3},{3,1},{4,6},{6,4},{5,7},{7,5},{8,10},{10,8},{9,1... | collective-permute-start | bytes 786440 | tf_op jit(solution)/shard_map/ppermute | solution.py:20
  6.4 11.1 %collective-permute-start.3 = (bf16[1024,128]{1,0:T(8,128)(2,1)S(1)}, bf16[1024,128]{1,0:T(8,128)(2,1)S(1)}, u32[]{:S(2)}, u32[]{:S(2)}) collective-permute-start(bf16[1024,128]{1,0:T(8,128)(2,1)S(1)} %get-tuple-element.91), channel_id=1, source_target_pairs={{0,2},{2,0},{1,3},{3,1},{4,6},{6,4},{5,7},{7,5},{8,10},{10,8},{9,1... | collective-permute-start | bytes 786440 | tf_op jit(solution)/shard_map/ppermute | solution.py:20
  12.4 10.5 %collective-permute-start.4 = (bf16[1024,128]{1,0:T(8,128)(2,1)S(1)}, bf16[1024,128]{1,0:T(8,128)(2,1)S(1)}, u32[]{:S(2)}, u32[]{:S(2)}) collective-permute-start(bf16[1024,128]{1,0:T(8,128)(2,1)S(1)} %collective-permute-done.2.refs_4_), channel_id=1, source_target_pairs={{0,1},{1,0},{2,3},{3,2},{4,5},{5,4},{6,7},{7,6},{8,9},{9,8},{10,11... | collective-permute-start | bytes 786440 | tf_op jit(solution)/shard_map/ppermute | solution.py:20
  17.5 6.7 %collective-permute-start.7 = (bf16[1024,128]{1,0:T(8,128)(2,1)S(1)}, bf16[1024,128]{1,0:T(8,128)(2,1)S(1)}, u32[]{:S(2)}, u32[]{:S(2)}) collective-permute-start(bf16[1024,128]{1,0:T(8,128)(2,1)S(1)} %collective-permute-done.3.refs_5_), channel_id=1, source_target_pairs={{0,1},{1,0},{2,3},{3,2},{4,5},{5,4},{6,7},{7,6},{8,9},{9,8},{10,11... | collective-permute-start | bytes 786440 | tf_op jit(solution)/shard_map/ppermute | solution.py:20
  17.5 7.9 %collective-permute-start.10 = (f32[4,80,128]{2,1,0:T(8,128)S(1)}, f32[4,80,128]{2,1,0:T(8,128)S(1)}, u32[]{:S(2)}, u32[]{:S(2)}) collective-permute-start(f32[4,80,128]{2,1,0:T(8,128)S(1)} %get-tuple-element.46), channel_id=1, source_target_pairs={{0,4},{4,0},{1,5},{5,1},{2,6},{6,2},{3,7},{7,3},{8,12},{12,8},{9,1... | collective-permute-start | bytes 491528 | tf_op jit(solution)/shard_map/ppermute | solution.py:20
  25.4 7.7 %collective-permute-start.13 = (f32[80,128]{1,0:T(8,128)S(1)}, f32[80,128]{1,0:T(8,128)S(1)}, u32[]{:S(2)}, u32[]{:S(2)}) collective-permute-start(f32[80,128]{1,0:T(8,128)S(1)} %get-tuple-element.99), channel_id=1, source_target_pairs={{0,24},{8,0},{16,8},{24,16},{1,25},{9,1},{17,9},{25,17},{2,26},{10... | collective-permute-start | bytes 122888 | tf_op jit(solution)/shard_map/ppermute | solution.py:407
  29.1 5.8 %collective-permute-start.11 = (f32[80,128]{1,0:T(8,128)S(1)}, f32[80,128]{1,0:T(8,128)S(1)}, u32[]{:S(2)}, u32[]{:S(2)}) collective-permute-start(f32[80,128]{1,0:T(8,128)S(1)} %get-tuple-element.98), channel_id=1, source_target_pairs={{0,8},{8,16},{16,24},{24,0},{1,9},{9,17},{17,25},{25,1},{2,10},{10... | collective-permute-start | bytes 122888 | tf_op jit(solution)/shard_map/ppermute | solution.py:407
  30.1 7.1 %collective-permute-start.16 = (f32[4,64,128]{2,1,0:T(8,128)S(1)}, f32[4,64,128]{2,1,0:T(8,128)S(1)}, u32[]{:S(2)}, u32[]{:S(2)}) collective-permute-start(f32[4,64,128]{2,1,0:T(8,128)S(1)} %get-tuple-element.58), channel_id=1, source_target_pairs={{0,6},{2,4},{4,2},{6,0},{1,7},{3,5},{5,3},{7,1},{8,14},{10,12},{12... | collective-permute-start | bytes 393224 | tf_op jit(solution)/shard_map/ppermute | solution.py:412
  31.6 7.0 %collective-permute-start.15 = (f32[4,64,128]{2,1,0:T(8,128)S(1)}, f32[4,64,128]{2,1,0:T(8,128)S(1)}, u32[]{:S(2)}, u32[]{:S(2)}) collective-permute-start(f32[4,64,128]{2,1,0:T(8,128)S(1)} %get-tuple-element.57), channel_id=1, source_target_pairs={{0,4},{4,0},{1,5},{5,1},{2,6},{6,2},{3,7},{7,3},{8,12},{12,8},{9,1... | collective-permute-start | bytes 393224 | tf_op jit(solution)/shard_map/ppermute | solution.py:20
  38.7 6.3 %collective-permute-start.19 = (f32[64,128]{1,0:T(8,128)S(1)}, f32[64,128]{1,0:T(8,128)S(1)}, u32[]{:S(2)}, u32[]{:S(2)}) collective-permute-start(f32[64,128]{1,0:T(8,128)S(1)} %get-tuple-element.102), channel_id=1, source_target_pairs={{0,24},{8,0},{16,8},{24,16},{1,25},{9,1},{17,9},{25,17},{2,26},{10... | collective-permute-start | bytes 98312 | tf_op jit(solution)/shard_map/ppermute | solution.py:407
  42.7 5.8 %collective-permute-start.17 = (f32[64,128]{1,0:T(8,128)S(1)}, f32[64,128]{1,0:T(8,128)S(1)}, u32[]{:S(2)}, u32[]{:S(2)}) collective-permute-start(f32[64,128]{1,0:T(8,128)S(1)} %get-tuple-element.101), channel_id=1, source_target_pairs={{0,8},{8,16},{16,24},{24,0},{1,9},{9,17},{17,25},{25,1},{2,10},{10... | collective-permute-start | bytes 98312 | tf_op jit(solution)/shard_map/ppermute | solution.py:407
  42.9 13.3 %collective-permute-start.23 = (bf16[1024,128]{1,0:T(8,128)(2,1)S(1)}, bf16[1024,128]{1,0:T(8,128)(2,1)S(1)}, u32[]{:S(2)}, u32[]{:S(2)}) collective-permute-start(bf16[1024,128]{1,0:T(8,128)(2,1)S(1)} %get-tuple-element.60), channel_id=1, source_target_pairs={{0,2},{2,0},{1,3},{3,1},{4,6},{6,4},{5,7},{7,5},{8,10},{10,8},{9,1... | collective-permute-start | bytes 786440 | tf_op jit(solution)/shard_map/ppermute | solution.py:20
  44.4 11.9 %collective-permute-start.24 = (bf16[1024,128]{1,0:T(8,128)(2,1)S(1)}, bf16[1024,128]{1,0:T(8,128)(2,1)S(1)}, u32[]{:S(2)}, u32[]{:S(2)}) collective-permute-start(bf16[1024,128]{1,0:T(8,128)(2,1)S(1)} %get-tuple-element.61), channel_id=1, source_target_pairs={{0,2},{2,0},{1,3},{3,1},{4,6},{6,4},{5,7},{7,5},{8,10},{10,8},{9,1... | collective-permute-start | bytes 786440 | tf_op jit(solution)/shard_map/ppermute | solution.py:20
  48.9 7.3 %collective-permute-start.20 = (f32[152,128]{1,0:T(8,128)S(1)}, f32[152,128]{1,0:T(8,128)S(1)}, u32[]{:S(2)}, u32[]{:S(2)}) collective-permute-start(f32[152,128]{1,0:T(8,128)S(1)} %constant_dynamic-update-slice_fusion), channel_id=1, source_target_pairs={{0,8},{8,16},{16,24},{24,0},{1,9},{9,17},{17,25},{25,1},{2,10},{10... | collective-permute-start | bytes 233480 | tf_op jit(solution)/shard_map/ppermute | solution.py:407
  56.2 5.7 %collective-permute-start.25 = (f32[4,80,128]{2,1,0:T(8,128)S(1)}, f32[4,80,128]{2,1,0:T(8,128)S(1)}, u32[]{:S(2)}, u32[]{:S(2)}) collective-permute-start(f32[4,80,128]{2,1,0:T(8,128)S(1)} %pad_maximum_fusion.2.refs_0_), channel_id=1, source_target_pairs={{0,2},{2,0},{1,3},{3,1},{4,6},{6,4},{5,7},{7,5},{8,10},{10,8},{9,1... | collective-permute-start | bytes 491528 | tf_op jit(solution)/shard_map/ppermute | solution.py:20
  58.3 8.0 %collective-permute-start.27 = (f32[4,80,128]{2,1,0:T(8,128)S(1)}, f32[4,80,128]{2,1,0:T(8,128)S(1)}, u32[]{:S(2)}, u32[]{:S(2)}) collective-permute-start(f32[4,80,128]{2,1,0:T(8,128)S(1)} %pad_maximum_fusion.2.refs_0_), channel_id=1, source_target_pairs={{0,6},{2,4},{4,2},{6,0},{1,7},{3,5},{5,3},{7,1},{8,14},{10,12},{12... | collective-permute-start | bytes 491528 | tf_op jit(solution)/shard_map/ppermute | solution.py:412
  66.2 8.8 %collective-permute-start.30 = (f32[4,72,128]{2,1,0:T(8,128)S(1)}, f32[4,72,128]{2,1,0:T(8,128)S(1)}, u32[]{:S(2)}, u32[]{:S(2)}) collective-permute-start(f32[4,72,128]{2,1,0:T(8,128)S(1)} %pad_maximum_fusion.5), channel_id=1, source_target_pairs={{0,6},{2,4},{4,2},{6,0},{1,7},{3,5},{5,3},{7,1},{8,14},{10,12},{12... | collective-permute-start | bytes 442376 | tf_op jit(solution)/shard_map/ppermute | solution.py:412
  67.2 7.9 %collective-permute-start.29 = (f32[4,72,128]{2,1,0:T(8,128)S(1)}, f32[4,72,128]{2,1,0:T(8,128)S(1)}, u32[]{:S(2)}, u32[]{:S(2)}) collective-permute-start(f32[4,72,128]{2,1,0:T(8,128)S(1)} %pad_maximum_fusion.5), channel_id=1, source_target_pairs={{0,4},{4,0},{1,5},{5,1},{2,6},{6,2},{3,7},{7,3},{8,12},{12,8},{9,1... | collective-permute-start | bytes 442376 | tf_op jit(solution)/shard_map/ppermute | solution.py:20
  68.7 6.4 %collective-permute-start.28 = (f32[4,72,128]{2,1,0:T(8,128)S(1)}, f32[4,72,128]{2,1,0:T(8,128)S(1)}, u32[]{:S(2)}, u32[]{:S(2)}) collective-permute-start(f32[4,72,128]{2,1,0:T(8,128)S(1)} %pad_maximum_fusion.5), channel_id=1, source_target_pairs={{0,2},{2,0},{1,3},{3,1},{4,6},{6,4},{5,7},{7,5},{8,10},{10,8},{9,1... | collective-permute-start | bytes 442376 | tf_op jit(solution)/shard_map/ppermute | solution.py:20
  83.3 5.9 %collective-permute-start.33 = (f32[512,512]{1,0:T(8,128)S(1)}, f32[512,512]{1,0:T(8,128)S(1)}, u32[]{:S(2)}, u32[]{:S(2)}) collective-permute-start(f32[512,512]{1,0:T(8,128)S(1)} %get-tuple-element.72.own), channel_id=1, source_target_pairs={{0,1},{1,0},{2,3},{3,2},{4,5},{5,4},{6,7},{7,6},{8,9},{9,8},{10,11... | collective-permute-start | bytes 3145736 | tf_op jit(solution)/shard_map/ppermute | solution.py:20
  85.6 7.3 %collective-permute-start.36 = (f32[4,64,128]{2,1,0:T(8,128)S(1)}, f32[4,64,128]{2,1,0:T(8,128)S(1)}, u32[]{:S(2)}, u32[]{:S(2)}) collective-permute-start(f32[4,64,128]{2,1,0:T(8,128)S(1)} %get-tuple-element.79), channel_id=1, source_target_pairs={{0,6},{2,4},{4,2},{6,0},{1,7},{3,5},{5,3},{7,1},{8,14},{10,12},{12... | collective-permute-start | bytes 393224 | tf_op jit(solution)/shard_map/ppermute | solution.py:412
  86.7 7.8 %collective-permute-start.35 = (f32[4,64,128]{2,1,0:T(8,128)S(1)}, f32[4,64,128]{2,1,0:T(8,128)S(1)}, u32[]{:S(2)}, u32[]{:S(2)}) collective-permute-start(f32[4,64,128]{2,1,0:T(8,128)S(1)} %get-tuple-element.78), channel_id=1, source_target_pairs={{0,4},{4,0},{1,5},{5,1},{2,6},{6,2},{3,7},{7,3},{8,12},{12,8},{9,1... | collective-permute-start | bytes 393224 | tf_op jit(solution)/shard_map/ppermute | solution.py:20
  88.2 6.8 %collective-permute-start.34 = (f32[4,64,128]{2,1,0:T(8,128)S(1)}, f32[4,64,128]{2,1,0:T(8,128)S(1)}, u32[]{:S(2)}, u32[]{:S(2)}) collective-permute-start(f32[4,64,128]{2,1,0:T(8,128)S(1)} %get-tuple-element.77), channel_id=1, source_target_pairs={{0,2},{2,0},{1,3},{3,1},{4,6},{6,4},{5,7},{7,5},{8,10},{10,8},{9,1... | collective-permute-start | bytes 393224 | tf_op jit(solution)/shard_map/ppermute | solution.py:20
  95.0 11.8 %collective-permute-start.39 = (f32[4,64,128]{2,1,0:T(8,128)S(1)}, f32[4,64,128]{2,1,0:T(8,128)S(1)}, u32[]{:S(2)}, u32[]{:S(2)}) collective-permute-start(f32[4,64,128]{2,1,0:T(8,128)S(1)} %add_add_fusion.1), channel_id=1, source_target_pairs={{0,24},{8,0},{16,8},{24,16},{1,25},{9,1},{17,9},{25,17},{2,26},{10... | collective-permute-start | bytes 393224 | tf_op jit(solution)/shard_map/ppermute | solution.py:407
  96.4 11.6 %collective-permute-start.38 = (f32[4,64,128]{2,1,0:T(8,128)S(1)}, f32[4,64,128]{2,1,0:T(8,128)S(1)}, u32[]{:S(2)}, u32[]{:S(2)}) collective-permute-start(f32[4,64,128]{2,1,0:T(8,128)S(1)} %add_add_fusion.1), channel_id=1, source_target_pairs={{0,16},{8,24},{16,0},{24,8},{1,17},{9,25},{17,1},{25,9},{2,18},{10... | collective-permute-start | bytes 393224 | tf_op jit(solution)/shard_map/ppermute | solution.py:407
  96.7 11.4 %collective-permute-start.37 = (f32[4,64,128]{2,1,0:T(8,128)S(1)}, f32[4,64,128]{2,1,0:T(8,128)S(1)}, u32[]{:S(2)}, u32[]{:S(2)}) collective-permute-start(f32[4,64,128]{2,1,0:T(8,128)S(1)} %add_add_fusion.1), channel_id=1, source_target_pairs={{0,8},{8,16},{16,24},{24,0},{1,9},{9,17},{17,25},{25,1},{2,10},{10... | collective-permute-start | bytes 393224 | tf_op jit(solution)/shard_map/ppermute | solution.py:407
  106.3 13.1 %collective-permute-start.46 = (bf16[2,512,512]{2,1,0:T(8,128)(2,1)S(1)}, bf16[2,512,512]{2,1,0:T(8,128)(2,1)S(1)}, u32[]{:S(2)}, u32[]{:S(2)}) collective-permute-start(bf16[2,512,512]{2,1,0:T(8,128)(2,1)S(1)} %shard_map.49.inv), channel_id=1, source_target_pairs={{0,1},{1,0},{2,3},{3,2},{4,5},{5,4},{6,7},{7,6},{8,9},{9,8},{10,11... | collective-permute-start | bytes 3145736 | tf_op jit(solution)/shard_map/ppermute | solution.py:20
  108.1 7.2 %collective-permute-start.42 = (f32[4,64,128]{2,1,0:T(8,128)S(1)}, f32[4,64,128]{2,1,0:T(8,128)S(1)}, u32[]{:S(2)}, u32[]{:S(2)}) collective-permute-start(f32[4,64,128]{2,1,0:T(8,128)S(1)} %add_add_fusion), channel_id=1, source_target_pairs={{0,6},{2,4},{4,2},{6,0},{1,7},{3,5},{5,3},{7,1},{8,14},{10,12},{12... | collective-permute-start | bytes 393224 | tf_op jit(solution)/shard_map/ppermute | solution.py:412
  109.8 7.5 %collective-permute-start.41 = (f32[4,64,128]{2,1,0:T(8,128)S(1)}, f32[4,64,128]{2,1,0:T(8,128)S(1)}, u32[]{:S(2)}, u32[]{:S(2)}) collective-permute-start(f32[4,64,128]{2,1,0:T(8,128)S(1)} %add_add_fusion), channel_id=1, source_target_pairs={{0,4},{4,0},{1,5},{5,1},{2,6},{6,2},{3,7},{7,3},{8,12},{12,8},{9,1... | collective-permute-start | bytes 393224 | tf_op jit(solution)/shard_map/ppermute | solution.py:20
  111.5 5.8 %collective-permute-start.40 = (f32[4,64,128]{2,1,0:T(8,128)S(1)}, f32[4,64,128]{2,1,0:T(8,128)S(1)}, u32[]{:S(2)}, u32[]{:S(2)}) collective-permute-start(f32[4,64,128]{2,1,0:T(8,128)S(1)} %add_add_fusion), channel_id=1, source_target_pairs={{0,2},{2,0},{1,3},{3,1},{4,6},{6,4},{5,7},{7,5},{8,10},{10,8},{9,1... | collective-permute-start | bytes 393224 | tf_op jit(solution)/shard_map/ppermute | solution.py:20
  (17 other events, 72.6 us)

commit v4 on v3

--- a/solution.py
+++ b/solution.py
@@ -29,12 +29,12 @@
     return lax.optimization_barrier((value,) + others)[0]
 
 
-def call(body, shapes, scratch, flops, *args):
+def call(body, shapes, scratch, flops, *args, outside=0):
     size = sum(a.size * a.dtype.itemsize for a in args) + sum(s.size * s.dtype.itemsize for s in shapes)
     return pl.pallas_call(
         body,
         out_shape=shapes,
-        in_specs=[VMEM] * len(args),
+        in_specs=[pl.BlockSpec(memory_space=pltpu.HBM)] * outside + [VMEM] * (len(args) - outside),
         out_specs=[VMEM] * len(shapes),
         scratch_shapes=scratch,
         compiler_params=pltpu.CompilerParams(vmem_limit_bytes=16 << 20),
@@ -101,7 +101,7 @@
     for i, out in enumerate(outs):
         for k in range(depth):
             part = (lax.rem(z + k, depth) if turned else k) * len(outs) + ((x * 2 + y if len(outs) == 4 else x) ^ i)
-            out[k, start : start + each] = flat[at(part, each)]
+            out[k, start : start + each] = flat[at(part, each)].astype(out.dtype)
 
 
 def sources(depth, turned=True):
@@ -121,25 +121,31 @@
 
 def steps(first, last, errors, highs, lows, its, ihighs, ilows, finish):
     channels = errors.shape[1]
-    step = channels // 2
+    half = channels // 2
+    top, left, right = slice(0, half), slice(0, half), slice(half, channels)
     for n in range(first, last):
         now, later = n % 2, (n + 1) % 2
-        for r in range(0, channels, step):
-            rows = pl.ds(r, step)
-            high, low = highs[now, rows], lows[now, rows]
-            if n < NSTEPS - 1:
-                value = dot(high, highs[now]) + dot(high, lows[now]) + dot(low, highs[now])
-                value = 2.0 * errors[now, rows] - value
-                errors[later, rows] = value
-                highs[later, rows], lows[later, rows] = halves(value)
-            if n >= 1:
-                value = dot(high, ihighs[now]) + dot(high, ilows[now]) + dot(low, ihighs[now])
-                value = 2.0 * its[now, rows] - value
-                if n == NSTEPS - 1:
-                    finish(rows, value)
-                else:
-                    its[later, rows] = value
-                    ihighs[later, rows], ilows[later, rows] = halves(value)
+
+        def store(table, high, low, rows, cols, value):
+            if n == NSTEPS - 1:
+                finish(rows, cols, value)
+            else:
+                table[later, rows, cols] = value
+                high[later, rows, cols], low[later, rows, cols] = halves(value)
+
+        def advance(table, high, low):
+            for rows, cols in ((top, slice(0, channels)), (right, right)):
+                ahigh, alow = highs[now, rows], lows[now, rows]
+                bhigh, blow = high[now, :, cols], low[now, :, cols]
+                value = 2.0 * table[now, rows, cols] - (dot(ahigh, bhigh) + dot(ahigh, blow) + dot(alow, bhigh))
+                store(table, high, low, rows, cols, value)
+                if rows == top:
+                    store(table, high, low, right, left, value[:, half:].T)
+
+        if n < NSTEPS - 1:
+            advance(errors, highs, lows)
+        if n >= 1:
+            advance(its, ihighs, ilows)
 
 
 def put(table, high, low, slot, rows, cols, value):
@@ -167,10 +173,40 @@
     out[...] = (late + dot_last(edge[0], refl[1])).astype(BF16)
 
 
+def copy_all(pairs, sems):
+    copies = [pltpu.make_async_copy(source, target, sems.at[i]) for i, (source, target) in enumerate(pairs)]
+    for copy in copies:
+        copy.start()
+    for copy in copies:
+        copy.wait()
+
+
+def cut_kernel(forward, backward, send, tail, sems):
+    half, end = send.shape[0], forward.shape[0]
+    last = pl.ds(end - 16, 16)
+    pairs = [(forward.at[at(1 - lax.axis_index("y"), half)], send)]
+    copy_all(pairs + [(forward.at[last], tail.at[0]), (backward.at[last], tail.at[1])], sems)
+
+
+def front_kernel(forward, backward, halo, send, sems):
+    half = forward.shape[0] // 2
+    ahead = pl.ds(half - 16, 16)
+    pairs = [
+        (backward.at[at(1 - lax.axis_index("y"), half)], send.at[pl.ds(64, half)]),
+        (forward.at[ahead], send.at[pl.ds(32, 16)]),
+        (backward.at[ahead], send.at[pl.ds(48, 16)]),
+    ]
+    send[0:16], send[16:32] = halo[0], halo[1]
+    copy_all(pairs, sems)
+
+
 def near_kernel(width, pd, xd, forward, backward, forward_core, backward_core, halo, halo_core, *refs):
-    packed, (chosen, behind, late, edge, flat) = refs[:2], refs[2:]
+    packed, back = refs[:2], refs[2]
+    chosen, behind, late, edge, flat = refs[3:]
     core = lax.axis_index("core")
     own, other = at(core, width), at(1 - core, width)
+    rows = at(lax.axis_index("y"), back.shape[1])
+    back[0], back[1] = forward[rows], backward[rows]
     behind[:, own], behind[:, other] = backward[...], backward_core[...]
     edge[:, own], edge[:, other] = halo[1], halo_core[1]
 
@@ -192,8 +228,8 @@
 
 
 def far_kernel(width, po, xo, *refs):
-    own, across, halos = (refs[0:2], refs[2:4]), (refs[4:6], refs[6:8]), refs[8:12]
-    (here, edges, shifted), packed, (tails, samples, flat) = refs[12:15], refs[15:19], refs[19:]
+    own, across, halos = (refs[0:2], refs[2:4]), (refs[4:6], refs[6:8]), refs[8:10]
+    (here, edges, shifted), packed, (tails, samples, flat) = refs[10:13], refs[13:17], refs[17:]
     y, core = lax.axis_index("y"), lax.axis_index("core")
     half = here.shape[1]
     pair = 2 * width
@@ -203,10 +239,11 @@
         over = at((1 - y) * 2 + (core ^ c), width)
         for kind in range(2):
             here[kind, :, mine] = own[c][kind][rows]
-            here[kind, :, over] = across[c][kind][...]
+            here[kind, :, over] = across[c][kind][64 * kind :]
+            edges[0, kind, :, mine] = halos[c][kind]
             edges[1, kind, :, mine] = own[c][kind][half - 16 : half]
-        edges[0, :, :, mine] = halos[c][...]
-        edges[:, :, :, over] = halos[2 + c][...]
+            for e in range(2):
+                edges[e, kind, :, over] = across[c][1][e * 32 + kind * 16 : e * 32 + kind * 16 + 16]
     samples[...] = here[core]
     drop_end(samples, lax.axis_index(PARTS) == lax.axis_size(PARTS) - 1)
     value = dot_first(samples[:, :pair], samples[:, pair:])
@@ -289,8 +326,8 @@
 
 
 def there_kernel(width, *refs):
-    own, across, (edges, ours, theirs) = (refs[0:2], refs[2:4]), (refs[4:6], refs[6:8]), refs[8:11]
-    out, late, refl, raw, shifted, ahead = refs[11:]
+    own, across, (edges, ours, theirs) = (refs[0:2], refs[2:4]), refs[4:6], refs[6:9]
+    out, late, refl, raw, shifted, ahead = refs[9:]
     y, core = lax.axis_index("y"), lax.axis_index("core")
     by_kind(ours, theirs, refl)
     edge = edges.at[1 - y]
@@ -298,7 +335,7 @@
     for c in range(2):
         for kind in range(2):
             raw[kind, :, at(y * 2 + (core ^ c), width)] = own[c][kind][rows]
-            raw[kind, :, at((1 - y) * 2 + (core ^ c), width)] = across[c][kind][...]
+            raw[kind, :, at((1 - y) * 2 + (core ^ c), width)] = across[c][kind]
     delay(raw.at[1], edge.at[1], shifted)
     update_edge(edge, refl, ahead)
     update(raw, shifted, refl, out)
@@ -362,23 +399,25 @@
     put(its, ihighs, ilows, start % 2, every, every, iterate[...])
     factor = scale[0:1, 0:1]
 
-    def finish(rows, value):
-        out[0, rows], out[1, rows] = halves(value * factor)
+    def finish(rows, cols, value):
+        out[0, rows, cols], out[1, rows, cols] = halves(value * factor)
 
     steps(start, NSTEPS, *tables, finish)
 
 
-def last_kernel(width, ours, theirs, inv, inv_core, here, shifted, there, there_shifted, forward, backward, flat, high, low):
+def last_kernel(width, ours, theirs, inv, inv_core, here, shifted, there, there_shifted, forward, backward, flat, rows_of, cols_of):
     y, core = lax.axis_index("y"), lax.axis_index("core")
     channels = here.shape[2]
     half, depth, each = channels // 2, ours.shape[1], ours.shape[2]
     for gathered, home in ((ours, core), (theirs, 1 - core)):
         for i, k, zx, ys in sources(depth, turned=False):
-            flat[at(zx * 2 + ys, each)] = gathered[i, k]
-        rows = at(home, half)
-        for j in range(channels // LANES):
-            cols = pl.ds(j * LANES, LANES)
-            high[rows, cols], low[rows, cols] = halves(flat[j * half : (j + 1) * half])
+            flat[home, at(zx * 2 + ys, each)] = gathered[i, k]
+    for n in range(channels // LANES):
+        value = flat[y, at(2 * n + core, width)]
+        rows_of[0, :, n * LANES : (n + 1) * LANES], rows_of[1, :, n * LANES : (n + 1) * LANES] = halves(value)
+    for home in range(2):
+        value = flat[home, at(y * 2 + core, half)]
+        cols_of[0, home * half : (home + 1) * half], cols_of[1, home * half : (home + 1) * half] = halves(value)
     mine = at(y * 2 + core, width)
 
     def reflect(lefts, rights, product):
@@ -386,8 +425,8 @@
         return (-value).astype(BF16)
 
     def final(of_fwd, of_bwd):
-        left = reflect((high[mine], low[mine]), (of_bwd[0], of_bwd[1]), dot)
-        right = reflect((high[:, mine], low[:, mine]), (of_fwd[0], of_fwd[1]), dot_first)
+        left = reflect((rows_of[0], rows_of[1]), (of_bwd[0], of_bwd[1]), dot)
+        right = reflect((cols_of[0], cols_of[1]), (of_fwd[0], of_fwd[1]), dot_first)
         for time, both, late in ((y, here, shifted), (1 - y, there, there_shifted)):
             rows = at(time, here.shape[1])
             forward[rows] = (both[0, :, mine].astype(F32) + dot_last(late[...], left)).astype(BF16)
@@ -446,22 +485,29 @@
     kernel = functools.partial
 
     own = (fwd_in, bwd_in)
-    cut = lambda which: [lax.dynamic_slice_in_dim(a, which * half, half, 0) for a in own]
-    across = [swap(a, "y") for a in cut(1 - y)]
-    tail = lambda end: jnp.stack([a[end - 16 : end] for a in own])
-    halo = from_behind(tail(samples), zx)
+    send, tail = call(
+        cut_kernel,
+        [shape((half, width), BF16), shape((2, 16, width), BF16)],
+        [pltpu.SemaphoreType.DMA((3,))],
+        0,
+        *own,
+        outside=2,
+    )
+    halo = from_behind(tail, zx)
+    (front,) = call(
+        front_kernel, [shape((64 + half, width), BF16)], [pltpu.SemaphoreType.DMA((3,))], 0, *own, halo, outside=2
+    )
+    across = [swap(send, "y"), swap(front, "y")]
     own_core = [swap(a, "core") for a in own]
     halo_core = swap(halo, "core")
-    halo_y = swap(jnp.stack([halo, tail(half)]), "y")
-    near = call(
+    *near, back = call(
         kernel(near_kernel, width, pd, xd),
-        [shape((depth, pd + xd, LANES), F32)] * 2,
+        [shape((depth, pd + xd, LANES), F32)] * 2 + [shape((2, half, width), BF16)],
         [pltpu.VMEM((samples, pair), BF16)] * 3 + [pltpu.VMEM((16, pair), BF16), flat(near_parts * pd, near_parts * xd)],
         3 * samples * pair * pair,
-        *own, *own_core, halo, halo_core,
+        *own, *own_core, halo, after(halo_core, across[0]),
     )
     near_x = swap(near[1], "x")
-    halo_y_core = swap(after(halo_y, near[1]), "core")
     across_core = [swap(across[0], "core"), swap(after(across[1], near[1]), "core")]
     here, edges, shifted, *far, tails = call(
         kernel(far_kernel, width, po, xo),
@@ -474,16 +520,15 @@
         ],
         [pltpu.VMEM((half, channels), BF16), flat(parts * po, parts * xo)],
         4 * half * pair * pair,
-        *own, *own_core, *across, *across_core, halo, halo_core, halo_y, halo_y_core,
-    )
-    near_sum = scatter_z([after(near[0], far[0]), near_x])
+        *own, *own_core, *across, *across_core, halo, halo_core,
+    )
     swapped = exchange(far)
-    swapped[0] = after(swapped[0], near_sum)
-    across2 = [swap(after(a, swapped[1]), "y") for a in cut(y)]
+    near_sum = scatter_z([near[0], after(near_x, swapped[1])])
+    across2 = swap(after(back, swapped[1]), "y")
     far_sum = scatter_z(swapped)
     chunk = jnp.concatenate([near_sum[:pd], far_sum[:po], near_sum[pd:], far_sum[po:], tails])
     column = z_gather(chunk)
-    pieces = xy_gather(after(column[:, : pd + po], *across2))
+    pieces = xy_gather(after(column[:, : pd + po], across2))
     stop = NSTEPS // 2
     state = [shape((channels, channels), F32)] * 2 + [shape((8, LANES), F32)]
     full, error, iterate, scale = call(
@@ -493,7 +538,7 @@
         30 * channels**3,
         *pieces,
     )
-    ours = jnp.stack(xy_gather(after(column[:, pd + po :], *pieces)))
+    ours = jnp.stack(xy_gather(after(column[:, pd + po :], pieces[1])))
     theirs = swap(after(ours, error), "core")
     finish = lambda *args: call(
         kernel(finish_kernel, stop), [shape((2, channels, channels), BF16)], tables, 30 * channels**3, *args
@@ -509,12 +554,12 @@
     refl_core = swap(refl, "core")
     here2, shifted2, *packed = call(
         kernel(update_cross_kernel, each),
-        [shape((2, half, channels), BF16), shape((half, channels), BF16)] + [shape((depth, each, LANES), F32)] * 4,
+        [shape((2, half, channels), BF16), shape((half, channels), BF16)] + [shape((depth, each, LANES), BF16)] * 4,
         [square16(2), pltpu.VMEM((16, channels), BF16), flat(parts * each)],
         5 * half * channels * channels,
         here, shifted, edges, refl, refl_core,
     )
-    across2_core = [swap(a, "core") for a in across2]
+    across2_core = swap(across2, "core")
     full_core = swap(after(full, refl_core), "core")
     matrix2, scale2 = call(
         predict_kernel,
@@ -528,7 +573,8 @@
     )
     swapped = exchange(packed)
     swapped[0] = after(swapped[0], matrix2)
-    column2 = jnp.sum(z_gather(sum(swapped[1:], swapped[0])), axis=0)
+    wide = lambda pieces: sum((p.astype(F32) for p in pieces[1:]), pieces[0].astype(F32))
+    column2 = wide(z_gather(wide(swapped).astype(BF16)))
     inv2 = finish(error2, iterate2, scale2)
     inv2_core = swap(inv2, "core")
     there2, there_shifted2 = call(
@@ -536,14 +582,14 @@
         [shape((2, half, channels), BF16), shape((half, channels), BF16)],
         [square16(2), pltpu.VMEM((2, half, channels), BF16), pltpu.VMEM((half, channels), BF16), pltpu.VMEM((16, channels), BF16)],
         4 * half * channels * channels,
-        *own, *own_core, *across2, *across2_core, edges, refl, after(refl_core, column2),
+        *own, *own_core, across2, across2_core, edges, refl, after(refl_core, column2),
     )
     ours2 = jnp.stack(xy_gather(after(column2, inv2)))
     theirs2 = swap(after(ours2, there2), "core")
     return call(
         kernel(last_kernel, width),
         [shape((samples, width), BF16)] * 2,
-        [flat(parts * each), square16(), square16()],
+        [pltpu.VMEM((2, parts * each, LANES), F32), pltpu.VMEM((2, width, channels), BF16), pltpu.VMEM((2, channels, width), BF16)],
         4 * samples * channels * width,
         ours2, theirs2, inv2, inv2_core, here2, shifted2, there2, there_shifted2,
     )

time: 122 us -> 114 us (0.934)
  waiting for transfers between devices: 40.4 us -> 36.1 us
  Pallas kernels: 33.2 us -> 30 us
  starting transfers between devices: 45.3 us -> 44 us
    ppermute x5, waiting for transfers between devices: 7.54 us -> 2.58 us  [exchange(): lax.ppermute(pieces[3], ('x', 'y'), both)]
    pallas_call x11 -> x13, Pallas kernels: 33.2 us -> 30 us  [call(): pl.pallas_call(body, out_shape=shapes, in_specs=[pl.BlockSpec(memory_spac...]
    ppermute x29 -> x25, starting transfers between devices: 21.5 us -> 18.7 us  [swap(): return lax.ppermute(value, axis, [(0, 1), (1, 0)])]
    dynamic_slice x2 -> x0, local copies, waits for them, and re-layouts: 2.13 us -> none  [local(): lax.dynamic_slice_in_dim(a, which * half, half, 0)]
    unnamed x8 -> x12, local copies, waits for them, and re-layouts: 0.02 us -> 2.11 us
    ppermute x29 -> x25, waiting for transfers between devices: 20.1 us -> 21.2 us  [swap(): return lax.ppermute(value, axis, [(0, 1), (1, 0)])]
  transfers between devices with their start and end apart: 47 -> 43, of which waited for: 27 -> 20; matrix products, arithmetic and copies ran while one was open for 2% -> 0% of each run, Pallas kernels for 24% -> 23%
where the time goes in v4:
time: 114 us
  starting transfers between devices  44 us (39%)
  waiting for transfers between devices  36.1 us (32%)
  Pallas kernels  30 us (26%)
  local copies, waits for them, and re-layouts  2.13 us (2%)
    pallas_call x13, Pallas kernels, call(): pl.pallas_call(body, out_shape=shapes, in_specs=[pl.BlockSpec(memory_spac...  30 us
    ppermute x25, waiting for transfers between devices, swap(): return lax.ppermute(value, axis, [(0, 1), (1, 0)])  21.2 us
    ppermute x25, starting transfers between devices, swap(): return lax.ppermute(value, axis, [(0, 1), (1, 0)])  18.7 us
    ppermute x12, starting transfers between devices, ahead(): return lax.ppermute(piece, 'z', [(i, (i + by) % size) for i in range(size)])  14.3 us
    ppermute x12, waiting for transfers between devices, ahead(): return lax.ppermute(piece, 'z', [(i, (i + by) % size) for i in range(size)])  11 us
    ppermute x5, starting transfers between devices, exchange(): lax.ppermute(pieces[3], ('x', 'y'), both)  7.69 us
    ppermute x1, starting transfers between devices, from_behind(): return lax.ppermute(value, axes, [(i, i + 1) for i in range(devices - 1)])  3.38 us
    ppermute x5, waiting for transfers between devices, exchange(): lax.ppermute(pieces[3], ('x', 'y'), both)  2.58 us
  transfers between devices with their start and end apart: 43, of which 20 were waited for; matrix products, arithmetic and copies ran while one was open for 0% of the time, Pallas kernels for 23%

profile of v4, /device:TPU:0, one launch (start us, length us, event | category | flops | bytes accessed | tf_op | source)
XLA Modules:
  0.0 113.6 jit_solution(10935285144556829269)
XLA Ops:
  3.4 3.0 %collective-permute-start.2 = (bf16[1024,128]{1,0:T(8,128)(2,1)S(1)}, bf16[1024,128]{1,0:T(8,128)(2,1)S(1)}, u32[]{:S(2)}, u32[]{:S(2)}) collective-permute-start(bf16[1024,128]{1,0:T(8,128)(2,1)S(1)} %get-tuple-element.47), channel_id=1, source_target_pairs={{0,2},{2,0},{1,3},{3,1},{4,6},{6,4},{5,7},{7,5},{8,10},{10,8},{9,1... | collective-permute-start | bytes 786440 | tf_op jit(solution)/shard_map/ppermute | solution.py:20
  6.4 3.4 %collective-permute-start.3 = (bf16[2,16,128]{2,1,0:T(8,128)(2,1)S(1)}, bf16[2,16,128]{2,1,0:T(8,128)(2,1)S(1)}, u32[]{:S(2)}, u32[]{:S(2)}) collective-permute-start(bf16[2,16,128]{2,1,0:T(8,128)(2,1)S(1)} %get-tuple-element.48), channel_id=1, source_target_pairs={{0,4},{4,8},{8,12},{12,16},{16,20},{20,24},{24,28},{1,5},{5,9},{9,... | collective-permute-start | bytes 24584 | tf_op jit(solution)/shard_map/ppermute | solution.py:25
  14.2 4.7 %collective-permute-done.4.refs_5_ = bf16[1088,128]{1,0:T(8,128)(2,1)S(1)} collective-permute-done((bf16[1088,128]{1,0:T(8,128)(2,1)S(1)}, bf16[1088,128]{1,0:T(8,128)(2,1)S(1)}, u32[]{:S(2)}, u32[]{:S(2)}) %collective-permute-start.4) | collective-permute-done | bytes 278560 | tf_op jit(solution)/shard_map/ppermute | solution.py:20
  19.4 2.1 %collective-permute-start.8 = (f32[4,80,128]{2,1,0:T(8,128)S(1)}, f32[4,80,128]{2,1,0:T(8,128)S(1)}, u32[]{:S(2)}, u32[]{:S(2)}) collective-permute-start(f32[4,80,128]{2,1,0:T(8,128)S(1)} %get-tuple-element.50), channel_id=1, source_target_pairs={{0,4},{4,0},{1,5},{5,1},{2,6},{6,2},{3,7},{7,3},{8,12},{12,8},{9,1... | collective-permute-start | bytes 491528 | tf_op jit(solution)/shard_map/ppermute | solution.py:20
  24.0 1.8 %collective-permute-start.14 = (f32[4,64,128]{2,1,0:T(8,128)S(1)}, f32[4,64,128]{2,1,0:T(8,128)S(1)}, u32[]{:S(2)}, u32[]{:S(2)}) collective-permute-start(f32[4,64,128]{2,1,0:T(8,128)S(1)} %get-tuple-element.60), channel_id=1, source_target_pairs={{0,6},{2,4},{4,2},{6,0},{1,7},{3,5},{5,3},{7,1},{8,14},{10,12},{12... | collective-permute-start | bytes 393224 | tf_op jit(solution)/shard_map/ppermute | solution.py:451
  26.4 4.0 %collective-permute-done.9 = f32[4,64,128]{2,1,0:T(8,128)S(1)} collective-permute-done((f32[4,64,128]{2,1,0:T(8,128)S(1)}, f32[4,64,128]{2,1,0:T(8,128)S(1)}, u32[]{:S(2)}, u32[]{:S(2)}) %collective-permute-start.9) | collective-permute-done | bytes 131104 | tf_op jit(solution)/shard_map/ppermute | solution.py:20
  32.2 4.5 %collective-permute-start.17 = (f32[64,128]{1,0:T(8,128)S(1)}, f32[64,128]{1,0:T(8,128)S(1)}, u32[]{:S(2)}, u32[]{:S(2)}) collective-permute-start(f32[64,128]{1,0:T(8,128)S(1)} %get-tuple-element.96), channel_id=1, source_target_pairs={{0,24},{8,0},{16,8},{24,16},{1,25},{9,1},{17,9},{25,17},{2,26},{10... | collective-permute-start | bytes 98312 | tf_op jit(solution)/shard_map/ppermute | solution.py:446
  37.7 2.9 %collective-permute-start.12 = (f32[80,128]{1,0:T(8,128)S(1)}, f32[80,128]{1,0:T(8,128)S(1)}, u32[]{:S(2)}, u32[]{:S(2)}) collective-permute-start(f32[80,128]{1,0:T(8,128)S(1)} %get-tuple-element.93), channel_id=1, source_target_pairs={{0,24},{8,0},{16,8},{24,16},{1,25},{9,1},{17,9},{25,17},{2,26},{10... | collective-permute-start | bytes 122888 | tf_op jit(solution)/shard_map/ppermute | solution.py:446
  43.0 2.7 %collective-permute-done.11 = f32[80,128]{1,0:T(8,128)S(1)} collective-permute-done((f32[80,128]{1,0:T(8,128)S(1)}, f32[80,128]{1,0:T(8,128)S(1)}, u32[]{:S(2)}, u32[]{:S(2)}) %collective-permute-start.11) | collective-permute-done | bytes 40992 | tf_op jit(solution)/shard_map/ppermute | solution.py:446
  45.7 2.0 %collective-permute-done.10 = f32[80,128]{1,0:T(8,128)S(1)} collective-permute-done((f32[80,128]{1,0:T(8,128)S(1)}, f32[80,128]{1,0:T(8,128)S(1)}, u32[]{:S(2)}, u32[]{:S(2)}) %collective-permute-start.10) | collective-permute-done | bytes 40992 | tf_op jit(solution)/shard_map/ppermute | solution.py:446
  47.9 1.9 %collective-permute-start.18 = (f32[152,128]{1,0:T(8,128)S(1)}, f32[152,128]{1,0:T(8,128)S(1)}, u32[]{:S(2)}, u32[]{:S(2)}) collective-permute-start(f32[152,128]{1,0:T(8,128)S(1)} %constant_dynamic-update-slice_fusion), channel_id=1, source_target_pairs={{0,8},{8,16},{16,24},{24,0},{1,9},{9,17},{17,25},{25,1},{2,10},{10... | collective-permute-start | bytes 233480 | tf_op jit(solution)/shard_map/ppermute | solution.py:446
  49.9 2.4 %collective-permute-done.20 = f32[152,128]{1,0:T(8,128)S(1)} collective-permute-done((f32[152,128]{1,0:T(8,128)S(1)}, f32[152,128]{1,0:T(8,128)S(1)}, u32[]{:S(2)}, u32[]{:S(2)}) %collective-permute-start.20) | collective-permute-done | bytes 77856 | tf_op jit(solution)/shard_map/ppermute | solution.py:446
  53.2 2.2 %collective-permute-done.18 = f32[152,128]{1,0:T(8,128)S(1)} collective-permute-done((f32[152,128]{1,0:T(8,128)S(1)}, f32[152,128]{1,0:T(8,128)S(1)}, u32[]{:S(2)}, u32[]{:S(2)}) %collective-permute-start.18) | collective-permute-done | bytes 77856 | tf_op jit(solution)/shard_map/ppermute | solution.py:446
  56.0 1.5 %collective-permute-start.26 = (f32[4,80,128]{2,1,0:T(8,128)S(1)}, f32[4,80,128]{2,1,0:T(8,128)S(1)}, u32[]{:S(2)}, u32[]{:S(2)}) collective-permute-start(f32[4,80,128]{2,1,0:T(8,128)S(1)} %pad_maximum_fusion.2.refs_0_), channel_id=1, source_target_pairs={{0,4},{4,0},{1,5},{5,1},{2,6},{6,2},{3,7},{7,3},{8,12},{12,8},{9,1... | collective-permute-start | bytes 491528 | tf_op jit(solution)/shard_map/ppermute | solution.py:20
  57.5 1.5 %collective-permute-start.27 = (f32[4,80,128]{2,1,0:T(8,128)S(1)}, f32[4,80,128]{2,1,0:T(8,128)S(1)}, u32[]{:S(2)}, u32[]{:S(2)}) collective-permute-start(f32[4,80,128]{2,1,0:T(8,128)S(1)} %pad_maximum_fusion.2.refs_0_), channel_id=1, source_target_pairs={{0,6},{2,4},{4,2},{6,0},{1,7},{3,5},{5,3},{7,1},{8,14},{10,12},{12... | collective-permute-start | bytes 491528 | tf_op jit(solution)/shard_map/ppermute | solution.py:451
  59.0 4.6 %collective-permute-done.22.refs_1_ = f32[4,80,128]{2,1,0:T(8,128)S(1)} collective-permute-done((f32[4,80,128]{2,1,0:T(8,128)S(1)}, f32[4,80,128]{2,1,0:T(8,128)S(1)}, u32[]{:S(2)}, u32[]{:S(2)}) %collective-permute-start.22) | collective-permute-done | bytes 163872 | tf_op jit(solution)/shard_map/ppermute | solution.py:20
  63.6 1.4 %collective-permute-start.25 = (f32[4,72,128]{2,1,0:T(8,128)S(1)}, f32[4,72,128]{2,1,0:T(8,128)S(1)}, u32[]{:S(2)}, u32[]{:S(2)}) collective-permute-start(f32[4,72,128]{2,1,0:T(8,128)S(1)} %pad_maximum_fusion.5), channel_id=1, source_target_pairs={{0,6},{2,4},{4,2},{6,0},{1,7},{3,5},{5,3},{7,1},{8,14},{10,12},{12... | collective-permute-start | bytes 442376 | tf_op jit(solution)/shard_map/ppermute | solution.py:451
  65.5 1.6 %collective-permute-start.23 = (f32[4,72,128]{2,1,0:T(8,128)S(1)}, f32[4,72,128]{2,1,0:T(8,128)S(1)}, u32[]{:S(2)}, u32[]{:S(2)}) collective-permute-start(f32[4,72,128]{2,1,0:T(8,128)S(1)} %pad_maximum_fusion.5), channel_id=1, source_target_pairs={{0,2},{2,0},{1,3},{3,1},{4,6},{6,4},{5,7},{7,5},{8,10},{10,8},{9,1... | collective-permute-start | bytes 442376 | tf_op jit(solution)/shard_map/ppermute | solution.py:20
  67.1 4.3 %shard_map.45 = (f32[512,512]{1,0:T(8,128)S(1)}, f32[512,512]{1,0:T(8,128)S(1)}, f32[512,512]{1,0:T(8,128)S(1)}, f32[8,128]{1,0:T(8,128)S(1)}) custom-call(f32[4,80,128]{2,1,0:T(8,128)S(1)} %pad_maximum_fusion.2.refs_0_, f32[4,80,128]{2,1,0:T(8,128)S(1)} %collective-permute-done.22.refs_1_, f32[4,80,128]{2,1,0:T(8,128)S(1)} %collective-permute-done.26.refs_2_, ...), custom_call_target="tpu_custom_call" | custom-call | flops 4026531840 | bytes 3805184 | tf_op jit(solution)/shard_map/pallas_call | solution.py:34
  71.6 3.9 %shard_map.46.inv = bf16[2,512,512]{2,1,0:T(8,128)(2,1)S(1)} custom-call(f32[512,512]{1,0:T(8,128)S(1)} %get-tuple-element.66.error, f32[512,512]{1,0:T(8,128)S(1)} %get-tuple-element.68.iterate, f32[8,128]{1,0:T(8,128)S(1)} %get-tuple-element.69.scale), custom_call_target="tpu_custom_call" | custom-call | flops 4026531840 | bytes 3149824 | tf_op jit(solution)/shard_map/pallas_call | solution.py:34
  77.4 1.5 %collective-permute-done.29.theirs.refs_8_ = bf16[512,512]{1,0:T(8,128)(2,1)S(1)} collective-permute-done((bf16[512,512]{1,0:T(8,128)(2,1)S(1)}, bf16[512,512]{1,0:T(8,128)(2,1)S(1)}, u32[]{:S(2)}, u32[]{:S(2)}) %collective-permute-start.29) | collective-permute-done | bytes 524320 | tf_op jit(solution)/shard_map/ppermute | solution.py:20
  79.5 2.0 %shard_map.48 = (bf16[2,1024,512]{2,1,0:T(8,128)(2,1)S(1)}, bf16[1024,512]{1,0:T(8,128)(2,1)S(1)}, bf16[4,64,128]{2,1,0:T(8,128)(2,1)S(1)}, bf16[4,64,128]{2,1,0...) custom-call(bf16[2,1024,512]{2,1,0:T(8,128)(2,1)S(1)} %get-tuple-element.52.here, ...), custom_call_target="tpu_custom_call" | custom-call | flops 1342177280 | bytes 7667712 | tf_op jit(solution)/shard_map/pallas_call | solution.py:34
  81.5 1.5 %collective-permute-start.33 = (bf16[4,64,128]{2,1,0:T(8,128)(2,1)S(1)}, bf16[4,64,128]{2,1,0:T(8,128)(2,1)S(1)}, u32[]{:S(2)}, u32[]{:S(2)}) collective-permute-start(bf16[4,64,128]{2,1,0:T(8,128)(2,1)S(1)} %get-tuple-element.81), channel_id=1, source_target_pairs={{0,6},{2,4},{4,2},{6,0},{1,7},{3,5},{5,3},{7,1},{8,14},{10,12},{12... | collective-permute-start | bytes 196616 | tf_op jit(solution)/shard_map/ppermute | solution.py:451
  85.1 3.4 %shard_map.49 = (f32[512,512]{1,0:T(8,128)S(1)}, f32[8,128]{1,0:T(8,128)S(1)}) custom-call(f32[512,512]{1,0:T(8,128)S(1)} %get-tuple-element.74.own, f32[512,512]{1,0:T(8,128)S(1)} %collective-permute-done.30.other, f32[512,512]{1,0:T(8,128)S(1)} %get-tuple-element.75.cross, bf16[512,512]{1,0:T(8,128)(2,1)S(1)} %collective-permute-done.29.theirs.refs_8_, ...), custom_call_target="tpu_custom_call" | custom-call | flops 2415919104 | bytes 4726784 | tf_op jit(solution)/shard_map/pallas_call | solution.py:34
  88.6 2.0 %collective-permute-start.36 = (bf16[4,64,128]{2,1,0:T(8,128)(2,1)S(1)}, bf16[4,64,128]{2,1,0:T(8,128)(2,1)S(1)}, u32[]{:S(2)}, u32[]{:S(2)}) collective-permute-start(bf16[4,64,128]{2,1,0:T(8,128)(2,1)S(1)} %add_convert_fusion), channel_id=1, source_target_pairs={{0,24},{8,0},{16,8},{24,16},{1,25},{9,1},{17,9},{25,17},{2,26},{10... | collective-permute-start | bytes 196616 | tf_op jit(solution)/shard_map/ppermute | solution.py:446
  91.3 3.6 %shard_map.50 = (f32[512,512]{1,0:T(8,128)S(1)}, f32[512,512]{1,0:T(8,128)S(1)}) custom-call(f32[512,512]{1,0:T(8,128)S(1)} %get-tuple-element.77.matrix, f32[8,128]{1,0:T(8,128)S(1)} %get-tuple-element.82.scale), custom_call_target="tpu_custom_call" | custom-call | flops 4026531840 | bytes 3149824 | tf_op jit(solution)/shard_map/pallas_call | solution.py:34
  94.8 3.8 %shard_map.51.inv = bf16[2,512,512]{2,1,0:T(8,128)(2,1)S(1)} custom-call(f32[512,512]{1,0:T(8,128)S(1)} %get-tuple-element.83.error, f32[512,512]{1,0:T(8,128)S(1)} %get-tuple-element.84.iterate, f32[8,128]{1,0:T(8,128)S(1)} %get-tuple-element.82.scale), custom_call_target="tpu_custom_call" | custom-call | flops 4026531840 | bytes 3149824 | tf_op jit(solution)/shard_map/pallas_call | solution.py:34
  102.4 2.1 %shard_map.52 = (bf16[2,1024,512]{2,1,0:T(8,128)(2,1)S(1)}, bf16[1024,512]{1,0:T(8,128)(2,1)S(1)}) custom-call(bf16[2048,128]{1,0:T(8,128)(2,1)S(1)} %copy-done.1, bf16[2048,128]{1,0:T(8,128)(2,1)S(1)} %copy-done.3, bf16[2048,128]{1,0:T(8,128)(2,1)S(1)} %collective-permute-done.forward_core.refs_2_, ...), custom_call_target="tpu_custom_call" | custom-call | flops 1073741824 | bytes 7405568 | tf_op jit(solution)/shard_map/pallas_call | solution.py:34
  104.5 1.6 %collective-permute-done.39 = f32[4,64,128]{2,1,0:T(8,128)S(1)} collective-permute-done((f32[4,64,128]{2,1,0:T(8,128)S(1)}, f32[4,64,128]{2,1,0:T(8,128)S(1)}, u32[]{:S(2)}, u32[]{:S(2)}) %collective-permute-start.39) | collective-permute-done | bytes 131104 | tf_op jit(solution)/shard_map/ppermute | solution.py:451
  106.1 1.7 %collective-permute-done.38 = f32[4,64,128]{2,1,0:T(8,128)S(1)} collective-permute-done((f32[4,64,128]{2,1,0:T(8,128)S(1)}, f32[4,64,128]{2,1,0:T(8,128)S(1)}, u32[]{:S(2)}, u32[]{:S(2)}) %collective-permute-start.38) | collective-permute-done | bytes 131104 | tf_op jit(solution)/shard_map/ppermute | solution.py:20
  108.6 1.9 %collective-permute-done.41.theirs = f32[4,4,64,128]{3,2,1,0:T(8,128)S(1)} collective-permute-done((f32[4,4,64,128]{3,2,1,0:T(8,128)S(1)}, f32[4,4,64,128]{3,2,1,0:T(8,128)S(1)}, u32[]{:S(2)}, u32[]{:S(2)}) %collective-permute-start.41) | collective-permute-done | bytes 524320 | tf_op jit(solution)/shard_map/ppermute | solution.py:20
  110.5 3.1 %shard_map.53 = (bf16[2048,128]{1,0:T(8,128)(2,1)}, bf16[2048,128]{1,0:T(8,128)(2,1)}) custom-call(f32[4,4,64,128]{3,2,1,0:T(8,128)S(1)} %pad_maximum_fusion.1.ours, f32[4,4,64,128]{3,2,1,0:T(8,128)S(1)} %collective-permute-done.41.theirs, bf16[2,512,512]{2,1,0:T(8,128)(2,1)S(1)} %shard_map.51.inv, ...), custom_call_target="tpu_custom_call" | custom-call | flops 536870912 | bytes 10485760 | tf_op jit(solution)/shard_map/pallas_call | solution.py:34
  (92 shorter events, 28.0 us)
Async XLA Ops:
  0.6 12.4 %collective-permute-start = (bf16[2048,128]{1,0:T(8,128)(2,1)}, bf16[2048,128]{1,0:T(8,128)(2,1)S(1)}, u32[]{:S(2)}, u32[]{:S(2)}) collective-permute-start(bf16[2048,128]{1,0:T(8,128)(2,1)} %refs_0_.3), channel_id=1, source_target_pairs={{0,1},{1,0},{2,3},{3,2},{4,5},{5,4},{6,7},{7,6},{8,9},{9,8},{10,11... | collective-permute-start | bytes 1572872 | tf_op jit(solution)/shard_map/ppermute | solution.py:20
  1.1 11.9 %collective-permute-start.1 = (bf16[2048,128]{1,0:T(8,128)(2,1)}, bf16[2048,128]{1,0:T(8,128)(2,1)S(1)}, u32[]{:S(2)}, u32[]{:S(2)}) collective-permute-start(bf16[2048,128]{1,0:T(8,128)(2,1)} %refs_1_.3), channel_id=1, source_target_pairs={{0,1},{1,0},{2,3},{3,2},{4,5},{5,4},{6,7},{7,6},{8,9},{9,8},{10,11... | collective-permute-start | bytes 1572872 | tf_op jit(solution)/shard_map/ppermute | solution.py:20
  3.4 9.7 %collective-permute-start.2 = (bf16[1024,128]{1,0:T(8,128)(2,1)S(1)}, bf16[1024,128]{1,0:T(8,128)(2,1)S(1)}, u32[]{:S(2)}, u32[]{:S(2)}) collective-permute-start(bf16[1024,128]{1,0:T(8,128)(2,1)S(1)} %get-tuple-element.47), channel_id=1, source_target_pairs={{0,2},{2,0},{1,3},{3,1},{4,6},{6,4},{5,7},{7,5},{8,10},{10,8},{9,1... | collective-permute-start | bytes 786440 | tf_op jit(solution)/shard_map/ppermute | solution.py:20
  11.2 7.7 %collective-permute-start.4 = (bf16[1088,128]{1,0:T(8,128)(2,1)S(1)}, bf16[1088,128]{1,0:T(8,128)(2,1)S(1)}, u32[]{:S(2)}, u32[]{:S(2)}) collective-permute-start(bf16[1088,128]{1,0:T(8,128)(2,1)S(1)} %shard_map.42), channel_id=1, source_target_pairs={{0,2},{2,0},{1,3},{3,1},{4,6},{6,4},{5,7},{7,5},{8,10},{10,8},{9,1... | collective-permute-start | bytes 835592 | tf_op jit(solution)/shard_map/ppermute | solution.py:20
  19.4 6.9 %collective-permute-start.8 = (f32[4,80,128]{2,1,0:T(8,128)S(1)}, f32[4,80,128]{2,1,0:T(8,128)S(1)}, u32[]{:S(2)}, u32[]{:S(2)}) collective-permute-start(f32[4,80,128]{2,1,0:T(8,128)S(1)} %get-tuple-element.50), channel_id=1, source_target_pairs={{0,4},{4,0},{1,5},{5,1},{2,6},{6,2},{3,7},{7,3},{8,12},{12,8},{9,1... | collective-permute-start | bytes 491528 | tf_op jit(solution)/shard_map/ppermute | solution.py:20
  22.8 7.5 %collective-permute-start.9 = (f32[4,64,128]{2,1,0:T(8,128)S(1)}, f32[4,64,128]{2,1,0:T(8,128)S(1)}, u32[]{:S(2)}, u32[]{:S(2)}) collective-permute-start(f32[4,64,128]{2,1,0:T(8,128)S(1)} %get-tuple-element.56), channel_id=1, source_target_pairs={{0,2},{2,0},{1,3},{3,1},{4,6},{6,4},{5,7},{7,5},{8,10},{10,8},{9,1... | collective-permute-start | bytes 393224 | tf_op jit(solution)/shard_map/ppermute | solution.py:20
  24.0 7.3 %collective-permute-start.14 = (f32[4,64,128]{2,1,0:T(8,128)S(1)}, f32[4,64,128]{2,1,0:T(8,128)S(1)}, u32[]{:S(2)}, u32[]{:S(2)}) collective-permute-start(f32[4,64,128]{2,1,0:T(8,128)S(1)} %get-tuple-element.60), channel_id=1, source_target_pairs={{0,6},{2,4},{4,2},{6,0},{1,7},{3,5},{5,3},{7,1},{8,14},{10,12},{12... | collective-permute-start | bytes 393224 | tf_op jit(solution)/shard_map/ppermute | solution.py:451
  25.8 6.4 %collective-permute-start.13 = (f32[4,64,128]{2,1,0:T(8,128)S(1)}, f32[4,64,128]{2,1,0:T(8,128)S(1)}, u32[]{:S(2)}, u32[]{:S(2)}) collective-permute-start(f32[4,64,128]{2,1,0:T(8,128)S(1)} %get-tuple-element.59), channel_id=1, source_target_pairs={{0,4},{4,0},{1,5},{5,1},{2,6},{6,2},{3,7},{7,3},{8,12},{12,8},{9,1... | collective-permute-start | bytes 393224 | tf_op jit(solution)/shard_map/ppermute | solution.py:20
  32.2 9.6 %collective-permute-start.17 = (f32[64,128]{1,0:T(8,128)S(1)}, f32[64,128]{1,0:T(8,128)S(1)}, u32[]{:S(2)}, u32[]{:S(2)}) collective-permute-start(f32[64,128]{1,0:T(8,128)S(1)} %get-tuple-element.96), channel_id=1, source_target_pairs={{0,24},{8,0},{16,8},{24,16},{1,25},{9,1},{17,9},{25,17},{2,26},{10... | collective-permute-start | bytes 98312 | tf_op jit(solution)/shard_map/ppermute | solution.py:446
  36.7 5.8 %collective-permute-start.15 = (f32[64,128]{1,0:T(8,128)S(1)}, f32[64,128]{1,0:T(8,128)S(1)}, u32[]{:S(2)}, u32[]{:S(2)}) collective-permute-start(f32[64,128]{1,0:T(8,128)S(1)} %get-tuple-element.95), channel_id=1, source_target_pairs={{0,8},{8,16},{16,24},{24,0},{1,9},{9,17},{17,25},{25,1},{2,10},{10... | collective-permute-start | bytes 98312 | tf_op jit(solution)/shard_map/ppermute | solution.py:446
  37.7 5.3 %collective-permute-start.12 = (f32[80,128]{1,0:T(8,128)S(1)}, f32[80,128]{1,0:T(8,128)S(1)}, u32[]{:S(2)}, u32[]{:S(2)}) collective-permute-start(f32[80,128]{1,0:T(8,128)S(1)} %get-tuple-element.93), channel_id=1, source_target_pairs={{0,24},{8,0},{16,8},{24,16},{1,25},{9,1},{17,9},{25,17},{2,26},{10... | collective-permute-start | bytes 122888 | tf_op jit(solution)/shard_map/ppermute | solution.py:446
  41.7 6.0 %collective-permute-start.10 = (f32[80,128]{1,0:T(8,128)S(1)}, f32[80,128]{1,0:T(8,128)S(1)}, u32[]{:S(2)}, u32[]{:S(2)}) collective-permute-start(f32[80,128]{1,0:T(8,128)S(1)} %get-tuple-element.92), channel_id=1, source_target_pairs={{0,8},{8,16},{16,24},{24,0},{1,9},{9,17},{17,25},{25,1},{2,10},{10... | collective-permute-start | bytes 122888 | tf_op jit(solution)/shard_map/ppermute | solution.py:446
  41.7 13.7 %collective-permute-start.21 = (bf16[2,1024,128]{2,1,0:T(8,128)(2,1)S(1)}, bf16[2,1024,128]{2,1,0:T(8,128)(2,1)S(1)}, u32[]{:S(2)}, u32[]{:S(2)}) collective-permute-start(bf16[2,1024,128]{2,1,0:T(8,128)(2,1)S(1)} %get-tuple-element.63), channel_id=1, source_target_pairs={{0,2},{2,0},{1,3},{3,1},{4,6},{6,4},{5,7},{7,5},{8,10},{10,8},{9,1... | collective-permute-start | bytes 1572872 | tf_op jit(solution)/shard_map/ppermute | solution.py:20
  47.8 5.4 %collective-permute-start.19 = (f32[152,128]{1,0:T(8,128)S(1)}, f32[152,128]{1,0:T(8,128)S(1)}, u32[]{:S(2)}, u32[]{:S(2)}) collective-permute-start(f32[152,128]{1,0:T(8,128)S(1)} %constant_dynamic-update-slice_fusion), channel_id=1, source_target_pairs={{0,16},{8,24},{16,0},{24,8},{1,17},{9,25},{17,1},{25,9},{2,18},{10... | collective-permute-start | bytes 233480 | tf_op jit(solution)/shard_map/ppermute | solution.py:446
  47.9 7.5 %collective-permute-start.18 = (f32[152,128]{1,0:T(8,128)S(1)}, f32[152,128]{1,0:T(8,128)S(1)}, u32[]{:S(2)}, u32[]{:S(2)}) collective-permute-start(f32[152,128]{1,0:T(8,128)S(1)} %constant_dynamic-update-slice_fusion), channel_id=1, source_target_pairs={{0,8},{8,16},{16,24},{24,0},{1,9},{9,17},{17,25},{25,1},{2,10},{10... | collective-permute-start | bytes 233480 | tf_op jit(solution)/shard_map/ppermute | solution.py:446
  55.5 8.2 %collective-permute-start.22 = (f32[4,80,128]{2,1,0:T(8,128)S(1)}, f32[4,80,128]{2,1,0:T(8,128)S(1)}, u32[]{:S(2)}, u32[]{:S(2)}) collective-permute-start(f32[4,80,128]{2,1,0:T(8,128)S(1)} %pad_maximum_fusion.2.refs_0_), channel_id=1, source_target_pairs={{0,2},{2,0},{1,3},{3,1},{4,6},{6,4},{5,7},{7,5},{8,10},{10,8},{9,1... | collective-permute-start | bytes 491528 | tf_op jit(solution)/shard_map/ppermute | solution.py:20
  56.0 11.1 %collective-permute-start.26 = (f32[4,80,128]{2,1,0:T(8,128)S(1)}, f32[4,80,128]{2,1,0:T(8,128)S(1)}, u32[]{:S(2)}, u32[]{:S(2)}) collective-permute-start(f32[4,80,128]{2,1,0:T(8,128)S(1)} %pad_maximum_fusion.2.refs_0_), channel_id=1, source_target_pairs={{0,4},{4,0},{1,5},{5,1},{2,6},{6,2},{3,7},{7,3},{8,12},{12,8},{9,1... | collective-permute-start | bytes 491528 | tf_op jit(solution)/shard_map/ppermute | solution.py:20
  57.5 9.6 %collective-permute-start.27 = (f32[4,80,128]{2,1,0:T(8,128)S(1)}, f32[4,80,128]{2,1,0:T(8,128)S(1)}, u32[]{:S(2)}, u32[]{:S(2)}) collective-permute-start(f32[4,80,128]{2,1,0:T(8,128)S(1)} %pad_maximum_fusion.2.refs_0_), channel_id=1, source_target_pairs={{0,6},{2,4},{4,2},{6,0},{1,7},{3,5},{5,3},{7,1},{8,14},{10,12},{12... | collective-permute-start | bytes 491528 | tf_op jit(solution)/shard_map/ppermute | solution.py:451
  63.6 7.8 %collective-permute-start.25 = (f32[4,72,128]{2,1,0:T(8,128)S(1)}, f32[4,72,128]{2,1,0:T(8,128)S(1)}, u32[]{:S(2)}, u32[]{:S(2)}) collective-permute-start(f32[4,72,128]{2,1,0:T(8,128)S(1)} %pad_maximum_fusion.5), channel_id=1, source_target_pairs={{0,6},{2,4},{4,2},{6,0},{1,7},{3,5},{5,3},{7,1},{8,14},{10,12},{12... | collective-permute-start | bytes 442376 | tf_op jit(solution)/shard_map/ppermute | solution.py:451
  65.1 6.4 %collective-permute-start.24 = (f32[4,72,128]{2,1,0:T(8,128)S(1)}, f32[4,72,128]{2,1,0:T(8,128)S(1)}, u32[]{:S(2)}, u32[]{:S(2)}) collective-permute-start(f32[4,72,128]{2,1,0:T(8,128)S(1)} %pad_maximum_fusion.5), channel_id=1, source_target_pairs={{0,4},{4,0},{1,5},{5,1},{2,6},{6,2},{3,7},{7,3},{8,12},{12,8},{9,1... | collective-permute-start | bytes 442376 | tf_op jit(solution)/shard_map/ppermute | solution.py:20
  65.5 5.9 %collective-permute-start.23 = (f32[4,72,128]{2,1,0:T(8,128)S(1)}, f32[4,72,128]{2,1,0:T(8,128)S(1)}, u32[]{:S(2)}, u32[]{:S(2)}) collective-permute-start(f32[4,72,128]{2,1,0:T(8,128)S(1)} %pad_maximum_fusion.5), channel_id=1, source_target_pairs={{0,2},{2,0},{1,3},{3,1},{4,6},{6,4},{5,7},{7,5},{8,10},{10,8},{9,1... | collective-permute-start | bytes 442376 | tf_op jit(solution)/shard_map/ppermute | solution.py:20
  79.0 6.1 %collective-permute-start.30 = (f32[512,512]{1,0:T(8,128)S(1)}, f32[512,512]{1,0:T(8,128)S(1)}, u32[]{:S(2)}, u32[]{:S(2)}) collective-permute-start(f32[512,512]{1,0:T(8,128)S(1)} %get-tuple-element.74.own), channel_id=1, source_target_pairs={{0,1},{1,0},{2,3},{3,2},{4,5},{5,4},{6,7},{7,6},{8,9},{9,8},{10,11... | collective-permute-start | bytes 3145736 | tf_op jit(solution)/shard_map/ppermute | solution.py:20
  79.4 23.1 %collective-permute-start.40 = (bf16[2,1024,128]{2,1,0:T(8,128)(2,1)S(1)}, bf16[2,1024,128]{2,1,0:T(8,128)(2,1)S(1)}, u32[]{:S(2)}, u32[]{:S(2)}) collective-permute-start(bf16[2,1024,128]{2,1,0:T(8,128)(2,1)S(1)} %collective-permute-done.21.refs_4_), channel_id=1, source_target_pairs={{0,1},{1,0},{2,3},{3,2},{4,5},{5,4},{6,7},{7,6},{8,9},{9,8},{10,11... | collective-permute-start | bytes 1572872 | tf_op jit(solution)/shard_map/ppermute | solution.py:20
  81.5 7.0 %collective-permute-start.33 = (bf16[4,64,128]{2,1,0:T(8,128)(2,1)S(1)}, bf16[4,64,128]{2,1,0:T(8,128)(2,1)S(1)}, u32[]{:S(2)}, u32[]{:S(2)}) collective-permute-start(bf16[4,64,128]{2,1,0:T(8,128)(2,1)S(1)} %get-tuple-element.81), channel_id=1, source_target_pairs={{0,6},{2,4},{4,2},{6,0},{1,7},{3,5},{5,3},{7,1},{8,14},{10,12},{12... | collective-permute-start | bytes 196616 | tf_op jit(solution)/shard_map/ppermute | solution.py:451
  83.0 5.5 %collective-permute-start.32 = (bf16[4,64,128]{2,1,0:T(8,128)(2,1)S(1)}, bf16[4,64,128]{2,1,0:T(8,128)(2,1)S(1)}, u32[]{:S(2)}, u32[]{:S(2)}) collective-permute-start(bf16[4,64,128]{2,1,0:T(8,128)(2,1)S(1)} %get-tuple-element.80), channel_id=1, source_target_pairs={{0,4},{4,0},{1,5},{5,1},{2,6},{6,2},{3,7},{7,3},{8,12},{12,8},{9,1... | collective-permute-start | bytes 196616 | tf_op jit(solution)/shard_map/ppermute | solution.py:20
  88.6 10.2 %collective-permute-start.36 = (bf16[4,64,128]{2,1,0:T(8,128)(2,1)S(1)}, bf16[4,64,128]{2,1,0:T(8,128)(2,1)S(1)}, u32[]{:S(2)}, u32[]{:S(2)}) collective-permute-start(bf16[4,64,128]{2,1,0:T(8,128)(2,1)S(1)} %add_convert_fusion), channel_id=1, source_target_pairs={{0,24},{8,0},{16,8},{24,16},{1,25},{9,1},{17,9},{25,17},{2,26},{10... | collective-permute-start | bytes 196616 | tf_op jit(solution)/shard_map/ppermute | solution.py:446
  90.6 8.2 %collective-permute-start.35 = (bf16[4,64,128]{2,1,0:T(8,128)(2,1)S(1)}, bf16[4,64,128]{2,1,0:T(8,128)(2,1)S(1)}, u32[]{:S(2)}, u32[]{:S(2)}) collective-permute-start(bf16[4,64,128]{2,1,0:T(8,128)(2,1)S(1)} %add_convert_fusion), channel_id=1, source_target_pairs={{0,16},{8,24},{16,0},{24,8},{1,17},{9,25},{17,1},{25,9},{2,18},{10... | collective-permute-start | bytes 196616 | tf_op jit(solution)/shard_map/ppermute | solution.py:446
  90.6 8.2 %collective-permute-start.34 = (bf16[4,64,128]{2,1,0:T(8,128)(2,1)S(1)}, bf16[4,64,128]{2,1,0:T(8,128)(2,1)S(1)}, u32[]{:S(2)}, u32[]{:S(2)}) collective-permute-start(bf16[4,64,128]{2,1,0:T(8,128)(2,1)S(1)} %add_convert_fusion), channel_id=1, source_target_pairs={{0,8},{8,16},{16,24},{24,0},{1,9},{9,17},{17,25},{25,1},{2,10},{10... | collective-permute-start | bytes 196616 | tf_op jit(solution)/shard_map/ppermute | solution.py:446
  98.7 11.8 %collective-permute-start.42 = (bf16[2,512,512]{2,1,0:T(8,128)(2,1)S(1)}, bf16[2,512,512]{2,1,0:T(8,128)(2,1)S(1)}, u32[]{:S(2)}, u32[]{:S(2)}) collective-permute-start(bf16[2,512,512]{2,1,0:T(8,128)(2,1)S(1)} %shard_map.51.inv), channel_id=1, source_target_pairs={{0,1},{1,0},{2,3},{3,2},{4,5},{5,4},{6,7},{7,6},{8,9},{9,8},{10,11... | collective-permute-start | bytes 3145736 | tf_op jit(solution)/shard_map/ppermute | solution.py:20
  98.8 7.3 %collective-permute-start.39 = (f32[4,64,128]{2,1,0:T(8,128)S(1)}, f32[4,64,128]{2,1,0:T(8,128)S(1)}, u32[]{:S(2)}, u32[]{:S(2)}) collective-permute-start(f32[4,64,128]{2,1,0:T(8,128)S(1)} %convert_add_fusion), channel_id=1, source_target_pairs={{0,6},{2,4},{4,2},{6,0},{1,7},{3,5},{5,3},{7,1},{8,14},{10,12},{12... | collective-permute-start | bytes 393224 | tf_op jit(solution)/shard_map/ppermute | solution.py:451
  100.3 7.5 %collective-permute-start.38 = (f32[4,64,128]{2,1,0:T(8,128)S(1)}, f32[4,64,128]{2,1,0:T(8,128)S(1)}, u32[]{:S(2)}, u32[]{:S(2)}) collective-permute-start(f32[4,64,128]{2,1,0:T(8,128)S(1)} %convert_add_fusion), channel_id=1, source_target_pairs={{0,4},{4,0},{1,5},{5,1},{2,6},{6,2},{3,7},{7,3},{8,12},{12,8},{9,1... | collective-permute-start | bytes 393224 | tf_op jit(solution)/shard_map/ppermute | solution.py:20
  101.2 7.3 %collective-permute-start.37 = (f32[4,64,128]{2,1,0:T(8,128)S(1)}, f32[4,64,128]{2,1,0:T(8,128)S(1)}, u32[]{:S(2)}, u32[]{:S(2)}) collective-permute-start(f32[4,64,128]{2,1,0:T(8,128)S(1)} %convert_add_fusion), channel_id=1, source_target_pairs={{0,2},{2,0},{1,3},{3,1},{4,6},{6,4},{5,7},{7,5},{8,10},{10,8},{9,1... | collective-permute-start | bytes 393224 | tf_op jit(solution)/shard_map/ppermute | solution.py:20
  (15 other events, 55.9 us)

commit v5 on v4

--- a/solution.py
+++ b/solution.py
@@ -201,8 +201,8 @@
 
 
 def near_kernel(width, pd, xd, forward, backward, forward_core, backward_core, halo, halo_core, *refs):
-    packed, back = refs[:2], refs[2]
-    chosen, behind, late, edge, flat = refs[3:]
+    packed, back = [refs[0].at[:, i] for i in range(2)], refs[1]
+    chosen, behind, late, edge, flat = refs[2:]
     core = lax.axis_index("core")
     own, other = at(core, width), at(1 - core, width)
     rows = at(lax.axis_index("y"), back.shape[1])
@@ -500,15 +500,15 @@
     across = [swap(send, "y"), swap(front, "y")]
     own_core = [swap(a, "core") for a in own]
     halo_core = swap(halo, "core")
-    *near, back = call(
+    near, back = call(
         kernel(near_kernel, width, pd, xd),
-        [shape((depth, pd + xd, LANES), F32)] * 2 + [shape((2, half, width), BF16)],
+        [shape((depth, 2, pd + xd, LANES), F32), shape((2, half, width), BF16)],
         [pltpu.VMEM((samples, pair), BF16)] * 3 + [pltpu.VMEM((16, pair), BF16), flat(near_parts * pd, near_parts * xd)],
         3 * samples * pair * pair,
         *own, *own_core, halo, after(halo_core, across[0]),
     )
-    near_x = swap(near[1], "x")
-    across_core = [swap(across[0], "core"), swap(after(across[1], near[1]), "core")]
+    near_got = [ahead(near[k], k) for k in range(1, depth)]
+    across_core = [swap(across[0], "core"), swap(after(across[1], near), "core")]
     here, edges, shifted, *far, tails = call(
         kernel(far_kernel, width, po, xo),
         [
@@ -523,7 +523,8 @@
         *own, *own_core, *across, *across_core, halo, halo_core,
     )
     swapped = exchange(far)
-    near_sum = scatter_z([near[0], after(near_x, swapped[1])])
+    near_z = sum((after(got, *swapped[1:]) for got in near_got), near[0])
+    near_sum = near_z[0] + swap(near_z[1], "x")
     across2 = swap(after(back, swapped[1]), "y")
     far_sum = scatter_z(swapped)
     chunk = jnp.concatenate([near_sum[:pd], far_sum[:po], near_sum[pd:], far_sum[po:], tails])

time: 114 us -> 112 us (0.982)
  waiting for transfers between devices: 36.1 us -> 31.8 us
  starting transfers between devices: 44 us -> 46.1 us
    ppermute x25, waiting for transfers between devices: 21.2 us -> 18 us  [swap(): return lax.ppermute(value, axis, [(0, 1), (1, 0)])]
    ppermute x12, starting transfers between devices: 14.3 us -> 17 us  [ahead(): return lax.ppermute(piece, 'z', [(i, (i + by) % size) for i in range(size)])]
    ppermute x12, waiting for transfers between devices: 11 us -> 8.64 us  [ahead(): return lax.ppermute(piece, 'z', [(i, (i + by) % size) for i in range(size)])]
    ppermute x5, waiting for transfers between devices: 2.58 us -> 3.87 us  [exchange(): lax.ppermute(pieces[3], ('x', 'y'), both)]
where the time goes in v5:
time: 112 us; the launch traced here: 111 us
  starting transfers between devices  46.1 us (41%)
  waiting for transfers between devices  31.8 us (28%)
  Pallas kernels  30 us (27%)
  local copies, waits for them, and re-layouts  2.14 us (2%)
    pallas_call x13, Pallas kernels, call(): pl.pallas_call(body, out_shape=shapes, in_specs=[pl.BlockSpec(memory_spac...  30 us
    ppermute x25, waiting for transfers between devices, swap(): return lax.ppermute(value, axis, [(0, 1), (1, 0)])  18 us
    ppermute x25, starting transfers between devices, swap(): return lax.ppermute(value, axis, [(0, 1), (1, 0)])  18 us
    ppermute x12, starting transfers between devices, ahead(): return lax.ppermute(piece, 'z', [(i, (i + by) % size) for i in range(size)])  17 us
    ppermute x12, waiting for transfers between devices, ahead(): return lax.ppermute(piece, 'z', [(i, (i + by) % size) for i in range(size)])  8.64 us
    ppermute x5, starting transfers between devices, exchange(): lax.ppermute(pieces[3], ('x', 'y'), both)  7.75 us
    ppermute x5, waiting for transfers between devices, exchange(): lax.ppermute(pieces[3], ('x', 'y'), both)  3.87 us
    ppermute x1, starting transfers between devices, from_behind(): return lax.ppermute(value, axes, [(i, i + 1) for i in range(devices - 1)])  3.38 us
  transfers between devices with their start and end apart: 43, of which 20 were waited for; matrix products, arithmetic and copies ran while one was open for 0% of the time, Pallas kernels for 23%

profile of v5, /device:TPU:0, one launch (start us, length us, event | category | flops | bytes accessed | tf_op | source)
XLA Modules:
  0.0 111.4 jit_solution(4782967806369838083)
XLA Ops:
  3.4 3.0 %collective-permute-start.2 = (bf16[1024,128]{1,0:T(8,128)(2,1)S(1)}, bf16[1024,128]{1,0:T(8,128)(2,1)S(1)}, u32[]{:S(2)}, u32[]{:S(2)}) collective-permute-start(bf16[1024,128]{1,0:T(8,128)(2,1)S(1)} %get-tuple-element.48), channel_id=1, source_target_pairs={{0,2},{2,0},{1,3},{3,1},{4,6},{6,4},{5,7},{7,5},{8,10},{10,8},{9,1... | collective-permute-start | bytes 786440 | tf_op jit(solution)/shard_map/ppermute | solution.py:20
  6.4 3.4 %collective-permute-start.3 = (bf16[2,16,128]{2,1,0:T(8,128)(2,1)S(1)}, bf16[2,16,128]{2,1,0:T(8,128)(2,1)S(1)}, u32[]{:S(2)}, u32[]{:S(2)}) collective-permute-start(bf16[2,16,128]{2,1,0:T(8,128)(2,1)S(1)} %get-tuple-element.49), channel_id=1, source_target_pairs={{0,4},{4,8},{8,12},{12,16},{16,20},{20,24},{24,28},{1,5},{5,9},{9,... | collective-permute-start | bytes 24584 | tf_op jit(solution)/shard_map/ppermute | solution.py:25
  14.2 4.7 %collective-permute-done.4.refs_5_ = bf16[1088,128]{1,0:T(8,128)(2,1)S(1)} collective-permute-done((bf16[1088,128]{1,0:T(8,128)(2,1)S(1)}, bf16[1088,128]{1,0:T(8,128)(2,1)S(1)}, u32[]{:S(2)}, u32[]{:S(2)}) %collective-permute-start.4) | collective-permute-done | bytes 278560 | tf_op jit(solution)/shard_map/ppermute | solution.py:20
  19.4 4.9 %collective-permute-start.13 = (f32[2,80,128]{2,1,0:T(8,128)S(1)}, f32[2,80,128]{2,1,0:T(8,128)S(1)}, u32[]{:S(2)}, u32[]{:S(2)}) collective-permute-start(f32[2,80,128]{2,1,0:T(8,128)S(1)} %get-tuple-element.95), channel_id=1, source_target_pairs={{0,24},{8,0},{16,8},{24,16},{1,25},{9,1},{17,9},{25,17},{2,26},{10... | collective-permute-start | bytes 245768 | tf_op jit(solution)/shard_map/ppermute | solution.py:446
  27.6 1.5 %collective-permute-start.11 = (f32[4,64,128]{2,1,0:T(8,128)S(1)}, f32[4,64,128]{2,1,0:T(8,128)S(1)}, u32[]{:S(2)}, u32[]{:S(2)}) collective-permute-start(f32[4,64,128]{2,1,0:T(8,128)S(1)} %get-tuple-element.58), channel_id=1, source_target_pairs={{0,6},{2,4},{4,2},{6,0},{1,7},{3,5},{5,3},{7,1},{8,14},{10,12},{12... | collective-permute-start | bytes 393224 | tf_op jit(solution)/shard_map/ppermute | solution.py:451
  29.5 1.6 %collective-permute-start.8 = (f32[2,80,128]{2,1,0:T(8,128)S(1)}, f32[2,80,128]{2,1,0:T(8,128)S(1)}, u32[]{:S(2)}, u32[]{:S(2)}) collective-permute-start(f32[2,80,128]{2,1,0:T(8,128)S(1)} %get-tuple-element.94), channel_id=1, source_target_pairs={{0,8},{8,16},{16,24},{24,0},{1,9},{9,17},{17,25},{25,1},{2,10},{10... | collective-permute-start | bytes 245768 | tf_op jit(solution)/shard_map/ppermute | solution.py:446
  32.5 2.2 %collective-permute-done.11 = f32[4,64,128]{2,1,0:T(8,128)S(1)} collective-permute-done((f32[4,64,128]{2,1,0:T(8,128)S(1)}, f32[4,64,128]{2,1,0:T(8,128)S(1)}, u32[]{:S(2)}, u32[]{:S(2)}) %collective-permute-start.11) | collective-permute-done | bytes 131104 | tf_op jit(solution)/shard_map/ppermute | solution.py:451
  36.0 1.7 %collective-permute-start.17 = (f32[64,128]{1,0:T(8,128)S(1)}, f32[64,128]{1,0:T(8,128)S(1)}, u32[]{:S(2)}, u32[]{:S(2)}) collective-permute-start(f32[64,128]{1,0:T(8,128)S(1)} %get-tuple-element.98), channel_id=1, source_target_pairs={{0,24},{8,0},{16,8},{24,16},{1,25},{9,1},{17,9},{25,17},{2,26},{10... | collective-permute-start | bytes 98312 | tf_op jit(solution)/shard_map/ppermute | solution.py:446
  37.7 1.9 %collective-permute-start.15 = (f32[64,128]{1,0:T(8,128)S(1)}, f32[64,128]{1,0:T(8,128)S(1)}, u32[]{:S(2)}, u32[]{:S(2)}) collective-permute-start(f32[64,128]{1,0:T(8,128)S(1)} %get-tuple-element.97), channel_id=1, source_target_pairs={{0,8},{8,16},{16,24},{24,0},{1,9},{9,17},{17,25},{25,1},{2,10},{10... | collective-permute-start | bytes 98312 | tf_op jit(solution)/shard_map/ppermute | solution.py:446
  43.8 1.9 %collective-permute-start.20 = (f32[152,128]{1,0:T(8,128)S(1)}, f32[152,128]{1,0:T(8,128)S(1)}, u32[]{:S(2)}, u32[]{:S(2)}) collective-permute-start(f32[152,128]{1,0:T(8,128)S(1)} %constant_dynamic-update-slice_fusion), channel_id=1, source_target_pairs={{0,24},{8,0},{16,8},{24,16},{1,25},{9,1},{17,9},{25,17},{2,26},{10... | collective-permute-start | bytes 233480 | tf_op jit(solution)/shard_map/ppermute | solution.py:446
  47.2 2.1 %collective-permute-done.20 = f32[152,128]{1,0:T(8,128)S(1)} collective-permute-done((f32[152,128]{1,0:T(8,128)S(1)}, f32[152,128]{1,0:T(8,128)S(1)}, u32[]{:S(2)}, u32[]{:S(2)}) %collective-permute-start.20) | collective-permute-done | bytes 77856 | tf_op jit(solution)/shard_map/ppermute | solution.py:446
  49.3 2.2 %collective-permute-done.19 = f32[152,128]{1,0:T(8,128)S(1)} collective-permute-done((f32[152,128]{1,0:T(8,128)S(1)}, f32[152,128]{1,0:T(8,128)S(1)}, u32[]{:S(2)}, u32[]{:S(2)}) %collective-permute-start.19) | collective-permute-done | bytes 77856 | tf_op jit(solution)/shard_map/ppermute | solution.py:446
  51.5 1.6 %collective-permute-done.18 = f32[152,128]{1,0:T(8,128)S(1)} collective-permute-done((f32[152,128]{1,0:T(8,128)S(1)}, f32[152,128]{1,0:T(8,128)S(1)}, u32[]{:S(2)}, u32[]{:S(2)}) %collective-permute-start.18) | collective-permute-done | bytes 77856 | tf_op jit(solution)/shard_map/ppermute | solution.py:446
  55.1 1.5 %collective-permute-start.27 = (f32[4,80,128]{2,1,0:T(8,128)S(1)}, f32[4,80,128]{2,1,0:T(8,128)S(1)}, u32[]{:S(2)}, u32[]{:S(2)}) collective-permute-start(f32[4,80,128]{2,1,0:T(8,128)S(1)} %pad_maximum_fusion.2.refs_0_), channel_id=1, source_target_pairs={{0,6},{2,4},{4,2},{6,0},{1,7},{3,5},{5,3},{7,1},{8,14},{10,12},{12... | collective-permute-start | bytes 491528 | tf_op jit(solution)/shard_map/ppermute | solution.py:451
  56.6 4.4 %collective-permute-done.22.refs_1_ = f32[4,80,128]{2,1,0:T(8,128)S(1)} collective-permute-done((f32[4,80,128]{2,1,0:T(8,128)S(1)}, f32[4,80,128]{2,1,0:T(8,128)S(1)}, u32[]{:S(2)}, u32[]{:S(2)}) %collective-permute-start.22) | collective-permute-done | bytes 163872 | tf_op jit(solution)/shard_map/ppermute | solution.py:20
  61.0 1.7 %collective-permute-start.25 = (f32[4,72,128]{2,1,0:T(8,128)S(1)}, f32[4,72,128]{2,1,0:T(8,128)S(1)}, u32[]{:S(2)}, u32[]{:S(2)}) collective-permute-start(f32[4,72,128]{2,1,0:T(8,128)S(1)} %pad_maximum_fusion.5), channel_id=1, source_target_pairs={{0,6},{2,4},{4,2},{6,0},{1,7},{3,5},{5,3},{7,1},{8,14},{10,12},{12... | collective-permute-start | bytes 442376 | tf_op jit(solution)/shard_map/ppermute | solution.py:451
  62.7 1.8 %collective-permute-start.23 = (f32[4,72,128]{2,1,0:T(8,128)S(1)}, f32[4,72,128]{2,1,0:T(8,128)S(1)}, u32[]{:S(2)}, u32[]{:S(2)}) collective-permute-start(f32[4,72,128]{2,1,0:T(8,128)S(1)} %pad_maximum_fusion.5), channel_id=1, source_target_pairs={{0,2},{2,0},{1,3},{3,1},{4,6},{6,4},{5,7},{7,5},{8,10},{10,8},{9,1... | collective-permute-start | bytes 442376 | tf_op jit(solution)/shard_map/ppermute | solution.py:20
  64.5 4.3 %shard_map.45 = (f32[512,512]{1,0:T(8,128)S(1)}, f32[512,512]{1,0:T(8,128)S(1)}, f32[512,512]{1,0:T(8,128)S(1)}, f32[8,128]{1,0:T(8,128)S(1)}) custom-call(f32[4,80,128]{2,1,0:T(8,128)S(1)} %pad_maximum_fusion.2.refs_0_, f32[4,80,128]{2,1,0:T(8,128)S(1)} %collective-permute-done.22.refs_1_, f32[4,80,128]{2,1,0:T(8,128)S(1)} %collective-permute-done.26.refs_2_, ...), custom_call_target="tpu_custom_call" | custom-call | flops 4026531840 | bytes 3805184 | tf_op jit(solution)/shard_map/pallas_call | solution.py:34
  69.0 3.9 %shard_map.46.inv = bf16[2,512,512]{2,1,0:T(8,128)(2,1)S(1)} custom-call(f32[512,512]{1,0:T(8,128)S(1)} %get-tuple-element.68.error, f32[512,512]{1,0:T(8,128)S(1)} %get-tuple-element.70.iterate, f32[8,128]{1,0:T(8,128)S(1)} %get-tuple-element.71.scale), custom_call_target="tpu_custom_call" | custom-call | flops 4026531840 | bytes 3149824 | tf_op jit(solution)/shard_map/pallas_call | solution.py:34
  74.8 1.5 %collective-permute-done.29.theirs.refs_8_ = bf16[512,512]{1,0:T(8,128)(2,1)S(1)} collective-permute-done((bf16[512,512]{1,0:T(8,128)(2,1)S(1)}, bf16[512,512]{1,0:T(8,128)(2,1)S(1)}, u32[]{:S(2)}, u32[]{:S(2)}) %collective-permute-start.29) | collective-permute-done | bytes 524320 | tf_op jit(solution)/shard_map/ppermute | solution.py:20
  76.8 2.0 %shard_map.48 = (bf16[2,1024,512]{2,1,0:T(8,128)(2,1)S(1)}, bf16[1024,512]{1,0:T(8,128)(2,1)S(1)}, bf16[4,64,128]{2,1,0:T(8,128)(2,1)S(1)}, bf16[4,64,128]{2,1,0...) custom-call(bf16[2,1024,512]{2,1,0:T(8,128)(2,1)S(1)} %get-tuple-element.53.here, ...), custom_call_target="tpu_custom_call" | custom-call | flops 1342177280 | bytes 7667712 | tf_op jit(solution)/shard_map/pallas_call | solution.py:34
  78.8 1.8 %collective-permute-start.33 = (bf16[4,64,128]{2,1,0:T(8,128)(2,1)S(1)}, bf16[4,64,128]{2,1,0:T(8,128)(2,1)S(1)}, u32[]{:S(2)}, u32[]{:S(2)}) collective-permute-start(bf16[4,64,128]{2,1,0:T(8,128)(2,1)S(1)} %get-tuple-element.83), channel_id=1, source_target_pairs={{0,6},{2,4},{4,2},{6,0},{1,7},{3,5},{5,3},{7,1},{8,14},{10,12},{12... | collective-permute-start | bytes 196616 | tf_op jit(solution)/shard_map/ppermute | solution.py:451
  82.4 3.4 %shard_map.49 = (f32[512,512]{1,0:T(8,128)S(1)}, f32[8,128]{1,0:T(8,128)S(1)}) custom-call(f32[512,512]{1,0:T(8,128)S(1)} %get-tuple-element.76.own, f32[512,512]{1,0:T(8,128)S(1)} %collective-permute-done.30.other, f32[512,512]{1,0:T(8,128)S(1)} %get-tuple-element.77.cross, bf16[512,512]{1,0:T(8,128)(2,1)S(1)} %collective-permute-done.29.theirs.refs_8_, ...), custom_call_target="tpu_custom_call" | custom-call | flops 2415919104 | bytes 4726784 | tf_op jit(solution)/shard_map/pallas_call | solution.py:34
  85.9 1.6 %collective-permute-start.36 = (bf16[4,64,128]{2,1,0:T(8,128)(2,1)S(1)}, bf16[4,64,128]{2,1,0:T(8,128)(2,1)S(1)}, u32[]{:S(2)}, u32[]{:S(2)}) collective-permute-start(bf16[4,64,128]{2,1,0:T(8,128)(2,1)S(1)} %add_convert_fusion), channel_id=1, source_target_pairs={{0,24},{8,0},{16,8},{24,16},{1,25},{9,1},{17,9},{25,17},{2,26},{10... | collective-permute-start | bytes 196616 | tf_op jit(solution)/shard_map/ppermute | solution.py:446
  89.1 3.5 %shard_map.50 = (f32[512,512]{1,0:T(8,128)S(1)}, f32[512,512]{1,0:T(8,128)S(1)}) custom-call(f32[512,512]{1,0:T(8,128)S(1)} %get-tuple-element.79.matrix, f32[8,128]{1,0:T(8,128)S(1)} %get-tuple-element.84.scale), custom_call_target="tpu_custom_call" | custom-call | flops 4026531840 | bytes 3149824 | tf_op jit(solution)/shard_map/pallas_call | solution.py:34
  92.6 3.9 %shard_map.51.inv = bf16[2,512,512]{2,1,0:T(8,128)(2,1)S(1)} custom-call(f32[512,512]{1,0:T(8,128)S(1)} %get-tuple-element.85.error, f32[512,512]{1,0:T(8,128)S(1)} %get-tuple-element.86.iterate, f32[8,128]{1,0:T(8,128)S(1)} %get-tuple-element.84.scale), custom_call_target="tpu_custom_call" | custom-call | flops 4026531840 | bytes 3149824 | tf_op jit(solution)/shard_map/pallas_call | solution.py:34
  97.9 1.5 %collective-permute-start.38 = (f32[4,64,128]{2,1,0:T(8,128)S(1)}, f32[4,64,128]{2,1,0:T(8,128)S(1)}, u32[]{:S(2)}, u32[]{:S(2)}) collective-permute-start(f32[4,64,128]{2,1,0:T(8,128)S(1)} %convert_add_fusion), channel_id=1, source_target_pairs={{0,4},{4,0},{1,5},{5,1},{2,6},{6,2},{3,7},{7,3},{8,12},{12,8},{9,1... | collective-permute-start | bytes 393224 | tf_op jit(solution)/shard_map/ppermute | solution.py:20
  100.2 2.1 %shard_map.52 = (bf16[2,1024,512]{2,1,0:T(8,128)(2,1)S(1)}, bf16[1024,512]{1,0:T(8,128)(2,1)S(1)}) custom-call(bf16[2048,128]{1,0:T(8,128)(2,1)S(1)} %copy-done.1, bf16[2048,128]{1,0:T(8,128)(2,1)S(1)} %copy-done.3, bf16[2048,128]{1,0:T(8,128)(2,1)S(1)} %collective-permute-done.forward_core.refs_2_, ...), custom_call_target="tpu_custom_call" | custom-call | flops 1073741824 | bytes 7405568 | tf_op jit(solution)/shard_map/pallas_call | solution.py:34
  102.3 1.6 %collective-permute-done.39 = f32[4,64,128]{2,1,0:T(8,128)S(1)} collective-permute-done((f32[4,64,128]{2,1,0:T(8,128)S(1)}, f32[4,64,128]{2,1,0:T(8,128)S(1)}, u32[]{:S(2)}, u32[]{:S(2)}) %collective-permute-start.39) | collective-permute-done | bytes 131104 | tf_op jit(solution)/shard_map/ppermute | solution.py:451
  103.9 2.2 %collective-permute-done.38 = f32[4,64,128]{2,1,0:T(8,128)S(1)} collective-permute-done((f32[4,64,128]{2,1,0:T(8,128)S(1)}, f32[4,64,128]{2,1,0:T(8,128)S(1)}, u32[]{:S(2)}, u32[]{:S(2)}) %collective-permute-start.38) | collective-permute-done | bytes 131104 | tf_op jit(solution)/shard_map/ppermute | solution.py:20
  106.4 1.9 %collective-permute-done.41.theirs = f32[4,4,64,128]{3,2,1,0:T(8,128)S(1)} collective-permute-done((f32[4,4,64,128]{3,2,1,0:T(8,128)S(1)}, f32[4,4,64,128]{3,2,1,0:T(8,128)S(1)}, u32[]{:S(2)}, u32[]{:S(2)}) %collective-permute-start.41) | collective-permute-done | bytes 524320 | tf_op jit(solution)/shard_map/ppermute | solution.py:20
  108.3 3.1 %shard_map.53 = (bf16[2048,128]{1,0:T(8,128)(2,1)}, bf16[2048,128]{1,0:T(8,128)(2,1)}) custom-call(f32[4,4,64,128]{3,2,1,0:T(8,128)S(1)} %pad_maximum_fusion.1.ours, f32[4,4,64,128]{3,2,1,0:T(8,128)S(1)} %collective-permute-done.41.theirs, bf16[2,512,512]{2,1,0:T(8,128)(2,1)S(1)} %shard_map.51.inv, ...), custom_call_target="tpu_custom_call" | custom-call | flops 536870912 | bytes 10485760 | tf_op jit(solution)/shard_map/pallas_call | solution.py:34
  (93 shorter events, 30.2 us)
Async XLA Ops:
  0.6 12.4 %collective-permute-start = (bf16[2048,128]{1,0:T(8,128)(2,1)}, bf16[2048,128]{1,0:T(8,128)(2,1)S(1)}, u32[]{:S(2)}, u32[]{:S(2)}) collective-permute-start(bf16[2048,128]{1,0:T(8,128)(2,1)} %refs_0_.3), channel_id=1, source_target_pairs={{0,1},{1,0},{2,3},{3,2},{4,5},{5,4},{6,7},{7,6},{8,9},{9,8},{10,11... | collective-permute-start | bytes 1572872 | tf_op jit(solution)/shard_map/ppermute | solution.py:20
  1.1 11.9 %collective-permute-start.1 = (bf16[2048,128]{1,0:T(8,128)(2,1)}, bf16[2048,128]{1,0:T(8,128)(2,1)S(1)}, u32[]{:S(2)}, u32[]{:S(2)}) collective-permute-start(bf16[2048,128]{1,0:T(8,128)(2,1)} %refs_1_.3), channel_id=1, source_target_pairs={{0,1},{1,0},{2,3},{3,2},{4,5},{5,4},{6,7},{7,6},{8,9},{9,8},{10,11... | collective-permute-start | bytes 1572872 | tf_op jit(solution)/shard_map/ppermute | solution.py:20
  3.4 9.7 %collective-permute-start.2 = (bf16[1024,128]{1,0:T(8,128)(2,1)S(1)}, bf16[1024,128]{1,0:T(8,128)(2,1)S(1)}, u32[]{:S(2)}, u32[]{:S(2)}) collective-permute-start(bf16[1024,128]{1,0:T(8,128)(2,1)S(1)} %get-tuple-element.48), channel_id=1, source_target_pairs={{0,2},{2,0},{1,3},{3,1},{4,6},{6,4},{5,7},{7,5},{8,10},{10,8},{9,1... | collective-permute-start | bytes 786440 | tf_op jit(solution)/shard_map/ppermute | solution.py:20
  11.2 7.7 %collective-permute-start.4 = (bf16[1088,128]{1,0:T(8,128)(2,1)S(1)}, bf16[1088,128]{1,0:T(8,128)(2,1)S(1)}, u32[]{:S(2)}, u32[]{:S(2)}) collective-permute-start(bf16[1088,128]{1,0:T(8,128)(2,1)S(1)} %shard_map.42), channel_id=1, source_target_pairs={{0,2},{2,0},{1,3},{3,1},{4,6},{6,4},{5,7},{7,5},{8,10},{10,8},{9,1... | collective-permute-start | bytes 835592 | tf_op jit(solution)/shard_map/ppermute | solution.py:20
  19.4 10.0 %collective-permute-start.13 = (f32[2,80,128]{2,1,0:T(8,128)S(1)}, f32[2,80,128]{2,1,0:T(8,128)S(1)}, u32[]{:S(2)}, u32[]{:S(2)}) collective-permute-start(f32[2,80,128]{2,1,0:T(8,128)S(1)} %get-tuple-element.95), channel_id=1, source_target_pairs={{0,24},{8,0},{16,8},{24,16},{1,25},{9,1},{17,9},{25,17},{2,26},{10... | collective-permute-start | bytes 245768 | tf_op jit(solution)/shard_map/ppermute | solution.py:446
  25.6 5.6 %collective-permute-start.9 = (f32[4,64,128]{2,1,0:T(8,128)S(1)}, f32[4,64,128]{2,1,0:T(8,128)S(1)}, u32[]{:S(2)}, u32[]{:S(2)}) collective-permute-start(f32[4,64,128]{2,1,0:T(8,128)S(1)} %get-tuple-element.56), channel_id=1, source_target_pairs={{0,2},{2,0},{1,3},{3,1},{4,6},{6,4},{5,7},{7,5},{8,10},{10,8},{9,1... | collective-permute-start | bytes 393224 | tf_op jit(solution)/shard_map/ppermute | solution.py:20
  26.2 6.4 %collective-permute-start.10 = (f32[4,64,128]{2,1,0:T(8,128)S(1)}, f32[4,64,128]{2,1,0:T(8,128)S(1)}, u32[]{:S(2)}, u32[]{:S(2)}) collective-permute-start(f32[4,64,128]{2,1,0:T(8,128)S(1)} %get-tuple-element.57), channel_id=1, source_target_pairs={{0,4},{4,0},{1,5},{5,1},{2,6},{6,2},{3,7},{7,3},{8,12},{12,8},{9,1... | collective-permute-start | bytes 393224 | tf_op jit(solution)/shard_map/ppermute | solution.py:20
  27.6 7.1 %collective-permute-start.11 = (f32[4,64,128]{2,1,0:T(8,128)S(1)}, f32[4,64,128]{2,1,0:T(8,128)S(1)}, u32[]{:S(2)}, u32[]{:S(2)}) collective-permute-start(f32[4,64,128]{2,1,0:T(8,128)S(1)} %get-tuple-element.58), channel_id=1, source_target_pairs={{0,6},{2,4},{4,2},{6,0},{1,7},{3,5},{5,3},{7,1},{8,14},{10,12},{12... | collective-permute-start | bytes 393224 | tf_op jit(solution)/shard_map/ppermute | solution.py:451
  29.1 6.8 %collective-permute-start.12 = (f32[2,80,128]{2,1,0:T(8,128)S(1)}, f32[2,80,128]{2,1,0:T(8,128)S(1)}, u32[]{:S(2)}, u32[]{:S(2)}) collective-permute-start(f32[2,80,128]{2,1,0:T(8,128)S(1)} %get-tuple-element.96), channel_id=1, source_target_pairs={{0,16},{8,24},{16,0},{24,8},{1,17},{9,25},{17,1},{25,9},{2,18},{10... | collective-permute-start | bytes 245768 | tf_op jit(solution)/shard_map/ppermute | solution.py:446
  29.5 6.5 %collective-permute-start.8 = (f32[2,80,128]{2,1,0:T(8,128)S(1)}, f32[2,80,128]{2,1,0:T(8,128)S(1)}, u32[]{:S(2)}, u32[]{:S(2)}) collective-permute-start(f32[2,80,128]{2,1,0:T(8,128)S(1)} %get-tuple-element.94), channel_id=1, source_target_pairs={{0,8},{8,16},{16,24},{24,0},{1,9},{9,17},{17,25},{25,1},{2,10},{10... | collective-permute-start | bytes 245768 | tf_op jit(solution)/shard_map/ppermute | solution.py:446
  36.0 5.7 %collective-permute-start.17 = (f32[64,128]{1,0:T(8,128)S(1)}, f32[64,128]{1,0:T(8,128)S(1)}, u32[]{:S(2)}, u32[]{:S(2)}) collective-permute-start(f32[64,128]{1,0:T(8,128)S(1)} %get-tuple-element.98), channel_id=1, source_target_pairs={{0,24},{8,0},{16,8},{24,16},{1,25},{9,1},{17,9},{25,17},{2,26},{10... | collective-permute-start | bytes 98312 | tf_op jit(solution)/shard_map/ppermute | solution.py:446
  37.7 5.7 %collective-permute-start.15 = (f32[64,128]{1,0:T(8,128)S(1)}, f32[64,128]{1,0:T(8,128)S(1)}, u32[]{:S(2)}, u32[]{:S(2)}) collective-permute-start(f32[64,128]{1,0:T(8,128)S(1)} %get-tuple-element.97), channel_id=1, source_target_pairs={{0,8},{8,16},{16,24},{24,0},{1,9},{9,17},{17,25},{25,1},{2,10},{10... | collective-permute-start | bytes 98312 | tf_op jit(solution)/shard_map/ppermute | solution.py:446
  40.6 12.4 %collective-permute-start.21 = (bf16[2,1024,128]{2,1,0:T(8,128)(2,1)S(1)}, bf16[2,1024,128]{2,1,0:T(8,128)(2,1)S(1)}, u32[]{:S(2)}, u32[]{:S(2)}) collective-permute-start(bf16[2,1024,128]{2,1,0:T(8,128)(2,1)S(1)} %get-tuple-element.65), channel_id=1, source_target_pairs={{0,2},{2,0},{1,3},{3,1},{4,6},{6,4},{5,7},{7,5},{8,10},{10,8},{9,1... | collective-permute-start | bytes 1572872 | tf_op jit(solution)/shard_map/ppermute | solution.py:20
  43.8 5.5 %collective-permute-start.20 = (f32[152,128]{1,0:T(8,128)S(1)}, f32[152,128]{1,0:T(8,128)S(1)}, u32[]{:S(2)}, u32[]{:S(2)}) collective-permute-start(f32[152,128]{1,0:T(8,128)S(1)} %constant_dynamic-update-slice_fusion), channel_id=1, source_target_pairs={{0,24},{8,0},{16,8},{24,16},{1,25},{9,1},{17,9},{25,17},{2,26},{10... | collective-permute-start | bytes 233480 | tf_op jit(solution)/shard_map/ppermute | solution.py:446
  45.7 5.7 %collective-permute-start.19 = (f32[152,128]{1,0:T(8,128)S(1)}, f32[152,128]{1,0:T(8,128)S(1)}, u32[]{:S(2)}, u32[]{:S(2)}) collective-permute-start(f32[152,128]{1,0:T(8,128)S(1)} %constant_dynamic-update-slice_fusion), channel_id=1, source_target_pairs={{0,16},{8,24},{16,0},{24,8},{1,17},{9,25},{17,1},{25,9},{2,18},{10... | collective-permute-start | bytes 233480 | tf_op jit(solution)/shard_map/ppermute | solution.py:446
  46.8 6.2 %collective-permute-start.18 = (f32[152,128]{1,0:T(8,128)S(1)}, f32[152,128]{1,0:T(8,128)S(1)}, u32[]{:S(2)}, u32[]{:S(2)}) collective-permute-start(f32[152,128]{1,0:T(8,128)S(1)} %constant_dynamic-update-slice_fusion), channel_id=1, source_target_pairs={{0,8},{8,16},{16,24},{24,0},{1,9},{9,17},{17,25},{25,1},{2,10},{10... | collective-permute-start | bytes 233480 | tf_op jit(solution)/shard_map/ppermute | solution.py:446
  53.0 7.9 %collective-permute-start.22 = (f32[4,80,128]{2,1,0:T(8,128)S(1)}, f32[4,80,128]{2,1,0:T(8,128)S(1)}, u32[]{:S(2)}, u32[]{:S(2)}) collective-permute-start(f32[4,80,128]{2,1,0:T(8,128)S(1)} %pad_maximum_fusion.2.refs_0_), channel_id=1, source_target_pairs={{0,2},{2,0},{1,3},{3,1},{4,6},{6,4},{5,7},{7,5},{8,10},{10,8},{9,1... | collective-permute-start | bytes 491528 | tf_op jit(solution)/shard_map/ppermute | solution.py:20
  53.8 10.7 %collective-permute-start.26 = (f32[4,80,128]{2,1,0:T(8,128)S(1)}, f32[4,80,128]{2,1,0:T(8,128)S(1)}, u32[]{:S(2)}, u32[]{:S(2)}) collective-permute-start(f32[4,80,128]{2,1,0:T(8,128)S(1)} %pad_maximum_fusion.2.refs_0_), channel_id=1, source_target_pairs={{0,4},{4,0},{1,5},{5,1},{2,6},{6,2},{3,7},{7,3},{8,12},{12,8},{9,1... | collective-permute-start | bytes 491528 | tf_op jit(solution)/shard_map/ppermute | solution.py:20
  55.1 9.4 %collective-permute-start.27 = (f32[4,80,128]{2,1,0:T(8,128)S(1)}, f32[4,80,128]{2,1,0:T(8,128)S(1)}, u32[]{:S(2)}, u32[]{:S(2)}) collective-permute-start(f32[4,80,128]{2,1,0:T(8,128)S(1)} %pad_maximum_fusion.2.refs_0_), channel_id=1, source_target_pairs={{0,6},{2,4},{4,2},{6,0},{1,7},{3,5},{5,3},{7,1},{8,14},{10,12},{12... | collective-permute-start | bytes 491528 | tf_op jit(solution)/shard_map/ppermute | solution.py:451
  61.0 7.8 %collective-permute-start.25 = (f32[4,72,128]{2,1,0:T(8,128)S(1)}, f32[4,72,128]{2,1,0:T(8,128)S(1)}, u32[]{:S(2)}, u32[]{:S(2)}) collective-permute-start(f32[4,72,128]{2,1,0:T(8,128)S(1)} %pad_maximum_fusion.5), channel_id=1, source_target_pairs={{0,6},{2,4},{4,2},{6,0},{1,7},{3,5},{5,3},{7,1},{8,14},{10,12},{12... | collective-permute-start | bytes 442376 | tf_op jit(solution)/shard_map/ppermute | solution.py:451
  62.7 6.1 %collective-permute-start.24 = (f32[4,72,128]{2,1,0:T(8,128)S(1)}, f32[4,72,128]{2,1,0:T(8,128)S(1)}, u32[]{:S(2)}, u32[]{:S(2)}) collective-permute-start(f32[4,72,128]{2,1,0:T(8,128)S(1)} %pad_maximum_fusion.5), channel_id=1, source_target_pairs={{0,4},{4,0},{1,5},{5,1},{2,6},{6,2},{3,7},{7,3},{8,12},{12,8},{9,1... | collective-permute-start | bytes 442376 | tf_op jit(solution)/shard_map/ppermute | solution.py:20
  62.7 6.1 %collective-permute-start.23 = (f32[4,72,128]{2,1,0:T(8,128)S(1)}, f32[4,72,128]{2,1,0:T(8,128)S(1)}, u32[]{:S(2)}, u32[]{:S(2)}) collective-permute-start(f32[4,72,128]{2,1,0:T(8,128)S(1)} %pad_maximum_fusion.5), channel_id=1, source_target_pairs={{0,2},{2,0},{1,3},{3,1},{4,6},{6,4},{5,7},{7,5},{8,10},{10,8},{9,1... | collective-permute-start | bytes 442376 | tf_op jit(solution)/shard_map/ppermute | solution.py:20
  76.3 6.1 %collective-permute-start.30 = (f32[512,512]{1,0:T(8,128)S(1)}, f32[512,512]{1,0:T(8,128)S(1)}, u32[]{:S(2)}, u32[]{:S(2)}) collective-permute-start(f32[512,512]{1,0:T(8,128)S(1)} %get-tuple-element.76.own), channel_id=1, source_target_pairs={{0,1},{1,0},{2,3},{3,2},{4,5},{5,4},{6,7},{7,6},{8,9},{9,8},{10,11... | collective-permute-start | bytes 3145736 | tf_op jit(solution)/shard_map/ppermute | solution.py:20
  76.7 23.5 %collective-permute-start.40 = (bf16[2,1024,128]{2,1,0:T(8,128)(2,1)S(1)}, bf16[2,1024,128]{2,1,0:T(8,128)(2,1)S(1)}, u32[]{:S(2)}, u32[]{:S(2)}) collective-permute-start(bf16[2,1024,128]{2,1,0:T(8,128)(2,1)S(1)} %collective-permute-done.21.refs_4_), channel_id=1, source_target_pairs={{0,1},{1,0},{2,3},{3,2},{4,5},{5,4},{6,7},{7,6},{8,9},{9,8},{10,11... | collective-permute-start | bytes 1572872 | tf_op jit(solution)/shard_map/ppermute | solution.py:20
  78.8 7.0 %collective-permute-start.33 = (bf16[4,64,128]{2,1,0:T(8,128)(2,1)S(1)}, bf16[4,64,128]{2,1,0:T(8,128)(2,1)S(1)}, u32[]{:S(2)}, u32[]{:S(2)}) collective-permute-start(bf16[4,64,128]{2,1,0:T(8,128)(2,1)S(1)} %get-tuple-element.83), channel_id=1, source_target_pairs={{0,6},{2,4},{4,2},{6,0},{1,7},{3,5},{5,3},{7,1},{8,14},{10,12},{12... | collective-permute-start | bytes 196616 | tf_op jit(solution)/shard_map/ppermute | solution.py:451
  85.9 10.6 %collective-permute-start.36 = (bf16[4,64,128]{2,1,0:T(8,128)(2,1)S(1)}, bf16[4,64,128]{2,1,0:T(8,128)(2,1)S(1)}, u32[]{:S(2)}, u32[]{:S(2)}) collective-permute-start(bf16[4,64,128]{2,1,0:T(8,128)(2,1)S(1)} %add_convert_fusion), channel_id=1, source_target_pairs={{0,24},{8,0},{16,8},{24,16},{1,25},{9,1},{17,9},{25,17},{2,26},{10... | collective-permute-start | bytes 196616 | tf_op jit(solution)/shard_map/ppermute | solution.py:446
  87.6 9.0 %collective-permute-start.35 = (bf16[4,64,128]{2,1,0:T(8,128)(2,1)S(1)}, bf16[4,64,128]{2,1,0:T(8,128)(2,1)S(1)}, u32[]{:S(2)}, u32[]{:S(2)}) collective-permute-start(bf16[4,64,128]{2,1,0:T(8,128)(2,1)S(1)} %add_convert_fusion), channel_id=1, source_target_pairs={{0,16},{8,24},{16,0},{24,8},{1,17},{9,25},{17,1},{25,9},{2,18},{10... | collective-permute-start | bytes 196616 | tf_op jit(solution)/shard_map/ppermute | solution.py:446
  88.9 7.7 %collective-permute-start.34 = (bf16[4,64,128]{2,1,0:T(8,128)(2,1)S(1)}, bf16[4,64,128]{2,1,0:T(8,128)(2,1)S(1)}, u32[]{:S(2)}, u32[]{:S(2)}) collective-permute-start(bf16[4,64,128]{2,1,0:T(8,128)(2,1)S(1)} %add_convert_fusion), channel_id=1, source_target_pairs={{0,8},{8,16},{16,24},{24,0},{1,9},{9,17},{17,25},{25,1},{2,10},{10... | collective-permute-start | bytes 196616 | tf_op jit(solution)/shard_map/ppermute | solution.py:446
  96.5 11.8 %collective-permute-start.42 = (bf16[2,512,512]{2,1,0:T(8,128)(2,1)S(1)}, bf16[2,512,512]{2,1,0:T(8,128)(2,1)S(1)}, u32[]{:S(2)}, u32[]{:S(2)}) collective-permute-start(bf16[2,512,512]{2,1,0:T(8,128)(2,1)S(1)} %shard_map.51.inv), channel_id=1, source_target_pairs={{0,1},{1,0},{2,3},{3,2},{4,5},{5,4},{6,7},{7,6},{8,9},{9,8},{10,11... | collective-permute-start | bytes 3145736 | tf_op jit(solution)/shard_map/ppermute | solution.py:20
  96.7 7.3 %collective-permute-start.39 = (f32[4,64,128]{2,1,0:T(8,128)S(1)}, f32[4,64,128]{2,1,0:T(8,128)S(1)}, u32[]{:S(2)}, u32[]{:S(2)}) collective-permute-start(f32[4,64,128]{2,1,0:T(8,128)S(1)} %convert_add_fusion), channel_id=1, source_target_pairs={{0,6},{2,4},{4,2},{6,0},{1,7},{3,5},{5,3},{7,1},{8,14},{10,12},{12... | collective-permute-start | bytes 393224 | tf_op jit(solution)/shard_map/ppermute | solution.py:451
  97.9 8.2 %collective-permute-start.38 = (f32[4,64,128]{2,1,0:T(8,128)S(1)}, f32[4,64,128]{2,1,0:T(8,128)S(1)}, u32[]{:S(2)}, u32[]{:S(2)}) collective-permute-start(f32[4,64,128]{2,1,0:T(8,128)S(1)} %convert_add_fusion), channel_id=1, source_target_pairs={{0,4},{4,0},{1,5},{5,1},{2,6},{6,2},{3,7},{7,3},{8,12},{12,8},{9,1... | collective-permute-start | bytes 393224 | tf_op jit(solution)/shard_map/ppermute | solution.py:20
  99.4 6.9 %collective-permute-start.37 = (f32[4,64,128]{2,1,0:T(8,128)S(1)}, f32[4,64,128]{2,1,0:T(8,128)S(1)}, u32[]{:S(2)}, u32[]{:S(2)}) collective-permute-start(f32[4,64,128]{2,1,0:T(8,128)S(1)} %convert_add_fusion), channel_id=1, source_target_pairs={{0,2},{2,0},{1,3},{3,1},{4,6},{6,4},{5,7},{7,5},{8,10},{10,8},{9,1... | collective-permute-start | bytes 393224 | tf_op jit(solution)/shard_map/ppermute | solution.py:20
  (15 other events, 61.1 us)

commit v6 on v5

--- a/solution.py
+++ b/solution.py
@@ -314,14 +314,34 @@
             out[...] = (-value).astype(BF16)
 
 
-def update_cross_kernel(each, here, shifted, edges, ours, theirs, out, late, *refs):
+def update_own_kernel(here, shifted, ours, out):
+    core = lax.axis_index("core")
+    for chosen, base, signal in ((0, shifted, here.at[0]), (1, here.at[0], shifted)):
+
+        @pl.when(core == chosen)
+        def _():
+            for r in range(0, out.shape[0], 256):
+                rows = slice(r, r + 256)
+                out[rows] = (base[rows].astype(F32) + dot_last(signal[rows], ours[...])).astype(BF16)
+
+
+def update_cross_kernel(each, here, shifted, done, edges, ours, theirs, out, late, *refs):
     packed, (refl, ahead, flat) = refs[:4], refs[4:]
+    core = lax.axis_index("core")
     by_kind(ours, theirs, refl)
     update_edge(edges.at[lax.axis_index("y")], refl, ahead)
-    update(here, shifted, refl, out)
+    out[1 - core] = done[...]
+    for chosen, base, signal in ((1, shifted, here.at[0]), (0, here.at[0], shifted)):
+
+        @pl.when(core == chosen)
+        def _():
+            for r in range(0, out.shape[1], 256):
+                rows = slice(r, r + 256)
+                out[chosen, rows] = (base[rows].astype(F32) + dot_last(signal[rows], theirs[...])).astype(BF16)
+
     delay(out.at[1], ahead, late)
     channels = here.shape[2]
-    value = dot_first(out[0, :, at(lax.axis_index("core"), channels // 2)], late[...])
+    value = dot_first(out[0, :, at(core, channels // 2)], late[...])
     emit([value[:, j : j + LANES] for j in range(0, channels, LANES)], flat, packed, 0, each, turned=False)
 
 
@@ -374,7 +394,7 @@
     scale[...] = jnp.broadcast_to(factor, scale.shape)
 
 
-def begin_kernel(stop, matrix, scale, error, iterate, *tables):
+def second_inverse_kernel(matrix, scale, out, *tables):
     errors, highs, lows, its, ihighs, ilows = tables
     channels = matrix.shape[0]
     factor = scale[0:1, 0:1]
@@ -387,8 +407,11 @@
         shape = (step, channels)
         eye = lax.broadcasted_iota(jnp.int32, shape, 0) + r == lax.broadcasted_iota(jnp.int32, shape, 1)
         put(its, ihighs, ilows, 1, rows, every, jnp.where(eye, 2.0, 0.0) - value)
-    steps(0, stop, *tables, None)
-    error[...], iterate[...] = errors[stop % 2], its[stop % 2]
+
+    def finish(rows, cols, value):
+        out[0, rows, cols], out[1, rows, cols] = halves(value * factor)
+
+    steps(0, NSTEPS, *tables, finish)
 
 
 def finish_kernel(start, error, iterate, scale, out, *tables):
@@ -553,12 +576,20 @@
         ours, theirs, inv,
     )
     refl_core = swap(refl, "core")
+    (done,) = call(
+        update_own_kernel,
+        [shape((half, channels), BF16)],
+        [],
+        2 * half * channels * channels,
+        here, shifted, refl,
+    )
+    refl_core = after(refl_core, done)
     here2, shifted2, *packed = call(
         kernel(update_cross_kernel, each),
         [shape((2, half, channels), BF16), shape((half, channels), BF16)] + [shape((depth, each, LANES), BF16)] * 4,
         [square16(2), pltpu.VMEM((16, channels), BF16), flat(parts * each)],
-        5 * half * channels * channels,
-        here, shifted, edges, refl, refl_core,
+        3 * half * channels * channels,
+        here, shifted, done, edges, refl, refl_core,
     )
     across2_core = swap(across2, "core")
     full_core = swap(after(full, refl_core), "core")
@@ -569,14 +600,13 @@
         18 * channels**3,
         after(full, packed[0]), full_core, cross, refl_core, last,
     )
-    error2, iterate2 = call(
-        kernel(begin_kernel, stop), state[:2], tables, 30 * channels**3, matrix2, scale2
-    )
     swapped = exchange(packed)
     swapped[0] = after(swapped[0], matrix2)
     wide = lambda pieces: sum((p.astype(F32) for p in pieces[1:]), pieces[0].astype(F32))
     column2 = wide(z_gather(wide(swapped).astype(BF16)))
-    inv2 = finish(error2, iterate2, scale2)
+    (inv2,) = call(
+        second_inverse_kernel, [shape((2, channels, channels), BF16)], tables, 60 * channels**3, matrix2, scale2
+    )
     inv2_core = swap(inv2, "core")
     there2, there_shifted2 = call(
         kernel(there_kernel, width),

time: 112 us -> 111 us (level)
  no operation moved by 1% of the time
where the time goes in v6:
time: 111 us
  starting transfers between devices  46.4 us (42%)
  waiting for transfers between devices  31.1 us (28%)
  Pallas kernels  29.7 us (27%)
  local copies, waits for them, and re-layouts  2.14 us (2%)
    pallas_call x13, Pallas kernels, call(): pl.pallas_call(body, out_shape=shapes, in_specs=[pl.BlockSpec(memory_spac...  29.7 us
    ppermute x25, starting transfers between devices, swap(): return lax.ppermute(value, axis, [(0, 1), (1, 0)])  18 us
    ppermute x12, starting transfers between devices, ahead(): return lax.ppermute(piece, 'z', [(i, (i + by) % size) for i in range(size)])  17.3 us
    ppermute x25, waiting for transfers between devices, swap(): return lax.ppermute(value, axis, [(0, 1), (1, 0)])  17.2 us
    ppermute x12, waiting for transfers between devices, ahead(): return lax.ppermute(piece, 'z', [(i, (i + by) % size) for i in range(size)])  8.64 us
    ppermute x5, starting transfers between devices, exchange(): lax.ppermute(pieces[3], ('x', 'y'), both)  7.72 us
    ppermute x5, waiting for transfers between devices, exchange(): lax.ppermute(pieces[3], ('x', 'y'), both)  3.89 us
    ppermute x1, starting transfers between devices, from_behind(): return lax.ppermute(value, axes, [(i, i + 1) for i in range(devices - 1)])  3.38 us
  transfers between devices with their start and end apart: 43, of which 20 were waited for; matrix products, arithmetic and copies ran while one was open for 0% of the time, Pallas kernels for 23%

profile of v6, /device:TPU:0, one launch (start us, length us, event | category | flops | bytes accessed | tf_op | source)
XLA Modules:
  0.0 110.6 jit_solution(4350159961082140036)
XLA Ops:
  3.4 3.0 %collective-permute-start.2 = (bf16[1024,128]{1,0:T(8,128)(2,1)S(1)}, bf16[1024,128]{1,0:T(8,128)(2,1)S(1)}, u32[]{:S(2)}, u32[]{:S(2)}) collective-permute-start(bf16[1024,128]{1,0:T(8,128)(2,1)S(1)} %get-tuple-element.47), channel_id=1, source_target_pairs={{0,2},{2,0},{1,3},{3,1},{4,6},{6,4},{5,7},{7,5},{8,10},{10,8},{9,1... | collective-permute-start | bytes 786440 | tf_op jit(solution)/shard_map/ppermute | solution.py:20
  6.4 3.4 %collective-permute-start.3 = (bf16[2,16,128]{2,1,0:T(8,128)(2,1)S(1)}, bf16[2,16,128]{2,1,0:T(8,128)(2,1)S(1)}, u32[]{:S(2)}, u32[]{:S(2)}) collective-permute-start(bf16[2,16,128]{2,1,0:T(8,128)(2,1)S(1)} %get-tuple-element.48), channel_id=1, source_target_pairs={{0,4},{4,8},{8,12},{12,16},{16,20},{20,24},{24,28},{1,5},{5,9},{9,... | collective-permute-start | bytes 24584 | tf_op jit(solution)/shard_map/ppermute | solution.py:25
  9.8 1.3 %collective-permute-done.3.halo.refs_8_ = bf16[2,16,128]{2,1,0:T(8,128)(2,1)S(1)} collective-permute-done((bf16[2,16,128]{2,1,0:T(8,128)(2,1)S(1)}, bf16[2,16,128]{2,1,0:T(8,128)(2,1)S(1)}, u32[]{:S(2)}, u32[]{:S(2)}) %collective-permute-start.3) | collective-permute-done | bytes 8224 | tf_op jit(solution)/shard_map/ppermute | solution.py:25
  14.2 4.7 %collective-permute-done.4.refs_5_ = bf16[1088,128]{1,0:T(8,128)(2,1)S(1)} collective-permute-done((bf16[1088,128]{1,0:T(8,128)(2,1)S(1)}, bf16[1088,128]{1,0:T(8,128)(2,1)S(1)}, u32[]{:S(2)}, u32[]{:S(2)}) %collective-permute-start.4) | collective-permute-done | bytes 278560 | tf_op jit(solution)/shard_map/ppermute | solution.py:20
  19.4 4.9 %collective-permute-start.13 = (f32[2,80,128]{2,1,0:T(8,128)S(1)}, f32[2,80,128]{2,1,0:T(8,128)S(1)}, u32[]{:S(2)}, u32[]{:S(2)}) collective-permute-start(f32[2,80,128]{2,1,0:T(8,128)S(1)} %get-tuple-element.93), channel_id=1, source_target_pairs={{0,24},{8,0},{16,8},{24,16},{1,25},{9,1},{17,9},{25,17},{2,26},{10... | collective-permute-start | bytes 245768 | tf_op jit(solution)/shard_map/ppermute | solution.py:469
  26.2 1.5 %collective-permute-start.10 = (f32[4,64,128]{2,1,0:T(8,128)S(1)}, f32[4,64,128]{2,1,0:T(8,128)S(1)}, u32[]{:S(2)}, u32[]{:S(2)}) collective-permute-start(f32[4,64,128]{2,1,0:T(8,128)S(1)} %get-tuple-element.55), channel_id=1, source_target_pairs={{0,4},{4,0},{1,5},{5,1},{2,6},{6,2},{3,7},{7,3},{8,12},{12,8},{9,1... | collective-permute-start | bytes 393224 | tf_op jit(solution)/shard_map/ppermute | solution.py:20
  27.6 1.5 %collective-permute-start.11 = (f32[4,64,128]{2,1,0:T(8,128)S(1)}, f32[4,64,128]{2,1,0:T(8,128)S(1)}, u32[]{:S(2)}, u32[]{:S(2)}) collective-permute-start(f32[4,64,128]{2,1,0:T(8,128)S(1)} %get-tuple-element.56), channel_id=1, source_target_pairs={{0,6},{2,4},{4,2},{6,0},{1,7},{3,5},{5,3},{7,1},{8,14},{10,12},{12... | collective-permute-start | bytes 393224 | tf_op jit(solution)/shard_map/ppermute | solution.py:474
  29.5 1.6 %collective-permute-start.8 = (f32[2,80,128]{2,1,0:T(8,128)S(1)}, f32[2,80,128]{2,1,0:T(8,128)S(1)}, u32[]{:S(2)}, u32[]{:S(2)}) collective-permute-start(f32[2,80,128]{2,1,0:T(8,128)S(1)} %get-tuple-element.92), channel_id=1, source_target_pairs={{0,8},{8,16},{16,24},{24,0},{1,9},{9,17},{17,25},{25,1},{2,10},{10... | collective-permute-start | bytes 245768 | tf_op jit(solution)/shard_map/ppermute | solution.py:469
  32.5 2.2 %collective-permute-done.11 = f32[4,64,128]{2,1,0:T(8,128)S(1)} collective-permute-done((f32[4,64,128]{2,1,0:T(8,128)S(1)}, f32[4,64,128]{2,1,0:T(8,128)S(1)}, u32[]{:S(2)}, u32[]{:S(2)}) %collective-permute-start.11) | collective-permute-done | bytes 131104 | tf_op jit(solution)/shard_map/ppermute | solution.py:474
  36.0 1.6 %collective-permute-start.17 = (f32[64,128]{1,0:T(8,128)S(1)}, f32[64,128]{1,0:T(8,128)S(1)}, u32[]{:S(2)}, u32[]{:S(2)}) collective-permute-start(f32[64,128]{1,0:T(8,128)S(1)} %get-tuple-element.96), channel_id=1, source_target_pairs={{0,24},{8,0},{16,8},{24,16},{1,25},{9,1},{17,9},{25,17},{2,26},{10... | collective-permute-start | bytes 98312 | tf_op jit(solution)/shard_map/ppermute | solution.py:469
  37.7 1.9 %collective-permute-start.15 = (f32[64,128]{1,0:T(8,128)S(1)}, f32[64,128]{1,0:T(8,128)S(1)}, u32[]{:S(2)}, u32[]{:S(2)}) collective-permute-start(f32[64,128]{1,0:T(8,128)S(1)} %get-tuple-element.95), channel_id=1, source_target_pairs={{0,8},{8,16},{16,24},{24,0},{1,9},{9,17},{17,25},{25,1},{2,10},{10... | collective-permute-start | bytes 98312 | tf_op jit(solution)/shard_map/ppermute | solution.py:469
  43.8 1.9 %collective-permute-start.20 = (f32[152,128]{1,0:T(8,128)S(1)}, f32[152,128]{1,0:T(8,128)S(1)}, u32[]{:S(2)}, u32[]{:S(2)}) collective-permute-start(f32[152,128]{1,0:T(8,128)S(1)} %constant_dynamic-update-slice_fusion), channel_id=1, source_target_pairs={{0,24},{8,0},{16,8},{24,16},{1,25},{9,1},{17,9},{25,17},{2,26},{10... | collective-permute-start | bytes 233480 | tf_op jit(solution)/shard_map/ppermute | solution.py:469
  47.2 2.1 %collective-permute-done.20 = f32[152,128]{1,0:T(8,128)S(1)} collective-permute-done((f32[152,128]{1,0:T(8,128)S(1)}, f32[152,128]{1,0:T(8,128)S(1)}, u32[]{:S(2)}, u32[]{:S(2)}) %collective-permute-start.20) | collective-permute-done | bytes 77856 | tf_op jit(solution)/shard_map/ppermute | solution.py:469
  49.3 2.2 %collective-permute-done.19 = f32[152,128]{1,0:T(8,128)S(1)} collective-permute-done((f32[152,128]{1,0:T(8,128)S(1)}, f32[152,128]{1,0:T(8,128)S(1)}, u32[]{:S(2)}, u32[]{:S(2)}) %collective-permute-start.19) | collective-permute-done | bytes 77856 | tf_op jit(solution)/shard_map/ppermute | solution.py:469
  51.5 1.6 %collective-permute-done.18 = f32[152,128]{1,0:T(8,128)S(1)} collective-permute-done((f32[152,128]{1,0:T(8,128)S(1)}, f32[152,128]{1,0:T(8,128)S(1)}, u32[]{:S(2)}, u32[]{:S(2)}) %collective-permute-start.18) | collective-permute-done | bytes 77856 | tf_op jit(solution)/shard_map/ppermute | solution.py:469
  55.1 1.5 %collective-permute-start.27 = (f32[4,80,128]{2,1,0:T(8,128)S(1)}, f32[4,80,128]{2,1,0:T(8,128)S(1)}, u32[]{:S(2)}, u32[]{:S(2)}) collective-permute-start(f32[4,80,128]{2,1,0:T(8,128)S(1)} %pad_maximum_fusion.2.refs_0_), channel_id=1, source_target_pairs={{0,6},{2,4},{4,2},{6,0},{1,7},{3,5},{5,3},{7,1},{8,14},{10,12},{12... | collective-permute-start | bytes 491528 | tf_op jit(solution)/shard_map/ppermute | solution.py:474
  56.6 4.4 %collective-permute-done.22.refs_1_ = f32[4,80,128]{2,1,0:T(8,128)S(1)} collective-permute-done((f32[4,80,128]{2,1,0:T(8,128)S(1)}, f32[4,80,128]{2,1,0:T(8,128)S(1)}, u32[]{:S(2)}, u32[]{:S(2)}) %collective-permute-start.22) | collective-permute-done | bytes 163872 | tf_op jit(solution)/shard_map/ppermute | solution.py:20
  61.0 1.7 %collective-permute-start.25 = (f32[4,72,128]{2,1,0:T(8,128)S(1)}, f32[4,72,128]{2,1,0:T(8,128)S(1)}, u32[]{:S(2)}, u32[]{:S(2)}) collective-permute-start(f32[4,72,128]{2,1,0:T(8,128)S(1)} %pad_maximum_fusion.5), channel_id=1, source_target_pairs={{0,6},{2,4},{4,2},{6,0},{1,7},{3,5},{5,3},{7,1},{8,14},{10,12},{12... | collective-permute-start | bytes 442376 | tf_op jit(solution)/shard_map/ppermute | solution.py:474
  62.7 1.8 %collective-permute-start.23 = (f32[4,72,128]{2,1,0:T(8,128)S(1)}, f32[4,72,128]{2,1,0:T(8,128)S(1)}, u32[]{:S(2)}, u32[]{:S(2)}) collective-permute-start(f32[4,72,128]{2,1,0:T(8,128)S(1)} %pad_maximum_fusion.5), channel_id=1, source_target_pairs={{0,2},{2,0},{1,3},{3,1},{4,6},{6,4},{5,7},{7,5},{8,10},{10,8},{9,1... | collective-permute-start | bytes 442376 | tf_op jit(solution)/shard_map/ppermute | solution.py:20
  64.5 4.3 %shard_map.45 = (f32[512,512]{1,0:T(8,128)S(1)}, f32[512,512]{1,0:T(8,128)S(1)}, f32[512,512]{1,0:T(8,128)S(1)}, f32[8,128]{1,0:T(8,128)S(1)}) custom-call(f32[4,80,128]{2,1,0:T(8,128)S(1)} %pad_maximum_fusion.2.refs_0_, f32[4,80,128]{2,1,0:T(8,128)S(1)} %collective-permute-done.22.refs_1_, f32[4,80,128]{2,1,0:T(8,128)S(1)} %collective-permute-done.26.refs_2_, ...), custom_call_target="tpu_custom_call" | custom-call | flops 4026531840 | bytes 3805184 | tf_op jit(solution)/shard_map/pallas_call | solution.py:34
  69.0 3.8 %shard_map.46.inv = bf16[2,512,512]{2,1,0:T(8,128)(2,1)S(1)} custom-call(f32[512,512]{1,0:T(8,128)S(1)} %get-tuple-element.66.error, f32[512,512]{1,0:T(8,128)S(1)} %get-tuple-element.68.iterate, f32[8,128]{1,0:T(8,128)S(1)} %get-tuple-element.69.scale), custom_call_target="tpu_custom_call" | custom-call | flops 4026531840 | bytes 3149824 | tf_op jit(solution)/shard_map/pallas_call | solution.py:34
  72.8 1.4 %shard_map.47 = (bf16[512,512]{1,0:T(8,128)(2,1)S(1)}, f32[512,512]{1,0:T(8,128)S(1)}, f32[8,128]{1,0:T(8,128)S(1)}) custom-call(f32[4,4,72,128]{3,2,1,0:T(8,128)S(1)} %pad_maximum_fusion.ours, f32[4,4,72,128]{3,2,1,0:T(8,128)S(1)} %collective-permute-done.28.theirs, bf16[2,512,512]{2,1,0:T(8,128)(2,1)S(1)} %shard_map.46.inv), custom_call_target="tpu_custom_call" | custom-call | flops 805306368 | bytes 3805184 | tf_op jit(solution)/shard_map/pallas_call | solution.py:34
  76.8 1.9 %shard_map.49 = (bf16[2,1024,512]{2,1,0:T(8,128)(2,1)S(1)}, bf16[1024,512]{1,0:T(8,128)(2,1)S(1)}, bf16[4,64,128]{2,1,0:T(8,128)(2,1)S(1)}, bf16[4,64,128]{2,1,0...) custom-call(bf16[2,1024,512]{2,1,0:T(8,128)(2,1)S(1)} %get-tuple-element.52.here, ...), custom_call_target="tpu_custom_call" | custom-call | flops 805306368 | bytes 8716288 | tf_op jit(solution)/shard_map/pallas_call | solution.py:34
  78.7 1.8 %collective-permute-start.33 = (bf16[4,64,128]{2,1,0:T(8,128)(2,1)S(1)}, bf16[4,64,128]{2,1,0:T(8,128)(2,1)S(1)}, u32[]{:S(2)}, u32[]{:S(2)}) collective-permute-start(bf16[4,64,128]{2,1,0:T(8,128)(2,1)S(1)} %get-tuple-element.83), channel_id=1, source_target_pairs={{0,6},{2,4},{4,2},{6,0},{1,7},{3,5},{5,3},{7,1},{8,14},{10,12},{12... | collective-permute-start | bytes 196616 | tf_op jit(solution)/shard_map/ppermute | solution.py:474
  82.2 3.2 %shard_map.50 = (f32[512,512]{1,0:T(8,128)S(1)}, f32[8,128]{1,0:T(8,128)S(1)}) custom-call(f32[512,512]{1,0:T(8,128)S(1)} %get-tuple-element.76.own, f32[512,512]{1,0:T(8,128)S(1)} %collective-permute-done.30.other, f32[512,512]{1,0:T(8,128)S(1)} %get-tuple-element.77.cross, bf16[512,512]{1,0:T(8,128)(2,1)S(1)} %collective-permute-done.29.theirs.refs_8_, ...), custom_call_target="tpu_custom_call" | custom-call | flops 2415919104 | bytes 4726784 | tf_op jit(solution)/shard_map/pallas_call | solution.py:34
  85.5 1.8 %collective-permute-start.36 = (bf16[4,64,128]{2,1,0:T(8,128)(2,1)S(1)}, bf16[4,64,128]{2,1,0:T(8,128)(2,1)S(1)}, u32[]{:S(2)}, u32[]{:S(2)}) collective-permute-start(bf16[4,64,128]{2,1,0:T(8,128)(2,1)S(1)} %add_convert_fusion), channel_id=1, source_target_pairs={{0,24},{8,0},{16,8},{24,16},{1,25},{9,1},{17,9},{25,17},{2,26},{10... | collective-permute-start | bytes 196616 | tf_op jit(solution)/shard_map/ppermute | solution.py:469
  88.9 7.0 %shard_map.51.inv = bf16[2,512,512]{2,1,0:T(8,128)(2,1)S(1)} custom-call(f32[512,512]{1,0:T(8,128)S(1)} %get-tuple-element.79.matrix, f32[8,128]{1,0:T(8,128)S(1)} %get-tuple-element.84.scale), custom_call_target="tpu_custom_call" | custom-call | flops 8053063680 | bytes 2101248 | tf_op jit(solution)/shard_map/pallas_call | solution.py:34
  99.7 2.0 %shard_map.52 = (bf16[2,1024,512]{2,1,0:T(8,128)(2,1)S(1)}, bf16[1024,512]{1,0:T(8,128)(2,1)S(1)}) custom-call(bf16[2048,128]{1,0:T(8,128)(2,1)S(1)} %copy-done.1, bf16[2048,128]{1,0:T(8,128)(2,1)S(1)} %copy-done.3, bf16[2048,128]{1,0:T(8,128)(2,1)S(1)} %collective-permute-done.forward_core.refs_2_, ...), custom_call_target="tpu_custom_call" | custom-call | flops 1073741824 | bytes 7405568 | tf_op jit(solution)/shard_map/pallas_call | solution.py:34
  101.7 1.6 %collective-permute-done.39 = f32[4,64,128]{2,1,0:T(8,128)S(1)} collective-permute-done((f32[4,64,128]{2,1,0:T(8,128)S(1)}, f32[4,64,128]{2,1,0:T(8,128)S(1)}, u32[]{:S(2)}, u32[]{:S(2)}) %collective-permute-start.39) | collective-permute-done | bytes 131104 | tf_op jit(solution)/shard_map/ppermute | solution.py:474
  103.4 1.9 %collective-permute-done.38 = f32[4,64,128]{2,1,0:T(8,128)S(1)} collective-permute-done((f32[4,64,128]{2,1,0:T(8,128)S(1)}, f32[4,64,128]{2,1,0:T(8,128)S(1)}, u32[]{:S(2)}, u32[]{:S(2)}) %collective-permute-start.38) | collective-permute-done | bytes 131104 | tf_op jit(solution)/shard_map/ppermute | solution.py:20
  105.9 1.9 %collective-permute-done.41.theirs = f32[4,4,64,128]{3,2,1,0:T(8,128)S(1)} collective-permute-done((f32[4,4,64,128]{3,2,1,0:T(8,128)S(1)}, f32[4,4,64,128]{3,2,1,0:T(8,128)S(1)}, u32[]{:S(2)}, u32[]{:S(2)}) %collective-permute-start.41) | collective-permute-done | bytes 524320 | tf_op jit(solution)/shard_map/ppermute | solution.py:20
  107.8 2.8 %shard_map.53 = (bf16[2048,128]{1,0:T(8,128)(2,1)}, bf16[2048,128]{1,0:T(8,128)(2,1)}) custom-call(f32[4,4,64,128]{3,2,1,0:T(8,128)S(1)} %pad_maximum_fusion.1.ours, f32[4,4,64,128]{3,2,1,0:T(8,128)S(1)} %collective-permute-done.41.theirs, bf16[2,512,512]{2,1,0:T(8,128)(2,1)S(1)} %shard_map.51.inv, ...), custom_call_target="tpu_custom_call" | custom-call | flops 536870912 | bytes 10485760 | tf_op jit(solution)/shard_map/pallas_call | solution.py:34
  (93 shorter events, 29.3 us)
Async XLA Ops:
  0.6 12.4 %collective-permute-start = (bf16[2048,128]{1,0:T(8,128)(2,1)}, bf16[2048,128]{1,0:T(8,128)(2,1)S(1)}, u32[]{:S(2)}, u32[]{:S(2)}) collective-permute-start(bf16[2048,128]{1,0:T(8,128)(2,1)} %refs_0_.3), channel_id=1, source_target_pairs={{0,1},{1,0},{2,3},{3,2},{4,5},{5,4},{6,7},{7,6},{8,9},{9,8},{10,11... | collective-permute-start | bytes 1572872 | tf_op jit(solution)/shard_map/ppermute | solution.py:20
  1.1 11.9 %collective-permute-start.1 = (bf16[2048,128]{1,0:T(8,128)(2,1)}, bf16[2048,128]{1,0:T(8,128)(2,1)S(1)}, u32[]{:S(2)}, u32[]{:S(2)}) collective-permute-start(bf16[2048,128]{1,0:T(8,128)(2,1)} %refs_1_.3), channel_id=1, source_target_pairs={{0,1},{1,0},{2,3},{3,2},{4,5},{5,4},{6,7},{7,6},{8,9},{9,8},{10,11... | collective-permute-start | bytes 1572872 | tf_op jit(solution)/shard_map/ppermute | solution.py:20
  3.4 9.7 %collective-permute-start.2 = (bf16[1024,128]{1,0:T(8,128)(2,1)S(1)}, bf16[1024,128]{1,0:T(8,128)(2,1)S(1)}, u32[]{:S(2)}, u32[]{:S(2)}) collective-permute-start(bf16[1024,128]{1,0:T(8,128)(2,1)S(1)} %get-tuple-element.47), channel_id=1, source_target_pairs={{0,2},{2,0},{1,3},{3,1},{4,6},{6,4},{5,7},{7,5},{8,10},{10,8},{9,1... | collective-permute-start | bytes 786440 | tf_op jit(solution)/shard_map/ppermute | solution.py:20
  11.2 7.7 %collective-permute-start.4 = (bf16[1088,128]{1,0:T(8,128)(2,1)S(1)}, bf16[1088,128]{1,0:T(8,128)(2,1)S(1)}, u32[]{:S(2)}, u32[]{:S(2)}) collective-permute-start(bf16[1088,128]{1,0:T(8,128)(2,1)S(1)} %shard_map.42), channel_id=1, source_target_pairs={{0,2},{2,0},{1,3},{3,1},{4,6},{6,4},{5,7},{7,5},{8,10},{10,8},{9,1... | collective-permute-start | bytes 835592 | tf_op jit(solution)/shard_map/ppermute | solution.py:20
  19.4 10.0 %collective-permute-start.13 = (f32[2,80,128]{2,1,0:T(8,128)S(1)}, f32[2,80,128]{2,1,0:T(8,128)S(1)}, u32[]{:S(2)}, u32[]{:S(2)}) collective-permute-start(f32[2,80,128]{2,1,0:T(8,128)S(1)} %get-tuple-element.93), channel_id=1, source_target_pairs={{0,24},{8,0},{16,8},{24,16},{1,25},{9,1},{17,9},{25,17},{2,26},{10... | collective-permute-start | bytes 245768 | tf_op jit(solution)/shard_map/ppermute | solution.py:469
  25.6 5.6 %collective-permute-start.9 = (f32[4,64,128]{2,1,0:T(8,128)S(1)}, f32[4,64,128]{2,1,0:T(8,128)S(1)}, u32[]{:S(2)}, u32[]{:S(2)}) collective-permute-start(f32[4,64,128]{2,1,0:T(8,128)S(1)} %get-tuple-element.54), channel_id=1, source_target_pairs={{0,2},{2,0},{1,3},{3,1},{4,6},{6,4},{5,7},{7,5},{8,10},{10,8},{9,1... | collective-permute-start | bytes 393224 | tf_op jit(solution)/shard_map/ppermute | solution.py:20
  26.2 6.4 %collective-permute-start.10 = (f32[4,64,128]{2,1,0:T(8,128)S(1)}, f32[4,64,128]{2,1,0:T(8,128)S(1)}, u32[]{:S(2)}, u32[]{:S(2)}) collective-permute-start(f32[4,64,128]{2,1,0:T(8,128)S(1)} %get-tuple-element.55), channel_id=1, source_target_pairs={{0,4},{4,0},{1,5},{5,1},{2,6},{6,2},{3,7},{7,3},{8,12},{12,8},{9,1... | collective-permute-start | bytes 393224 | tf_op jit(solution)/shard_map/ppermute | solution.py:20
  27.6 7.1 %collective-permute-start.11 = (f32[4,64,128]{2,1,0:T(8,128)S(1)}, f32[4,64,128]{2,1,0:T(8,128)S(1)}, u32[]{:S(2)}, u32[]{:S(2)}) collective-permute-start(f32[4,64,128]{2,1,0:T(8,128)S(1)} %get-tuple-element.56), channel_id=1, source_target_pairs={{0,6},{2,4},{4,2},{6,0},{1,7},{3,5},{5,3},{7,1},{8,14},{10,12},{12... | collective-permute-start | bytes 393224 | tf_op jit(solution)/shard_map/ppermute | solution.py:474
  29.1 6.8 %collective-permute-start.12 = (f32[2,80,128]{2,1,0:T(8,128)S(1)}, f32[2,80,128]{2,1,0:T(8,128)S(1)}, u32[]{:S(2)}, u32[]{:S(2)}) collective-permute-start(f32[2,80,128]{2,1,0:T(8,128)S(1)} %get-tuple-element.94), channel_id=1, source_target_pairs={{0,16},{8,24},{16,0},{24,8},{1,17},{9,25},{17,1},{25,9},{2,18},{10... | collective-permute-start | bytes 245768 | tf_op jit(solution)/shard_map/ppermute | solution.py:469
  29.5 6.5 %collective-permute-start.8 = (f32[2,80,128]{2,1,0:T(8,128)S(1)}, f32[2,80,128]{2,1,0:T(8,128)S(1)}, u32[]{:S(2)}, u32[]{:S(2)}) collective-permute-start(f32[2,80,128]{2,1,0:T(8,128)S(1)} %get-tuple-element.92), channel_id=1, source_target_pairs={{0,8},{8,16},{16,24},{24,0},{1,9},{9,17},{17,25},{25,1},{2,10},{10... | collective-permute-start | bytes 245768 | tf_op jit(solution)/shard_map/ppermute | solution.py:469
  36.0 5.7 %collective-permute-start.17 = (f32[64,128]{1,0:T(8,128)S(1)}, f32[64,128]{1,0:T(8,128)S(1)}, u32[]{:S(2)}, u32[]{:S(2)}) collective-permute-start(f32[64,128]{1,0:T(8,128)S(1)} %get-tuple-element.96), channel_id=1, source_target_pairs={{0,24},{8,0},{16,8},{24,16},{1,25},{9,1},{17,9},{25,17},{2,26},{10... | collective-permute-start | bytes 98312 | tf_op jit(solution)/shard_map/ppermute | solution.py:469
  37.7 5.7 %collective-permute-start.15 = (f32[64,128]{1,0:T(8,128)S(1)}, f32[64,128]{1,0:T(8,128)S(1)}, u32[]{:S(2)}, u32[]{:S(2)}) collective-permute-start(f32[64,128]{1,0:T(8,128)S(1)} %get-tuple-element.95), channel_id=1, source_target_pairs={{0,8},{8,16},{16,24},{24,0},{1,9},{9,17},{17,25},{25,1},{2,10},{10... | collective-permute-start | bytes 98312 | tf_op jit(solution)/shard_map/ppermute | solution.py:469
  40.6 12.4 %collective-permute-start.21 = (bf16[2,1024,128]{2,1,0:T(8,128)(2,1)S(1)}, bf16[2,1024,128]{2,1,0:T(8,128)(2,1)S(1)}, u32[]{:S(2)}, u32[]{:S(2)}) collective-permute-start(bf16[2,1024,128]{2,1,0:T(8,128)(2,1)S(1)} %get-tuple-element.63), channel_id=1, source_target_pairs={{0,2},{2,0},{1,3},{3,1},{4,6},{6,4},{5,7},{7,5},{8,10},{10,8},{9,1... | collective-permute-start | bytes 1572872 | tf_op jit(solution)/shard_map/ppermute | solution.py:20
  43.8 5.5 %collective-permute-start.20 = (f32[152,128]{1,0:T(8,128)S(1)}, f32[152,128]{1,0:T(8,128)S(1)}, u32[]{:S(2)}, u32[]{:S(2)}) collective-permute-start(f32[152,128]{1,0:T(8,128)S(1)} %constant_dynamic-update-slice_fusion), channel_id=1, source_target_pairs={{0,24},{8,0},{16,8},{24,16},{1,25},{9,1},{17,9},{25,17},{2,26},{10... | collective-permute-start | bytes 233480 | tf_op jit(solution)/shard_map/ppermute | solution.py:469
  45.7 5.7 %collective-permute-start.19 = (f32[152,128]{1,0:T(8,128)S(1)}, f32[152,128]{1,0:T(8,128)S(1)}, u32[]{:S(2)}, u32[]{:S(2)}) collective-permute-start(f32[152,128]{1,0:T(8,128)S(1)} %constant_dynamic-update-slice_fusion), channel_id=1, source_target_pairs={{0,16},{8,24},{16,0},{24,8},{1,17},{9,25},{17,1},{25,9},{2,18},{10... | collective-permute-start | bytes 233480 | tf_op jit(solution)/shard_map/ppermute | solution.py:469
  46.8 6.2 %collective-permute-start.18 = (f32[152,128]{1,0:T(8,128)S(1)}, f32[152,128]{1,0:T(8,128)S(1)}, u32[]{:S(2)}, u32[]{:S(2)}) collective-permute-start(f32[152,128]{1,0:T(8,128)S(1)} %constant_dynamic-update-slice_fusion), channel_id=1, source_target_pairs={{0,8},{8,16},{16,24},{24,0},{1,9},{9,17},{17,25},{25,1},{2,10},{10... | collective-permute-start | bytes 233480 | tf_op jit(solution)/shard_map/ppermute | solution.py:469
  53.0 7.9 %collective-permute-start.22 = (f32[4,80,128]{2,1,0:T(8,128)S(1)}, f32[4,80,128]{2,1,0:T(8,128)S(1)}, u32[]{:S(2)}, u32[]{:S(2)}) collective-permute-start(f32[4,80,128]{2,1,0:T(8,128)S(1)} %pad_maximum_fusion.2.refs_0_), channel_id=1, source_target_pairs={{0,2},{2,0},{1,3},{3,1},{4,6},{6,4},{5,7},{7,5},{8,10},{10,8},{9,1... | collective-permute-start | bytes 491528 | tf_op jit(solution)/shard_map/ppermute | solution.py:20
  53.8 10.6 %collective-permute-start.26 = (f32[4,80,128]{2,1,0:T(8,128)S(1)}, f32[4,80,128]{2,1,0:T(8,128)S(1)}, u32[]{:S(2)}, u32[]{:S(2)}) collective-permute-start(f32[4,80,128]{2,1,0:T(8,128)S(1)} %pad_maximum_fusion.2.refs_0_), channel_id=1, source_target_pairs={{0,4},{4,0},{1,5},{5,1},{2,6},{6,2},{3,7},{7,3},{8,12},{12,8},{9,1... | collective-permute-start | bytes 491528 | tf_op jit(solution)/shard_map/ppermute | solution.py:20
  55.1 9.4 %collective-permute-start.27 = (f32[4,80,128]{2,1,0:T(8,128)S(1)}, f32[4,80,128]{2,1,0:T(8,128)S(1)}, u32[]{:S(2)}, u32[]{:S(2)}) collective-permute-start(f32[4,80,128]{2,1,0:T(8,128)S(1)} %pad_maximum_fusion.2.refs_0_), channel_id=1, source_target_pairs={{0,6},{2,4},{4,2},{6,0},{1,7},{3,5},{5,3},{7,1},{8,14},{10,12},{12... | collective-permute-start | bytes 491528 | tf_op jit(solution)/shard_map/ppermute | solution.py:474
  61.0 7.8 %collective-permute-start.25 = (f32[4,72,128]{2,1,0:T(8,128)S(1)}, f32[4,72,128]{2,1,0:T(8,128)S(1)}, u32[]{:S(2)}, u32[]{:S(2)}) collective-permute-start(f32[4,72,128]{2,1,0:T(8,128)S(1)} %pad_maximum_fusion.5), channel_id=1, source_target_pairs={{0,6},{2,4},{4,2},{6,0},{1,7},{3,5},{5,3},{7,1},{8,14},{10,12},{12... | collective-permute-start | bytes 442376 | tf_op jit(solution)/shard_map/ppermute | solution.py:474
  62.7 6.1 %collective-permute-start.24 = (f32[4,72,128]{2,1,0:T(8,128)S(1)}, f32[4,72,128]{2,1,0:T(8,128)S(1)}, u32[]{:S(2)}, u32[]{:S(2)}) collective-permute-start(f32[4,72,128]{2,1,0:T(8,128)S(1)} %pad_maximum_fusion.5), channel_id=1, source_target_pairs={{0,4},{4,0},{1,5},{5,1},{2,6},{6,2},{3,7},{7,3},{8,12},{12,8},{9,1... | collective-permute-start | bytes 442376 | tf_op jit(solution)/shard_map/ppermute | solution.py:20
  62.7 6.1 %collective-permute-start.23 = (f32[4,72,128]{2,1,0:T(8,128)S(1)}, f32[4,72,128]{2,1,0:T(8,128)S(1)}, u32[]{:S(2)}, u32[]{:S(2)}) collective-permute-start(f32[4,72,128]{2,1,0:T(8,128)S(1)} %pad_maximum_fusion.5), channel_id=1, source_target_pairs={{0,2},{2,0},{1,3},{3,1},{4,6},{6,4},{5,7},{7,5},{8,10},{10,8},{9,1... | collective-permute-start | bytes 442376 | tf_op jit(solution)/shard_map/ppermute | solution.py:20
  76.3 5.9 %collective-permute-start.30 = (f32[512,512]{1,0:T(8,128)S(1)}, f32[512,512]{1,0:T(8,128)S(1)}, u32[]{:S(2)}, u32[]{:S(2)}) collective-permute-start(f32[512,512]{1,0:T(8,128)S(1)} %get-tuple-element.76.own), channel_id=1, source_target_pairs={{0,1},{1,0},{2,3},{3,2},{4,5},{5,4},{6,7},{7,6},{8,9},{9,8},{10,11... | collective-permute-start | bytes 3145736 | tf_op jit(solution)/shard_map/ppermute | solution.py:20
  76.7 23.0 %collective-permute-start.40 = (bf16[2,1024,128]{2,1,0:T(8,128)(2,1)S(1)}, bf16[2,1024,128]{2,1,0:T(8,128)(2,1)S(1)}, u32[]{:S(2)}, u32[]{:S(2)}) collective-permute-start(bf16[2,1024,128]{2,1,0:T(8,128)(2,1)S(1)} %collective-permute-done.21.refs_4_), channel_id=1, source_target_pairs={{0,1},{1,0},{2,3},{3,2},{4,5},{5,4},{6,7},{7,6},{8,9},{9,8},{10,11... | collective-permute-start | bytes 1572872 | tf_op jit(solution)/shard_map/ppermute | solution.py:20
  78.7 6.8 %collective-permute-start.33 = (bf16[4,64,128]{2,1,0:T(8,128)(2,1)S(1)}, bf16[4,64,128]{2,1,0:T(8,128)(2,1)S(1)}, u32[]{:S(2)}, u32[]{:S(2)}) collective-permute-start(bf16[4,64,128]{2,1,0:T(8,128)(2,1)S(1)} %get-tuple-element.83), channel_id=1, source_target_pairs={{0,6},{2,4},{4,2},{6,0},{1,7},{3,5},{5,3},{7,1},{8,14},{10,12},{12... | collective-permute-start | bytes 196616 | tf_op jit(solution)/shard_map/ppermute | solution.py:474
  85.5 10.5 %collective-permute-start.36 = (bf16[4,64,128]{2,1,0:T(8,128)(2,1)S(1)}, bf16[4,64,128]{2,1,0:T(8,128)(2,1)S(1)}, u32[]{:S(2)}, u32[]{:S(2)}) collective-permute-start(bf16[4,64,128]{2,1,0:T(8,128)(2,1)S(1)} %add_convert_fusion), channel_id=1, source_target_pairs={{0,24},{8,0},{16,8},{24,16},{1,25},{9,1},{17,9},{25,17},{2,26},{10... | collective-permute-start | bytes 196616 | tf_op jit(solution)/shard_map/ppermute | solution.py:469
  87.4 8.7 %collective-permute-start.35 = (bf16[4,64,128]{2,1,0:T(8,128)(2,1)S(1)}, bf16[4,64,128]{2,1,0:T(8,128)(2,1)S(1)}, u32[]{:S(2)}, u32[]{:S(2)}) collective-permute-start(bf16[4,64,128]{2,1,0:T(8,128)(2,1)S(1)} %add_convert_fusion), channel_id=1, source_target_pairs={{0,16},{8,24},{16,0},{24,8},{1,17},{9,25},{17,1},{25,9},{2,18},{10... | collective-permute-start | bytes 196616 | tf_op jit(solution)/shard_map/ppermute | solution.py:469
  88.6 7.5 %collective-permute-start.34 = (bf16[4,64,128]{2,1,0:T(8,128)(2,1)S(1)}, bf16[4,64,128]{2,1,0:T(8,128)(2,1)S(1)}, u32[]{:S(2)}, u32[]{:S(2)}) collective-permute-start(bf16[4,64,128]{2,1,0:T(8,128)(2,1)S(1)} %add_convert_fusion), channel_id=1, source_target_pairs={{0,8},{8,16},{16,24},{24,0},{1,9},{9,17},{17,25},{25,1},{2,10},{10... | collective-permute-start | bytes 196616 | tf_op jit(solution)/shard_map/ppermute | solution.py:469
  96.0 11.8 %collective-permute-start.42 = (bf16[2,512,512]{2,1,0:T(8,128)(2,1)S(1)}, bf16[2,512,512]{2,1,0:T(8,128)(2,1)S(1)}, u32[]{:S(2)}, u32[]{:S(2)}) collective-permute-start(bf16[2,512,512]{2,1,0:T(8,128)(2,1)S(1)} %shard_map.51.inv), channel_id=1, source_target_pairs={{0,1},{1,0},{2,3},{3,2},{4,5},{5,4},{6,7},{7,6},{8,9},{9,8},{10,11... | collective-permute-start | bytes 3145736 | tf_op jit(solution)/shard_map/ppermute | solution.py:20
  96.1 7.3 %collective-permute-start.39 = (f32[4,64,128]{2,1,0:T(8,128)S(1)}, f32[4,64,128]{2,1,0:T(8,128)S(1)}, u32[]{:S(2)}, u32[]{:S(2)}) collective-permute-start(f32[4,64,128]{2,1,0:T(8,128)S(1)} %convert_add_fusion), channel_id=1, source_target_pairs={{0,6},{2,4},{4,2},{6,0},{1,7},{3,5},{5,3},{7,1},{8,14},{10,12},{12... | collective-permute-start | bytes 393224 | tf_op jit(solution)/shard_map/ppermute | solution.py:474
  97.4 7.9 %collective-permute-start.38 = (f32[4,64,128]{2,1,0:T(8,128)S(1)}, f32[4,64,128]{2,1,0:T(8,128)S(1)}, u32[]{:S(2)}, u32[]{:S(2)}) collective-permute-start(f32[4,64,128]{2,1,0:T(8,128)S(1)} %convert_add_fusion), channel_id=1, source_target_pairs={{0,4},{4,0},{1,5},{5,1},{2,6},{6,2},{3,7},{7,3},{8,12},{12,8},{9,1... | collective-permute-start | bytes 393224 | tf_op jit(solution)/shard_map/ppermute | solution.py:20
  98.6 7.1 %collective-permute-start.37 = (f32[4,64,128]{2,1,0:T(8,128)S(1)}, f32[4,64,128]{2,1,0:T(8,128)S(1)}, u32[]{:S(2)}, u32[]{:S(2)}) collective-permute-start(f32[4,64,128]{2,1,0:T(8,128)S(1)} %convert_add_fusion), channel_id=1, source_target_pairs={{0,2},{2,0},{1,3},{3,1},{4,6},{6,4},{5,7},{7,5},{8,10},{10,8},{9,1... | collective-permute-start | bytes 393224 | tf_op jit(solution)/shard_map/ppermute | solution.py:20
  (15 other events, 66.9 us)

commit v7 on v6

--- a/solution.py
+++ b/solution.py
@@ -137,7 +137,8 @@
             for rows, cols in ((top, slice(0, channels)), (right, right)):
                 ahigh, alow = highs[now, rows], lows[now, rows]
                 bhigh, blow = high[now, :, cols], low[now, :, cols]
-                value = 2.0 * table[now, rows, cols] - (dot(ahigh, bhigh) + dot(ahigh, blow) + dot(alow, bhigh))
+                left_side = jnp.concatenate([ahigh, ahigh, alow], axis=1)
+                value = 2.0 * table[now, rows, cols] - dot(left_side, jnp.concatenate([bhigh, blow, bhigh], axis=0))
                 store(table, high, low, rows, cols, value)
                 if rows == top:
                     store(table, high, low, right, left, value[:, half:].T)

time: 111 us -> 110 us (level)
  no operation moved by 1% of the time
where the time goes in v7:
time: 110 us
  starting transfers between devices  46.4 us (42%)
  waiting for transfers between devices  31.1 us (28%)
  Pallas kernels  29 us (26%)
  local copies, waits for them, and re-layouts  2.14 us (2%)
    pallas_call x13, Pallas kernels, call(): pl.pallas_call(body, out_shape=shapes, in_specs=[pl.BlockSpec(memory_spac...  29 us
    ppermute x25, starting transfers between devices, swap(): return lax.ppermute(value, axis, [(0, 1), (1, 0)])  18 us
    ppermute x12, starting transfers between devices, ahead(): return lax.ppermute(piece, 'z', [(i, (i + by) % size) for i in range(size)])  17.3 us
    ppermute x25, waiting for transfers between devices, swap(): return lax.ppermute(value, axis, [(0, 1), (1, 0)])  17.2 us
    ppermute x12, waiting for transfers between devices, ahead(): return lax.ppermute(piece, 'z', [(i, (i + by) % size) for i in range(size)])  8.64 us
    ppermute x5, starting transfers between devices, exchange(): lax.ppermute(pieces[3], ('x', 'y'), both)  7.73 us
    ppermute x5, waiting for transfers between devices, exchange(): lax.ppermute(pieces[3], ('x', 'y'), both)  3.88 us
    ppermute x1, starting transfers between devices, from_behind(): return lax.ppermute(value, axes, [(i, i + 1) for i in range(devices - 1)])  3.38 us
  transfers between devices with their start and end apart: 43, of which 20 were waited for; matrix products, arithmetic and copies ran while one was open for 0% of the time, Pallas kernels for 23%

profile of v7, /device:TPU:0, one launch (start us, length us, event | category | flops | bytes accessed | tf_op | source)
XLA Modules:
  0.0 109.8 jit_solution(18245255089102263155)
XLA Ops:
  3.4 3.0 %collective-permute-start.2 = (bf16[1024,128]{1,0:T(8,128)(2,1)S(1)}, bf16[1024,128]{1,0:T(8,128)(2,1)S(1)}, u32[]{:S(2)}, u32[]{:S(2)}) collective-permute-start(bf16[1024,128]{1,0:T(8,128)(2,1)S(1)} %get-tuple-element.47), channel_id=1, source_target_pairs={{0,2},{2,0},{1,3},{3,1},{4,6},{6,4},{5,7},{7,5},{8,10},{10,8},{9,1... | collective-permute-start | bytes 786440 | tf_op jit(solution)/shard_map/ppermute | solution.py:20
  6.4 3.4 %collective-permute-start.3 = (bf16[2,16,128]{2,1,0:T(8,128)(2,1)S(1)}, bf16[2,16,128]{2,1,0:T(8,128)(2,1)S(1)}, u32[]{:S(2)}, u32[]{:S(2)}) collective-permute-start(bf16[2,16,128]{2,1,0:T(8,128)(2,1)S(1)} %get-tuple-element.48), channel_id=1, source_target_pairs={{0,4},{4,8},{8,12},{12,16},{16,20},{20,24},{24,28},{1,5},{5,9},{9,... | collective-permute-start | bytes 24584 | tf_op jit(solution)/shard_map/ppermute | solution.py:25
  9.8 1.3 %collective-permute-done.3.halo.refs_8_ = bf16[2,16,128]{2,1,0:T(8,128)(2,1)S(1)} collective-permute-done((bf16[2,16,128]{2,1,0:T(8,128)(2,1)S(1)}, bf16[2,16,128]{2,1,0:T(8,128)(2,1)S(1)}, u32[]{:S(2)}, u32[]{:S(2)}) %collective-permute-start.3) | collective-permute-done | bytes 8224 | tf_op jit(solution)/shard_map/ppermute | solution.py:25
  14.2 4.7 %collective-permute-done.4.refs_5_ = bf16[1088,128]{1,0:T(8,128)(2,1)S(1)} collective-permute-done((bf16[1088,128]{1,0:T(8,128)(2,1)S(1)}, bf16[1088,128]{1,0:T(8,128)(2,1)S(1)}, u32[]{:S(2)}, u32[]{:S(2)}) %collective-permute-start.4) | collective-permute-done | bytes 278560 | tf_op jit(solution)/shard_map/ppermute | solution.py:20
  19.4 4.9 %collective-permute-start.13 = (f32[2,80,128]{2,1,0:T(8,128)S(1)}, f32[2,80,128]{2,1,0:T(8,128)S(1)}, u32[]{:S(2)}, u32[]{:S(2)}) collective-permute-start(f32[2,80,128]{2,1,0:T(8,128)S(1)} %get-tuple-element.93), channel_id=1, source_target_pairs={{0,24},{8,0},{16,8},{24,16},{1,25},{9,1},{17,9},{25,17},{2,26},{10... | collective-permute-start | bytes 245768 | tf_op jit(solution)/shard_map/ppermute | solution.py:470
  26.2 1.5 %collective-permute-start.10 = (f32[4,64,128]{2,1,0:T(8,128)S(1)}, f32[4,64,128]{2,1,0:T(8,128)S(1)}, u32[]{:S(2)}, u32[]{:S(2)}) collective-permute-start(f32[4,64,128]{2,1,0:T(8,128)S(1)} %get-tuple-element.55), channel_id=1, source_target_pairs={{0,4},{4,0},{1,5},{5,1},{2,6},{6,2},{3,7},{7,3},{8,12},{12,8},{9,1... | collective-permute-start | bytes 393224 | tf_op jit(solution)/shard_map/ppermute | solution.py:20
  27.6 1.5 %collective-permute-start.11 = (f32[4,64,128]{2,1,0:T(8,128)S(1)}, f32[4,64,128]{2,1,0:T(8,128)S(1)}, u32[]{:S(2)}, u32[]{:S(2)}) collective-permute-start(f32[4,64,128]{2,1,0:T(8,128)S(1)} %get-tuple-element.56), channel_id=1, source_target_pairs={{0,6},{2,4},{4,2},{6,0},{1,7},{3,5},{5,3},{7,1},{8,14},{10,12},{12... | collective-permute-start | bytes 393224 | tf_op jit(solution)/shard_map/ppermute | solution.py:475
  29.5 1.6 %collective-permute-start.8 = (f32[2,80,128]{2,1,0:T(8,128)S(1)}, f32[2,80,128]{2,1,0:T(8,128)S(1)}, u32[]{:S(2)}, u32[]{:S(2)}) collective-permute-start(f32[2,80,128]{2,1,0:T(8,128)S(1)} %get-tuple-element.92), channel_id=1, source_target_pairs={{0,8},{8,16},{16,24},{24,0},{1,9},{9,17},{17,25},{25,1},{2,10},{10... | collective-permute-start | bytes 245768 | tf_op jit(solution)/shard_map/ppermute | solution.py:470
  32.5 2.2 %collective-permute-done.11 = f32[4,64,128]{2,1,0:T(8,128)S(1)} collective-permute-done((f32[4,64,128]{2,1,0:T(8,128)S(1)}, f32[4,64,128]{2,1,0:T(8,128)S(1)}, u32[]{:S(2)}, u32[]{:S(2)}) %collective-permute-start.11) | collective-permute-done | bytes 131104 | tf_op jit(solution)/shard_map/ppermute | solution.py:475
  36.0 1.6 %collective-permute-start.17 = (f32[64,128]{1,0:T(8,128)S(1)}, f32[64,128]{1,0:T(8,128)S(1)}, u32[]{:S(2)}, u32[]{:S(2)}) collective-permute-start(f32[64,128]{1,0:T(8,128)S(1)} %get-tuple-element.96), channel_id=1, source_target_pairs={{0,24},{8,0},{16,8},{24,16},{1,25},{9,1},{17,9},{25,17},{2,26},{10... | collective-permute-start | bytes 98312 | tf_op jit(solution)/shard_map/ppermute | solution.py:470
  37.7 1.9 %collective-permute-start.15 = (f32[64,128]{1,0:T(8,128)S(1)}, f32[64,128]{1,0:T(8,128)S(1)}, u32[]{:S(2)}, u32[]{:S(2)}) collective-permute-start(f32[64,128]{1,0:T(8,128)S(1)} %get-tuple-element.95), channel_id=1, source_target_pairs={{0,8},{8,16},{16,24},{24,0},{1,9},{9,17},{17,25},{25,1},{2,10},{10... | collective-permute-start | bytes 98312 | tf_op jit(solution)/shard_map/ppermute | solution.py:470
  43.8 1.9 %collective-permute-start.20 = (f32[152,128]{1,0:T(8,128)S(1)}, f32[152,128]{1,0:T(8,128)S(1)}, u32[]{:S(2)}, u32[]{:S(2)}) collective-permute-start(f32[152,128]{1,0:T(8,128)S(1)} %constant_dynamic-update-slice_fusion), channel_id=1, source_target_pairs={{0,24},{8,0},{16,8},{24,16},{1,25},{9,1},{17,9},{25,17},{2,26},{10... | collective-permute-start | bytes 233480 | tf_op jit(solution)/shard_map/ppermute | solution.py:470
  47.2 2.1 %collective-permute-done.20 = f32[152,128]{1,0:T(8,128)S(1)} collective-permute-done((f32[152,128]{1,0:T(8,128)S(1)}, f32[152,128]{1,0:T(8,128)S(1)}, u32[]{:S(2)}, u32[]{:S(2)}) %collective-permute-start.20) | collective-permute-done | bytes 77856 | tf_op jit(solution)/shard_map/ppermute | solution.py:470
  49.3 2.2 %collective-permute-done.19 = f32[152,128]{1,0:T(8,128)S(1)} collective-permute-done((f32[152,128]{1,0:T(8,128)S(1)}, f32[152,128]{1,0:T(8,128)S(1)}, u32[]{:S(2)}, u32[]{:S(2)}) %collective-permute-start.19) | collective-permute-done | bytes 77856 | tf_op jit(solution)/shard_map/ppermute | solution.py:470
  51.5 1.6 %collective-permute-done.18 = f32[152,128]{1,0:T(8,128)S(1)} collective-permute-done((f32[152,128]{1,0:T(8,128)S(1)}, f32[152,128]{1,0:T(8,128)S(1)}, u32[]{:S(2)}, u32[]{:S(2)}) %collective-permute-start.18) | collective-permute-done | bytes 77856 | tf_op jit(solution)/shard_map/ppermute | solution.py:470
  55.1 1.5 %collective-permute-start.27 = (f32[4,80,128]{2,1,0:T(8,128)S(1)}, f32[4,80,128]{2,1,0:T(8,128)S(1)}, u32[]{:S(2)}, u32[]{:S(2)}) collective-permute-start(f32[4,80,128]{2,1,0:T(8,128)S(1)} %pad_maximum_fusion.2.refs_0_), channel_id=1, source_target_pairs={{0,6},{2,4},{4,2},{6,0},{1,7},{3,5},{5,3},{7,1},{8,14},{10,12},{12... | collective-permute-start | bytes 491528 | tf_op jit(solution)/shard_map/ppermute | solution.py:475
  56.6 4.4 %collective-permute-done.22.refs_1_ = f32[4,80,128]{2,1,0:T(8,128)S(1)} collective-permute-done((f32[4,80,128]{2,1,0:T(8,128)S(1)}, f32[4,80,128]{2,1,0:T(8,128)S(1)}, u32[]{:S(2)}, u32[]{:S(2)}) %collective-permute-start.22) | collective-permute-done | bytes 163872 | tf_op jit(solution)/shard_map/ppermute | solution.py:20
  61.0 1.7 %collective-permute-start.25 = (f32[4,72,128]{2,1,0:T(8,128)S(1)}, f32[4,72,128]{2,1,0:T(8,128)S(1)}, u32[]{:S(2)}, u32[]{:S(2)}) collective-permute-start(f32[4,72,128]{2,1,0:T(8,128)S(1)} %pad_maximum_fusion.5), channel_id=1, source_target_pairs={{0,6},{2,4},{4,2},{6,0},{1,7},{3,5},{5,3},{7,1},{8,14},{10,12},{12... | collective-permute-start | bytes 442376 | tf_op jit(solution)/shard_map/ppermute | solution.py:475
  62.7 1.8 %collective-permute-start.23 = (f32[4,72,128]{2,1,0:T(8,128)S(1)}, f32[4,72,128]{2,1,0:T(8,128)S(1)}, u32[]{:S(2)}, u32[]{:S(2)}) collective-permute-start(f32[4,72,128]{2,1,0:T(8,128)S(1)} %pad_maximum_fusion.5), channel_id=1, source_target_pairs={{0,2},{2,0},{1,3},{3,1},{4,6},{6,4},{5,7},{7,5},{8,10},{10,8},{9,1... | collective-permute-start | bytes 442376 | tf_op jit(solution)/shard_map/ppermute | solution.py:20
  64.5 4.2 %shard_map.45 = (f32[512,512]{1,0:T(8,128)S(1)}, f32[512,512]{1,0:T(8,128)S(1)}, f32[512,512]{1,0:T(8,128)S(1)}, f32[8,128]{1,0:T(8,128)S(1)}) custom-call(f32[4,80,128]{2,1,0:T(8,128)S(1)} %pad_maximum_fusion.2.refs_0_, f32[4,80,128]{2,1,0:T(8,128)S(1)} %collective-permute-done.22.refs_1_, f32[4,80,128]{2,1,0:T(8,128)S(1)} %collective-permute-done.26.refs_2_, ...), custom_call_target="tpu_custom_call" | custom-call | flops 4026531840 | bytes 3805184 | tf_op jit(solution)/shard_map/pallas_call | solution.py:34
  68.9 3.5 %shard_map.46.inv = bf16[2,512,512]{2,1,0:T(8,128)(2,1)S(1)} custom-call(f32[512,512]{1,0:T(8,128)S(1)} %get-tuple-element.66.error, f32[512,512]{1,0:T(8,128)S(1)} %get-tuple-element.68.iterate, f32[8,128]{1,0:T(8,128)S(1)} %get-tuple-element.69.scale), custom_call_target="tpu_custom_call" | custom-call | flops 4026531840 | bytes 3149824 | tf_op jit(solution)/shard_map/pallas_call | solution.py:34
  72.4 1.4 %shard_map.47 = (bf16[512,512]{1,0:T(8,128)(2,1)S(1)}, f32[512,512]{1,0:T(8,128)S(1)}, f32[8,128]{1,0:T(8,128)S(1)}) custom-call(f32[4,4,72,128]{3,2,1,0:T(8,128)S(1)} %pad_maximum_fusion.ours, f32[4,4,72,128]{3,2,1,0:T(8,128)S(1)} %collective-permute-done.28.theirs, bf16[2,512,512]{2,1,0:T(8,128)(2,1)S(1)} %shard_map.46.inv), custom_call_target="tpu_custom_call" | custom-call | flops 805306368 | bytes 3805184 | tf_op jit(solution)/shard_map/pallas_call | solution.py:34
  76.4 1.9 %shard_map.49 = (bf16[2,1024,512]{2,1,0:T(8,128)(2,1)S(1)}, bf16[1024,512]{1,0:T(8,128)(2,1)S(1)}, bf16[4,64,128]{2,1,0:T(8,128)(2,1)S(1)}, bf16[4,64,128]{2,1,0...) custom-call(bf16[2,1024,512]{2,1,0:T(8,128)(2,1)S(1)} %get-tuple-element.52.here, ...), custom_call_target="tpu_custom_call" | custom-call | flops 805306368 | bytes 8716288 | tf_op jit(solution)/shard_map/pallas_call | solution.py:34
  78.2 1.8 %collective-permute-start.33 = (bf16[4,64,128]{2,1,0:T(8,128)(2,1)S(1)}, bf16[4,64,128]{2,1,0:T(8,128)(2,1)S(1)}, u32[]{:S(2)}, u32[]{:S(2)}) collective-permute-start(bf16[4,64,128]{2,1,0:T(8,128)(2,1)S(1)} %get-tuple-element.83), channel_id=1, source_target_pairs={{0,6},{2,4},{4,2},{6,0},{1,7},{3,5},{5,3},{7,1},{8,14},{10,12},{12... | collective-permute-start | bytes 196616 | tf_op jit(solution)/shard_map/ppermute | solution.py:475
  81.8 3.2 %shard_map.50 = (f32[512,512]{1,0:T(8,128)S(1)}, f32[8,128]{1,0:T(8,128)S(1)}) custom-call(f32[512,512]{1,0:T(8,128)S(1)} %get-tuple-element.76.own, f32[512,512]{1,0:T(8,128)S(1)} %collective-permute-done.30.other, f32[512,512]{1,0:T(8,128)S(1)} %get-tuple-element.77.cross, bf16[512,512]{1,0:T(8,128)(2,1)S(1)} %collective-permute-done.29.theirs.refs_8_, ...), custom_call_target="tpu_custom_call" | custom-call | flops 2415919104 | bytes 4726784 | tf_op jit(solution)/shard_map/pallas_call | solution.py:34
  85.1 1.9 %collective-permute-start.36 = (bf16[4,64,128]{2,1,0:T(8,128)(2,1)S(1)}, bf16[4,64,128]{2,1,0:T(8,128)(2,1)S(1)}, u32[]{:S(2)}, u32[]{:S(2)}) collective-permute-start(bf16[4,64,128]{2,1,0:T(8,128)(2,1)S(1)} %add_convert_fusion), channel_id=1, source_target_pairs={{0,24},{8,0},{16,8},{24,16},{1,25},{9,1},{17,9},{25,17},{2,26},{10... | collective-permute-start | bytes 196616 | tf_op jit(solution)/shard_map/ppermute | solution.py:470
  88.5 6.7 %shard_map.51.inv = bf16[2,512,512]{2,1,0:T(8,128)(2,1)S(1)} custom-call(f32[512,512]{1,0:T(8,128)S(1)} %get-tuple-element.79.matrix, f32[8,128]{1,0:T(8,128)S(1)} %get-tuple-element.84.scale), custom_call_target="tpu_custom_call" | custom-call | flops 8053063680 | bytes 2101248 | tf_op jit(solution)/shard_map/pallas_call | solution.py:34
  98.9 2.1 %shard_map.52 = (bf16[2,1024,512]{2,1,0:T(8,128)(2,1)S(1)}, bf16[1024,512]{1,0:T(8,128)(2,1)S(1)}) custom-call(bf16[2048,128]{1,0:T(8,128)(2,1)S(1)} %copy-done.1, bf16[2048,128]{1,0:T(8,128)(2,1)S(1)} %copy-done.3, bf16[2048,128]{1,0:T(8,128)(2,1)S(1)} %collective-permute-done.forward_core.refs_2_, ...), custom_call_target="tpu_custom_call" | custom-call | flops 1073741824 | bytes 7405568 | tf_op jit(solution)/shard_map/pallas_call | solution.py:34
  100.9 1.6 %collective-permute-done.39 = f32[4,64,128]{2,1,0:T(8,128)S(1)} collective-permute-done((f32[4,64,128]{2,1,0:T(8,128)S(1)}, f32[4,64,128]{2,1,0:T(8,128)S(1)}, u32[]{:S(2)}, u32[]{:S(2)}) %collective-permute-start.39) | collective-permute-done | bytes 131104 | tf_op jit(solution)/shard_map/ppermute | solution.py:475
  102.6 1.9 %collective-permute-done.38 = f32[4,64,128]{2,1,0:T(8,128)S(1)} collective-permute-done((f32[4,64,128]{2,1,0:T(8,128)S(1)}, f32[4,64,128]{2,1,0:T(8,128)S(1)}, u32[]{:S(2)}, u32[]{:S(2)}) %collective-permute-start.38) | collective-permute-done | bytes 131104 | tf_op jit(solution)/shard_map/ppermute | solution.py:20
  105.1 1.9 %collective-permute-done.41.theirs = f32[4,4,64,128]{3,2,1,0:T(8,128)S(1)} collective-permute-done((f32[4,4,64,128]{3,2,1,0:T(8,128)S(1)}, f32[4,4,64,128]{3,2,1,0:T(8,128)S(1)}, u32[]{:S(2)}, u32[]{:S(2)}) %collective-permute-start.41) | collective-permute-done | bytes 524320 | tf_op jit(solution)/shard_map/ppermute | solution.py:20
  107.0 2.8 %shard_map.53 = (bf16[2048,128]{1,0:T(8,128)(2,1)}, bf16[2048,128]{1,0:T(8,128)(2,1)}) custom-call(f32[4,4,64,128]{3,2,1,0:T(8,128)S(1)} %pad_maximum_fusion.1.ours, f32[4,4,64,128]{3,2,1,0:T(8,128)S(1)} %collective-permute-done.41.theirs, bf16[2,512,512]{2,1,0:T(8,128)(2,1)S(1)} %shard_map.51.inv, ...), custom_call_target="tpu_custom_call" | custom-call | flops 536870912 | bytes 10485760 | tf_op jit(solution)/shard_map/pallas_call | solution.py:34
  (93 shorter events, 29.3 us)
Async XLA Ops:
  0.6 12.4 %collective-permute-start = (bf16[2048,128]{1,0:T(8,128)(2,1)}, bf16[2048,128]{1,0:T(8,128)(2,1)S(1)}, u32[]{:S(2)}, u32[]{:S(2)}) collective-permute-start(bf16[2048,128]{1,0:T(8,128)(2,1)} %refs_0_.3), channel_id=1, source_target_pairs={{0,1},{1,0},{2,3},{3,2},{4,5},{5,4},{6,7},{7,6},{8,9},{9,8},{10,11... | collective-permute-start | bytes 1572872 | tf_op jit(solution)/shard_map/ppermute | solution.py:20
  1.1 11.9 %collective-permute-start.1 = (bf16[2048,128]{1,0:T(8,128)(2,1)}, bf16[2048,128]{1,0:T(8,128)(2,1)S(1)}, u32[]{:S(2)}, u32[]{:S(2)}) collective-permute-start(bf16[2048,128]{1,0:T(8,128)(2,1)} %refs_1_.3), channel_id=1, source_target_pairs={{0,1},{1,0},{2,3},{3,2},{4,5},{5,4},{6,7},{7,6},{8,9},{9,8},{10,11... | collective-permute-start | bytes 1572872 | tf_op jit(solution)/shard_map/ppermute | solution.py:20
  3.4 9.7 %collective-permute-start.2 = (bf16[1024,128]{1,0:T(8,128)(2,1)S(1)}, bf16[1024,128]{1,0:T(8,128)(2,1)S(1)}, u32[]{:S(2)}, u32[]{:S(2)}) collective-permute-start(bf16[1024,128]{1,0:T(8,128)(2,1)S(1)} %get-tuple-element.47), channel_id=1, source_target_pairs={{0,2},{2,0},{1,3},{3,1},{4,6},{6,4},{5,7},{7,5},{8,10},{10,8},{9,1... | collective-permute-start | bytes 786440 | tf_op jit(solution)/shard_map/ppermute | solution.py:20
  11.2 7.7 %collective-permute-start.4 = (bf16[1088,128]{1,0:T(8,128)(2,1)S(1)}, bf16[1088,128]{1,0:T(8,128)(2,1)S(1)}, u32[]{:S(2)}, u32[]{:S(2)}) collective-permute-start(bf16[1088,128]{1,0:T(8,128)(2,1)S(1)} %shard_map.42), channel_id=1, source_target_pairs={{0,2},{2,0},{1,3},{3,1},{4,6},{6,4},{5,7},{7,5},{8,10},{10,8},{9,1... | collective-permute-start | bytes 835592 | tf_op jit(solution)/shard_map/ppermute | solution.py:20
  19.4 10.0 %collective-permute-start.13 = (f32[2,80,128]{2,1,0:T(8,128)S(1)}, f32[2,80,128]{2,1,0:T(8,128)S(1)}, u32[]{:S(2)}, u32[]{:S(2)}) collective-permute-start(f32[2,80,128]{2,1,0:T(8,128)S(1)} %get-tuple-element.93), channel_id=1, source_target_pairs={{0,24},{8,0},{16,8},{24,16},{1,25},{9,1},{17,9},{25,17},{2,26},{10... | collective-permute-start | bytes 245768 | tf_op jit(solution)/shard_map/ppermute | solution.py:470
  25.6 5.6 %collective-permute-start.9 = (f32[4,64,128]{2,1,0:T(8,128)S(1)}, f32[4,64,128]{2,1,0:T(8,128)S(1)}, u32[]{:S(2)}, u32[]{:S(2)}) collective-permute-start(f32[4,64,128]{2,1,0:T(8,128)S(1)} %get-tuple-element.54), channel_id=1, source_target_pairs={{0,2},{2,0},{1,3},{3,1},{4,6},{6,4},{5,7},{7,5},{8,10},{10,8},{9,1... | collective-permute-start | bytes 393224 | tf_op jit(solution)/shard_map/ppermute | solution.py:20
  26.2 6.4 %collective-permute-start.10 = (f32[4,64,128]{2,1,0:T(8,128)S(1)}, f32[4,64,128]{2,1,0:T(8,128)S(1)}, u32[]{:S(2)}, u32[]{:S(2)}) collective-permute-start(f32[4,64,128]{2,1,0:T(8,128)S(1)} %get-tuple-element.55), channel_id=1, source_target_pairs={{0,4},{4,0},{1,5},{5,1},{2,6},{6,2},{3,7},{7,3},{8,12},{12,8},{9,1... | collective-permute-start | bytes 393224 | tf_op jit(solution)/shard_map/ppermute | solution.py:20
  27.6 7.1 %collective-permute-start.11 = (f32[4,64,128]{2,1,0:T(8,128)S(1)}, f32[4,64,128]{2,1,0:T(8,128)S(1)}, u32[]{:S(2)}, u32[]{:S(2)}) collective-permute-start(f32[4,64,128]{2,1,0:T(8,128)S(1)} %get-tuple-element.56), channel_id=1, source_target_pairs={{0,6},{2,4},{4,2},{6,0},{1,7},{3,5},{5,3},{7,1},{8,14},{10,12},{12... | collective-permute-start | bytes 393224 | tf_op jit(solution)/shard_map/ppermute | solution.py:475
  29.1 6.8 %collective-permute-start.12 = (f32[2,80,128]{2,1,0:T(8,128)S(1)}, f32[2,80,128]{2,1,0:T(8,128)S(1)}, u32[]{:S(2)}, u32[]{:S(2)}) collective-permute-start(f32[2,80,128]{2,1,0:T(8,128)S(1)} %get-tuple-element.94), channel_id=1, source_target_pairs={{0,16},{8,24},{16,0},{24,8},{1,17},{9,25},{17,1},{25,9},{2,18},{10... | collective-permute-start | bytes 245768 | tf_op jit(solution)/shard_map/ppermute | solution.py:470
  29.5 6.5 %collective-permute-start.8 = (f32[2,80,128]{2,1,0:T(8,128)S(1)}, f32[2,80,128]{2,1,0:T(8,128)S(1)}, u32[]{:S(2)}, u32[]{:S(2)}) collective-permute-start(f32[2,80,128]{2,1,0:T(8,128)S(1)} %get-tuple-element.92), channel_id=1, source_target_pairs={{0,8},{8,16},{16,24},{24,0},{1,9},{9,17},{17,25},{25,1},{2,10},{10... | collective-permute-start | bytes 245768 | tf_op jit(solution)/shard_map/ppermute | solution.py:470
  36.0 5.7 %collective-permute-start.17 = (f32[64,128]{1,0:T(8,128)S(1)}, f32[64,128]{1,0:T(8,128)S(1)}, u32[]{:S(2)}, u32[]{:S(2)}) collective-permute-start(f32[64,128]{1,0:T(8,128)S(1)} %get-tuple-element.96), channel_id=1, source_target_pairs={{0,24},{8,0},{16,8},{24,16},{1,25},{9,1},{17,9},{25,17},{2,26},{10... | collective-permute-start | bytes 98312 | tf_op jit(solution)/shard_map/ppermute | solution.py:470
  37.7 5.7 %collective-permute-start.15 = (f32[64,128]{1,0:T(8,128)S(1)}, f32[64,128]{1,0:T(8,128)S(1)}, u32[]{:S(2)}, u32[]{:S(2)}) collective-permute-start(f32[64,128]{1,0:T(8,128)S(1)} %get-tuple-element.95), channel_id=1, source_target_pairs={{0,8},{8,16},{16,24},{24,0},{1,9},{9,17},{17,25},{25,1},{2,10},{10... | collective-permute-start | bytes 98312 | tf_op jit(solution)/shard_map/ppermute | solution.py:470
  40.6 12.4 %collective-permute-start.21 = (bf16[2,1024,128]{2,1,0:T(8,128)(2,1)S(1)}, bf16[2,1024,128]{2,1,0:T(8,128)(2,1)S(1)}, u32[]{:S(2)}, u32[]{:S(2)}) collective-permute-start(bf16[2,1024,128]{2,1,0:T(8,128)(2,1)S(1)} %get-tuple-element.63), channel_id=1, source_target_pairs={{0,2},{2,0},{1,3},{3,1},{4,6},{6,4},{5,7},{7,5},{8,10},{10,8},{9,1... | collective-permute-start | bytes 1572872 | tf_op jit(solution)/shard_map/ppermute | solution.py:20
  43.8 5.5 %collective-permute-start.20 = (f32[152,128]{1,0:T(8,128)S(1)}, f32[152,128]{1,0:T(8,128)S(1)}, u32[]{:S(2)}, u32[]{:S(2)}) collective-permute-start(f32[152,128]{1,0:T(8,128)S(1)} %constant_dynamic-update-slice_fusion), channel_id=1, source_target_pairs={{0,24},{8,0},{16,8},{24,16},{1,25},{9,1},{17,9},{25,17},{2,26},{10... | collective-permute-start | bytes 233480 | tf_op jit(solution)/shard_map/ppermute | solution.py:470
  45.7 5.7 %collective-permute-start.19 = (f32[152,128]{1,0:T(8,128)S(1)}, f32[152,128]{1,0:T(8,128)S(1)}, u32[]{:S(2)}, u32[]{:S(2)}) collective-permute-start(f32[152,128]{1,0:T(8,128)S(1)} %constant_dynamic-update-slice_fusion), channel_id=1, source_target_pairs={{0,16},{8,24},{16,0},{24,8},{1,17},{9,25},{17,1},{25,9},{2,18},{10... | collective-permute-start | bytes 233480 | tf_op jit(solution)/shard_map/ppermute | solution.py:470
  46.8 6.2 %collective-permute-start.18 = (f32[152,128]{1,0:T(8,128)S(1)}, f32[152,128]{1,0:T(8,128)S(1)}, u32[]{:S(2)}, u32[]{:S(2)}) collective-permute-start(f32[152,128]{1,0:T(8,128)S(1)} %constant_dynamic-update-slice_fusion), channel_id=1, source_target_pairs={{0,8},{8,16},{16,24},{24,0},{1,9},{9,17},{17,25},{25,1},{2,10},{10... | collective-permute-start | bytes 233480 | tf_op jit(solution)/shard_map/ppermute | solution.py:470
  53.0 7.9 %collective-permute-start.22 = (f32[4,80,128]{2,1,0:T(8,128)S(1)}, f32[4,80,128]{2,1,0:T(8,128)S(1)}, u32[]{:S(2)}, u32[]{:S(2)}) collective-permute-start(f32[4,80,128]{2,1,0:T(8,128)S(1)} %pad_maximum_fusion.2.refs_0_), channel_id=1, source_target_pairs={{0,2},{2,0},{1,3},{3,1},{4,6},{6,4},{5,7},{7,5},{8,10},{10,8},{9,1... | collective-permute-start | bytes 491528 | tf_op jit(solution)/shard_map/ppermute | solution.py:20
  53.8 10.6 %collective-permute-start.26 = (f32[4,80,128]{2,1,0:T(8,128)S(1)}, f32[4,80,128]{2,1,0:T(8,128)S(1)}, u32[]{:S(2)}, u32[]{:S(2)}) collective-permute-start(f32[4,80,128]{2,1,0:T(8,128)S(1)} %pad_maximum_fusion.2.refs_0_), channel_id=1, source_target_pairs={{0,4},{4,0},{1,5},{5,1},{2,6},{6,2},{3,7},{7,3},{8,12},{12,8},{9,1... | collective-permute-start | bytes 491528 | tf_op jit(solution)/shard_map/ppermute | solution.py:20
  55.1 9.4 %collective-permute-start.27 = (f32[4,80,128]{2,1,0:T(8,128)S(1)}, f32[4,80,128]{2,1,0:T(8,128)S(1)}, u32[]{:S(2)}, u32[]{:S(2)}) collective-permute-start(f32[4,80,128]{2,1,0:T(8,128)S(1)} %pad_maximum_fusion.2.refs_0_), channel_id=1, source_target_pairs={{0,6},{2,4},{4,2},{6,0},{1,7},{3,5},{5,3},{7,1},{8,14},{10,12},{12... | collective-permute-start | bytes 491528 | tf_op jit(solution)/shard_map/ppermute | solution.py:475
  61.0 7.8 %collective-permute-start.25 = (f32[4,72,128]{2,1,0:T(8,128)S(1)}, f32[4,72,128]{2,1,0:T(8,128)S(1)}, u32[]{:S(2)}, u32[]{:S(2)}) collective-permute-start(f32[4,72,128]{2,1,0:T(8,128)S(1)} %pad_maximum_fusion.5), channel_id=1, source_target_pairs={{0,6},{2,4},{4,2},{6,0},{1,7},{3,5},{5,3},{7,1},{8,14},{10,12},{12... | collective-permute-start | bytes 442376 | tf_op jit(solution)/shard_map/ppermute | solution.py:475
  62.7 6.1 %collective-permute-start.24 = (f32[4,72,128]{2,1,0:T(8,128)S(1)}, f32[4,72,128]{2,1,0:T(8,128)S(1)}, u32[]{:S(2)}, u32[]{:S(2)}) collective-permute-start(f32[4,72,128]{2,1,0:T(8,128)S(1)} %pad_maximum_fusion.5), channel_id=1, source_target_pairs={{0,4},{4,0},{1,5},{5,1},{2,6},{6,2},{3,7},{7,3},{8,12},{12,8},{9,1... | collective-permute-start | bytes 442376 | tf_op jit(solution)/shard_map/ppermute | solution.py:20
  62.7 6.1 %collective-permute-start.23 = (f32[4,72,128]{2,1,0:T(8,128)S(1)}, f32[4,72,128]{2,1,0:T(8,128)S(1)}, u32[]{:S(2)}, u32[]{:S(2)}) collective-permute-start(f32[4,72,128]{2,1,0:T(8,128)S(1)} %pad_maximum_fusion.5), channel_id=1, source_target_pairs={{0,2},{2,0},{1,3},{3,1},{4,6},{6,4},{5,7},{7,5},{8,10},{10,8},{9,1... | collective-permute-start | bytes 442376 | tf_op jit(solution)/shard_map/ppermute | solution.py:20
  75.9 5.9 %collective-permute-start.30 = (f32[512,512]{1,0:T(8,128)S(1)}, f32[512,512]{1,0:T(8,128)S(1)}, u32[]{:S(2)}, u32[]{:S(2)}) collective-permute-start(f32[512,512]{1,0:T(8,128)S(1)} %get-tuple-element.76.own), channel_id=1, source_target_pairs={{0,1},{1,0},{2,3},{3,2},{4,5},{5,4},{6,7},{7,6},{8,9},{9,8},{10,11... | collective-permute-start | bytes 3145736 | tf_op jit(solution)/shard_map/ppermute | solution.py:20
  76.2 22.6 %collective-permute-start.40 = (bf16[2,1024,128]{2,1,0:T(8,128)(2,1)S(1)}, bf16[2,1024,128]{2,1,0:T(8,128)(2,1)S(1)}, u32[]{:S(2)}, u32[]{:S(2)}) collective-permute-start(bf16[2,1024,128]{2,1,0:T(8,128)(2,1)S(1)} %collective-permute-done.21.refs_4_), channel_id=1, source_target_pairs={{0,1},{1,0},{2,3},{3,2},{4,5},{5,4},{6,7},{7,6},{8,9},{9,8},{10,11... | collective-permute-start | bytes 1572872 | tf_op jit(solution)/shard_map/ppermute | solution.py:20
  78.2 6.8 %collective-permute-start.33 = (bf16[4,64,128]{2,1,0:T(8,128)(2,1)S(1)}, bf16[4,64,128]{2,1,0:T(8,128)(2,1)S(1)}, u32[]{:S(2)}, u32[]{:S(2)}) collective-permute-start(bf16[4,64,128]{2,1,0:T(8,128)(2,1)S(1)} %get-tuple-element.83), channel_id=1, source_target_pairs={{0,6},{2,4},{4,2},{6,0},{1,7},{3,5},{5,3},{7,1},{8,14},{10,12},{12... | collective-permute-start | bytes 196616 | tf_op jit(solution)/shard_map/ppermute | solution.py:475
  85.1 10.2 %collective-permute-start.36 = (bf16[4,64,128]{2,1,0:T(8,128)(2,1)S(1)}, bf16[4,64,128]{2,1,0:T(8,128)(2,1)S(1)}, u32[]{:S(2)}, u32[]{:S(2)}) collective-permute-start(bf16[4,64,128]{2,1,0:T(8,128)(2,1)S(1)} %add_convert_fusion), channel_id=1, source_target_pairs={{0,24},{8,0},{16,8},{24,16},{1,25},{9,1},{17,9},{25,17},{2,26},{10... | collective-permute-start | bytes 196616 | tf_op jit(solution)/shard_map/ppermute | solution.py:470
  86.9 8.3 %collective-permute-start.35 = (bf16[4,64,128]{2,1,0:T(8,128)(2,1)S(1)}, bf16[4,64,128]{2,1,0:T(8,128)(2,1)S(1)}, u32[]{:S(2)}, u32[]{:S(2)}) collective-permute-start(bf16[4,64,128]{2,1,0:T(8,128)(2,1)S(1)} %add_convert_fusion), channel_id=1, source_target_pairs={{0,16},{8,24},{16,0},{24,8},{1,17},{9,25},{17,1},{25,9},{2,18},{10... | collective-permute-start | bytes 196616 | tf_op jit(solution)/shard_map/ppermute | solution.py:470
  88.1 7.1 %collective-permute-start.34 = (bf16[4,64,128]{2,1,0:T(8,128)(2,1)S(1)}, bf16[4,64,128]{2,1,0:T(8,128)(2,1)S(1)}, u32[]{:S(2)}, u32[]{:S(2)}) collective-permute-start(bf16[4,64,128]{2,1,0:T(8,128)(2,1)S(1)} %add_convert_fusion), channel_id=1, source_target_pairs={{0,8},{8,16},{16,24},{24,0},{1,9},{9,17},{17,25},{25,1},{2,10},{10... | collective-permute-start | bytes 196616 | tf_op jit(solution)/shard_map/ppermute | solution.py:470
  95.2 11.8 %collective-permute-start.42 = (bf16[2,512,512]{2,1,0:T(8,128)(2,1)S(1)}, bf16[2,512,512]{2,1,0:T(8,128)(2,1)S(1)}, u32[]{:S(2)}, u32[]{:S(2)}) collective-permute-start(bf16[2,512,512]{2,1,0:T(8,128)(2,1)S(1)} %shard_map.51.inv), channel_id=1, source_target_pairs={{0,1},{1,0},{2,3},{3,2},{4,5},{5,4},{6,7},{7,6},{8,9},{9,8},{10,11... | collective-permute-start | bytes 3145736 | tf_op jit(solution)/shard_map/ppermute | solution.py:20
  95.3 7.3 %collective-permute-start.39 = (f32[4,64,128]{2,1,0:T(8,128)S(1)}, f32[4,64,128]{2,1,0:T(8,128)S(1)}, u32[]{:S(2)}, u32[]{:S(2)}) collective-permute-start(f32[4,64,128]{2,1,0:T(8,128)S(1)} %convert_add_fusion), channel_id=1, source_target_pairs={{0,6},{2,4},{4,2},{6,0},{1,7},{3,5},{5,3},{7,1},{8,14},{10,12},{12... | collective-permute-start | bytes 393224 | tf_op jit(solution)/shard_map/ppermute | solution.py:475
  96.6 7.9 %collective-permute-start.38 = (f32[4,64,128]{2,1,0:T(8,128)S(1)}, f32[4,64,128]{2,1,0:T(8,128)S(1)}, u32[]{:S(2)}, u32[]{:S(2)}) collective-permute-start(f32[4,64,128]{2,1,0:T(8,128)S(1)} %convert_add_fusion), channel_id=1, source_target_pairs={{0,4},{4,0},{1,5},{5,1},{2,6},{6,2},{3,7},{7,3},{8,12},{12,8},{9,1... | collective-permute-start | bytes 393224 | tf_op jit(solution)/shard_map/ppermute | solution.py:20
  97.8 7.1 %collective-permute-start.37 = (f32[4,64,128]{2,1,0:T(8,128)S(1)}, f32[4,64,128]{2,1,0:T(8,128)S(1)}, u32[]{:S(2)}, u32[]{:S(2)}) collective-permute-start(f32[4,64,128]{2,1,0:T(8,128)S(1)} %convert_add_fusion), channel_id=1, source_target_pairs={{0,2},{2,0},{1,3},{3,1},{4,6},{6,4},{5,7},{7,5},{8,10},{10,8},{9,1... | collective-permute-start | bytes 393224 | tf_op jit(solution)/shard_map/ppermute | solution.py:20
  (15 other events, 65.8 us)
